TPU v7x, 256 devices: a whole 4x4x8 slice. The times are simulated.
256 devices in a mesh: ctx: 32 (over y, x, z_hi), tp: 8 (over z_lo, core).
Axes of the slice: x: 4, y: 4, z: 8 (z_hi: 2, z_lo: 4; z = z_hi * 4 + z_lo), core: 2. Of those that a mesh axis runs over, the one named last changes fastest.
Arguments:
- queries: bfloat16 [4096, 16384], P('ctx', 'tp'), may hold values from -128 to 128
- keys: bfloat16 [4096, 1024], P('ctx', 'tp'), may hold values from -8 to 8
- values: bfloat16 [4096, 1024], P('ctx', 'tp'), may hold values from -6 to 6
- outputs: bfloat16 [4096, 16384], P('ctx', 'tp'), may hold values from -6 to 6
- out_grad: bfloat16 [4096, 16384], P('ctx', 'tp'), may hold values from -8 to 8
- doc_lengths: int32 [8], replicated, may hold values from 1 to 2048, 4096 in all
- span_perm: int32 [64], replicated, may hold values from 0 to 63, each once
Outputs:
- query_grad: bfloat16 [4096, 16384], P('ctx', 'tp')
- key_grad: bfloat16 [4096, 1024], P('ctx', 'tp')
- value_grad: bfloat16 [4096, 1024], P('ctx', 'tp')
- grad_square: float32 [], replicated
Inputs may be any that keep to these rules, and one draw needn't show every extreme that they name: `doc_lengths`: the lengths sum to 4096; the longest is exactly 2048. `span_perm`: each span number appears once.
All inputs are finite; a program needn't handle non-finite values.
Results may differ from a plain program's by a relative error of at most 0.0065.
Values may be sent and summed in bfloat16 or wider, within the bound.
No kernel may reach another device: no remote copies, remote signals or barrier semaphores. Data moves between devices by JAX's collectives and lax.ppermute only.
A program may use at most 64 MiB of HBM per device.

v0:
```python
import jax
import jax.numpy as jnp
from jax import lax
from jax.sharding import PartitionSpec as P

HD = 128
GROUP = 16


masked_score = -1e30


def block_rows(count):
    for width in (512, 256, 128):
        return width
    return count


def over_blocks(count, step, carry):
    width = block_rows(count)
    return lax.fori_loop(
        0, count // width, lambda index, state: step(index * width, width, state), carry
    )


def place_rows(span_perm, start, count, span):
    rows = start + jnp.arange(count, dtype=jnp.int32)
    slots = rows // span
    onehot = slots[:, None] == jnp.arange(span_perm.shape[0], dtype=jnp.int32)[None, :]
    return jnp.sum(jnp.where(onehot, span_perm[None, :], 0), axis=1) * span + rows % span


def document_of(places, ends):
    return jnp.sum((places[:, None] >= ends[None, :]).astype(jnp.int32), axis=1)


def shards(queries, keys, values, outputs, out_grad, doc_lengths, span_perm):
    tq = queries.shape[0]
    kvd = keys.shape[1] // HD
    total_rows = tq * lax.axis_size("ctx")
    span = tq // 2
    scale = HD ** (-0.5)
    ends = jnp.cumsum(doc_lengths)
    qplace = place_rows(span_perm, lax.axis_index("ctx") * tq, tq, span)
    qdoc = document_of(qplace, ends)
    query4 = queries.reshape(tq, kvd, GROUP, HD)
    grad4 = out_grad.reshape(tq, kvd, GROUP, HD)
    delta = jnp.einsum(
        "qgjd,qgjd->gjq",
        grad4,
        outputs.reshape(tq, kvd, GROUP, HD),
        preferred_element_type=jnp.float32,
    )

    def visible(start, count):
        kplace = place_rows(span_perm, start, count, span)
        kdoc = document_of(kplace, ends)
        return (kplace[None, :] <= qplace[:, None]) & (kdoc[None, :] == qdoc[:, None])

    def guarded(compute):
        result = compute()
        return result

    def stats_block(key_block, allowed, state):
        maxima, totals = state

        def compute():
            scores = (
                jnp.einsum("qgjd,kgd->gjqk", query4, key_block, preferred_element_type=jnp.float32)
                * scale
            )
            masked = jnp.where(allowed, scores, masked_score)
            fresh = jnp.maximum(maxima, jnp.max(masked, axis=-1))
            weights = jnp.where(allowed, jnp.exp(masked - fresh[..., None]), 0.0)
            return (fresh, totals * jnp.exp(maxima - fresh) + jnp.sum(weights, axis=-1))

        return guarded(compute)

    def backward_core(key_block, value_block, allowed, lse):
        scores = (
            jnp.einsum("qgjd,kgd->gjqk", query4, key_block, preferred_element_type=jnp.float32)
            * scale
        )
        probs = jnp.where(
            allowed, jnp.exp(jnp.where(allowed, scores, masked_score) - lse[..., None]), 0.0
        )
        dprobs = jnp.einsum(
            "qgjd,kgd->gjqk", grad4, value_block, preferred_element_type=jnp.float32
        )
        dscores = (probs * (dprobs - delta[..., None])).astype(jnp.bfloat16)
        return (probs, dscores)

    def query_end(dscores, key_block):
        return (
            jnp.einsum("gjqk,kgd->qgjd", dscores, key_block, preferred_element_type=jnp.float32)
            * scale
        )

    def keyval_end(probs, dscores):
        key_part = (
            jnp.einsum("gjqk,qgjd->kgd", dscores, query4, preferred_element_type=jnp.float32)
            * scale
        )
        value_part = jnp.einsum(
            "gjqk,qgjd->kgd", probs.astype(jnp.bfloat16), grad4, preferred_element_type=jnp.float32
        )
        return (key_part, value_part)

    def grad_block(key_block, value_block, allowed, lse):
        width = key_block.shape[0]

        def compute():
            probs, dscores = backward_core(key_block, value_block, allowed, lse)
            key_part, value_part = keyval_end(probs, dscores)
            return (query_end(dscores, key_block), key_part, value_part)

        return guarded(compute)

    def joined(key_part, value_part):
        width = key_part.shape[0]
        return jnp.concatenate(
            [key_part.reshape(width, kvd * HD), value_part.reshape(width, kvd * HD)], axis=1
        )

    start_stats = (
        jnp.full((kvd, GROUP, tq), masked_score, jnp.float32),
        jnp.zeros((kvd, GROUP, tq), jnp.float32),
    )
    query_zero = jnp.zeros((tq, kvd, GROUP, HD), jnp.float32)
    key_piece = lax.all_gather(keys, "ctx", axis=0, tiled=True)
    key3 = key_piece.reshape(key_piece.shape[0], kvd, HD)

    def step(offset, width, inner):
        key_block = lax.dynamic_slice_in_dim(key3, offset, width, 0)
        return stats_block(key_block, visible(offset, width), inner)

    maxima, totals = over_blocks(key_piece.shape[0], step, start_stats)
    lse = maxima + jnp.log(totals)
    start_grads = (query_zero, jnp.zeros((total_rows, 2 * kvd * HD), jnp.float32))
    pieces = (
        lax.all_gather(keys, "ctx", axis=0, tiled=True),
        lax.all_gather(values, "ctx", axis=0, tiled=True),
    )
    count = pieces[0].shape[0]
    grad_key3 = pieces[0].reshape(count, kvd, HD)
    value3 = pieces[1].reshape(count, kvd, HD)

    def step(offset, width, inner):
        accum, buffer = inner
        key_block = lax.dynamic_slice_in_dim(grad_key3, offset, width, 0)
        value_block = lax.dynamic_slice_in_dim(value3, offset, width, 0)
        parts = grad_block(key_block, value_block, visible(offset, width), lse)
        buffer = lax.dynamic_update_slice_in_dim(buffer, joined(parts[1], parts[2]), offset, 0)
        return (accum + parts[0], buffer)

    query_sum, partials = over_blocks(count, step, start_grads)
    both_grads = lax.psum_scatter(partials, "ctx", scatter_dimension=0, tiled=True)
    query_grad = query_sum.reshape(tq, kvd * GROUP * HD).astype(jnp.bfloat16)
    key_grad = both_grads[:, : kvd * HD].astype(jnp.bfloat16)
    value_grad = both_grads[:, kvd * HD :].astype(jnp.bfloat16)
    local_square = (
        jnp.sum(jnp.square(query_grad.astype(jnp.float32)))
        + jnp.sum(jnp.square(key_grad.astype(jnp.float32)))
        + jnp.sum(jnp.square(value_grad.astype(jnp.float32)))
    )
    grad_square = lax.psum(local_square, ("ctx", "tp"))
    return (query_grad, key_grad, value_grad, grad_square)


def solution(mesh):
    placed = (
        P("ctx", "tp"),
        P("ctx", "tp"),
        P("ctx", "tp"),
        P("ctx", "tp"),
        P("ctx", "tp"),
        P(),
        P(),
    )
    return jax.shard_map(
        shards,
        mesh=mesh,
        in_specs=placed,
        out_specs=(P("ctx", "tp"), P("ctx", "tp"), P("ctx", "tp"), P()),
        check_vma=False,
    )
```

profile of v0, /device:TPU:1, one launch (start us, length us, event | category | flops | bytes accessed | tf_op | source)
XLA Modules:
  0.0 590.4 jit_solution(5448613191214888495)
XLA Ops:
  13.1 2.0 copy.30
  15.8 79.6 %all-gather.3.cloned.1.call-done = bf16[4096,128]{1,0:T(8,128)(2,1)} async-done(((bf16[128,128]{1,0:T(8,128)(2,1)}), bf16[4096,128]{1,0:T(8,128)(2,1)}) %all-gather.3.cloned.1.call-update) | async-done | bytes 1048592 | tf_op jit(solution)/shard_map/all_gather | solution.py:141
  95.4 25.2 %while.36 = (s32[]{:T(128)}, f32[1,16,128]{2,1,0:T(8,128)S(1)}, f32[1,16,128]{2,1,0:T(8,128)S(1)}, s32[64]{0:T(128)S(1)}, s32[128]{0:T(128)S(1)}, /*index=5*/s32...) while((s32[]{:T(128)}, f32[1,16,128]{2,1,0:T(8,128)S(1)}, ...), condition=%wide.region_8.9_spmd.clone, body=%wide.region_3.8_spmd.clone.sunk | while | flops 277155840 | bytes 9367018 | solution.py:21
  95.8 1.6 fusion.84
  99.0 1.6 fusion.84
  102.1 1.6 fusion.84
  105.3 1.6 fusion.84
  108.4 1.6 fusion.84
  111.6 1.6 fusion.84
  114.7 1.6 fusion.84
  117.9 1.6 fusion.84
  120.6 54.0 %all-gather.5.cloned.1.call-done = bf16[4096,128]{1,0:T(8,128)(2,1)} async-done(((bf16[128,128]{1,0:T(8,128)(2,1)}), bf16[4096,128]{1,0:T(8,128)(2,1)}) %all-gather.5.cloned.1.call-update) | async-done | bytes 1048592 | tf_op jit(solution)/shard_map/all_gather | solution.py:142
  174.7 2.2 broadcast_in_dim.213.clone
  176.9 73.3 %while.37 = (s32[]{:T(128)}, f32[128,1,16,128]{0,3,2,1:T(8,128)S(1)}, f32[4096,256]{1,0:T(8,128)}, bf16[4096,1,128]{2,0,1:T(8,128)(2,1)}, s32[64]{0:T(128)S(1)},...) while((s32[]{:T(128)}, ...), condition=%wide.region_12.13_spmd.clone, body=%wide.region_9.12_spmd.clone.sunk | while | flops 1356064768 | bytes 27373076 | solution.py:21
  180.1 2.4 fusion.97
  189.3 2.4 fusion.97
  198.4 2.4 fusion.97
  207.6 2.4 fusion.97
  216.8 2.4 fusion.97
  225.9 2.4 fusion.97
  235.1 2.4 fusion.97
  244.2 2.4 fusion.97
  251.0 233.0 %reduce-scatter.2.cloned.1.call-done = f32[128,256]{1,0:T(8,128)} async-done(((f32[4096,256]{1,0:T(8,128)}), f32[128,256]{1,0:T(8,128)}) %reduce-scatter.2.cloned.1.call-update) | async-done | bytes 131088 | tf_op jit(solution)/shard_map/reduce_scatter | solution.py:157
  489.3 94.6 %psum.7 = f32[]{:T(128)} all-reduce(f32[]{:T(128)S(6)} %add.324), channel_id=1, replica_groups=mesh['ctx'=32,'tp'=8] {'ctx','tp'}, use_global_device_ids=true, to_apply=%region_17.18 | all-reduce | flops 1 | bytes 8 | tf_op jit(solution)/shard_map/psum | solution.py:166
  (199 shorter events, 75.3 us)
Async XLA Ops:
  7.2 88.3 %copy-start.2 = (s32[64]{0:T(128)S(1)}, s32[64]{0:T(128)}, u32[]{:S(2)}) copy-start(s32[64]{0:T(128)} %param.17) | copy-start | bytes 772
  7.2 8.0 %copy-start = (bf16[128,2048]{1,0:T(8,128)(2,1)S(1)}, bf16[128,2048]{1,0:T(8,128)(2,1)}, u32[]{:S(2)}) copy-start(bf16[128,2048]{1,0:T(8,128)(2,1)} %param.15) | copy-start | bytes 1572868
  7.2 88.2 %all-gather.3.cloned.1.call-start = ((), (), s32[]{:S(2)}) async-start(), calls=%async_computation.1 | async-start | bytes 1081344 | tf_op jit(solution)/shard_map/all_gather | solution.py:141
  7.9 166.7 %all-gather.5.cloned.1.call-start = ((), (), s32[]{:S(2)}) async-start(), calls=%async_computation.2 | async-start | bytes 1081344 | tf_op jit(solution)/shard_map/all_gather | solution.py:142
  8.7 475.4 %reduce-scatter.2.cloned.1.call-start = ((), (), s32[]{:S(2)}) async-start(), calls=%async_computation.3 | async-start | bytes 4325376 | tf_op jit(solution)/shard_map/reduce_scatter | solution.py:157
  120.6 56.3 %copy-start.1 = (bf16[128,2048]{0,1:T(8,128)(2,1)S(1)}, bf16[128,2048]{0,1:T(8,128)(2,1)}, u32[]{:S(2)}) copy-start(bf16[128,2048]{0,1:T(8,128)(2,1)} %copy.30) | copy-start | bytes 1572868
Sparse Core Ops, SparseCore 0:
  11.4 83.9 all-gather.2
  98.8 75.7 all-gather.4
  250.3 233.7 reduce-scatter.1
where the time goes:
time: 591 us; the launch traced here: 590 us
  waiting for transfers between devices  368 us (62%)
  blocking collectives  94.6 us (16%)
  matrix products  74 us (13%)
  other arithmetic  20.2 us (3%)
  local copies, waits for them, and re-layouts  16.5 us (3%)
  between operations  15.8 us (3%)
    reduce_scatter x1, waiting for transfers between devices, shards(): lax.psum_scatter(partials, 'ctx', scatter_dimension=0, tiled=True)  233 us
    psum x1, blocking collectives, shards(): grad_square = lax.psum(local_square, ('ctx', 'tp'))  94.6 us
    all_gather x1, waiting for transfers between devices, shards(): lax.all_gather(keys, 'ctx', axis=0, tiled=True)  79.6 us
    all_gather x1, waiting for transfers between devices, shards(): lax.all_gather(values, 'ctx', axis=0, tiled=True)  54 us
    dot_general x8, matrix products, backward_core(): jnp.einsum('qgjd,kgd->gjqk', grad4, value_block, preferred_element_type=j...  19.6 us
    dot_general x8, matrix products, compute(): jnp.einsum('qgjd,kgd->gjqk', query4, key_block, preferred_element_type=jn...  13.1 us
    dot_general x8, matrix products, backward_core(): jnp.einsum('qgjd,kgd->gjqk', query4, key_block, preferred_element_type=jn...  12.8 us
    dot_general x8, matrix products, query_end(): jnp.einsum('gjqk,kgd->qgjd', dscores, key_block, preferred_element_type=j...  12.3 us
  transfers between devices with their start and end apart: 3, of which 3 were waited for; matrix products, arithmetic and copies ran while one was open for 6% of the time, Pallas kernels for 0%

commit v1 on v0

v1 whole, which is shorter than its diff:
```python
import functools

import jax
import jax.numpy as jnp
from jax import lax
from jax.experimental import pallas as pl
from jax.experimental.pallas import tpu as pltpu
from jax.sharding import PartitionSpec as P

HD = 128
GROUP = 16
SPAN = 64
SPANS = 64
NY, NX, NZ = 4, 4, 2
ROWS = SPAN * GROUP
TILE = 256
TOTAL = SPAN * SPANS
SCALE = HD ** (-0.5)
LOG2E = 1.4426950408889634
NEG = -1e30

f32, bf16, i32 = jnp.float32, jnp.bfloat16, jnp.int32


def nt(a, b):
    return lax.dot_general(a, b, (((1,), (1,)), ((), ())), preferred_element_type=f32)


def nn(a, b):
    return lax.dot_general(a, b, (((1,), (0,)), ((), ())), preferred_element_type=f32)


def tn(a, b):
    return lax.dot_general(a, b, (((0,), (0,)), ((), ())), preferred_element_type=f32)


def rel_slots():
    return [
        (sy, sx, sz, half)
        for sy in range(NY)
        for sx in range(NX)
        for sz in range(NZ)
        for half in range(2)
    ]


def attention_kernel(
    perm_ref, lens_ref, q_ref, o_ref, g_ref, kv0, kv1, kv2, kv3,
    dq_ref, d0, d1, d2, d3, sq_ref,
    qs, gs, kseq, vseq, acc, dqt,
):
    kvs, outs = (kv0, kv1, kv2, kv3), (d0, d1, d2, d3)
    me = lax.axis_index("ctx")
    y, x, z = me // (NX * NZ), (me // NZ) % NX, me % NZ

    def span_of(sy, sx, sz, half):
        slot = ((((y + NY - sy) % NY) * NX + (x + NX - sx) % NX) * NZ + (z + sz) % NZ) * 2 + half
        return perm_ref[slot]

    for a in range(2):
        for h in range(GROUP):
            dst = pl.ds(a * ROWS + h * SPAN, SPAN)
            src = (pl.ds(a * SPAN, SPAN), pl.ds(h * HD, HD))
            qs[dst, :] = q_ref[src]
            gs[dst, :] = g_ref[src]

    for i, (sy, sx, sz, half) in enumerate(rel_slots()):
        at = pl.multiple_of(span_of(sy, sx, sz, half) * SPAN, SPAN)
        row = (i * SPAN) % (TOTAL // NY)
        kseq[pl.ds(at, SPAN), :] = kvs[sy][pl.ds(row, SPAN), :HD]
        vseq[pl.ds(at, SPAN), :] = kvs[sy][pl.ds(row, SPAN), HD:]
    kseq[pl.ds(TOTAL, TILE), :] = jnp.zeros((TILE, HD), bf16)
    vseq[pl.ds(TOTAL, TILE), :] = jnp.zeros((TILE, HD), bf16)
    acc[...] = jnp.zeros_like(acc)

    ends, total = [], 0
    for d in range(lens_ref.shape[0]):
        total = total + lens_ref[d]
        ends.append(total)

    lane = lax.broadcasted_iota(i32, (1, ROWS), 1)
    square = jnp.zeros((1, 1), f32)
    for a in range(2):
        span = perm_ref[me * 2 + a]
        place = span * SPAN + (lane & (SPAN - 1))
        begin = jnp.zeros_like(place)
        first = 0
        for end in ends:
            begin = jnp.maximum(begin, jnp.where(end <= place, end, 0))
            first = jnp.maximum(first, jnp.where(end <= span * SPAN, end, 0))
        start = (first // SPAN) * SPAN
        count = (span * SPAN + SPAN - start + TILE - 1) // TILE
        q = qs[pl.ds(a * ROWS, ROWS), :]
        g = gs[pl.ds(a * ROWS, ROWS), :]

        prods = []
        for h in range(GROUP):
            src = (pl.ds(a * SPAN, SPAN), pl.ds(h * HD, HD))
            prods.append(g_ref[src].astype(f32) * o_ref[src].astype(f32))
        prod = jnp.concatenate(prods, axis=0)
        high = prod.astype(bf16)
        low = (prod - high.astype(f32)).astype(bf16)
        ones = jnp.ones((16, HD), bf16)
        delta = (nt(ones, high) + nt(ones, low))[:1]

        def visible(k0):
            kp = k0 + lax.broadcasted_iota(i32, (TILE, 1), 0)
            return (kp <= place) & (kp >= begin)

        def stats(t, state):
            peak, mass = state
            k0 = pl.multiple_of(start + t * TILE, SPAN)
            s = nt(kseq[pl.ds(k0, TILE), :], q) * (SCALE * LOG2E)
            s = jnp.where(visible(k0), s, NEG)
            fresh = jnp.maximum(peak, jnp.max(s, axis=0, keepdims=True))
            part = jnp.sum(jnp.exp2(s - fresh), axis=0, keepdims=True)
            return fresh, mass * jnp.exp2(peak - fresh) + part

        peak, mass = lax.fori_loop(
            0, count, stats, (jnp.full((1, ROWS), NEG, f32), jnp.zeros((1, ROWS), f32))
        )
        lse = peak + jnp.log2(mass)

        dqt[...] = jnp.zeros_like(dqt)

        def grads(t, carry):
            k0 = pl.multiple_of(start + t * TILE, SPAN)
            k = kseq[pl.ds(k0, TILE), :]
            v = vseq[pl.ds(k0, TILE), :]
            s = nt(k, q) * (SCALE * LOG2E)
            p = jnp.where(visible(k0), jnp.exp2(s - lse), 0.0)
            ds = (p * (nt(v, g) - delta)).astype(bf16)
            acc[pl.ds(k0, TILE), :HD] += nn(ds, q)
            acc[pl.ds(k0, TILE), HD:] += nn(p.astype(bf16), g)
            dqt[...] += tn(k, ds)
            return carry

        lax.fori_loop(0, count, grads, 0)
        dq = (dqt[...] * SCALE).T.astype(bf16)
        for h in range(GROUP):
            dq_ref[pl.ds(a * SPAN, SPAN), pl.ds(h * HD, HD)] = dq[h * SPAN : (h + 1) * SPAN]
        dq = dq.astype(f32)
        square = square + jnp.sum(jnp.sum(dq * dq, axis=0, keepdims=True), axis=1, keepdims=True)

    sq_ref[...] = jnp.broadcast_to(square, sq_ref.shape)
    for i, (sy, sx, sz, half) in enumerate(rel_slots()):
        at = pl.multiple_of(span_of(sy, sx, sz, half) * SPAN, SPAN)
        row = (i * SPAN) % (TOTAL // NY)
        outs[sy][pl.ds(row, SPAN), :HD] = (acc[pl.ds(at, SPAN), :HD] * SCALE).astype(bf16)
        outs[sy][pl.ds(row, SPAN), HD:] = acc[pl.ds(at, SPAN), HD:].astype(bf16)


def attention(span_perm, doc_lengths, queries, outputs, out_grad, kvs):
    tq = queries.shape[0]
    vm = pl.BlockSpec(memory_space=pltpu.VMEM)
    sm = pl.BlockSpec(memory_space=pltpu.SMEM)
    chunk = jax.ShapeDtypeStruct((TOTAL // NY, 2 * HD), bf16)
    return pl.pallas_call(
        attention_kernel,
        out_shape=(
            jax.ShapeDtypeStruct(queries.shape, bf16),
            chunk, chunk, chunk, chunk,
            jax.ShapeDtypeStruct((8, HD), f32),
        ),
        in_specs=[sm, sm] + [vm] * 7,
        out_specs=(vm,) * 6,
        scratch_shapes=[
            pltpu.VMEM((2 * ROWS, HD), bf16),
            pltpu.VMEM((2 * ROWS, HD), bf16),
            pltpu.VMEM((TOTAL + TILE, HD), bf16),
            pltpu.VMEM((TOTAL + TILE, HD), bf16),
            pltpu.VMEM((TOTAL + TILE, 2 * HD), f32),
            pltpu.VMEM((HD, ROWS), f32),
        ],
        compiler_params=pltpu.CompilerParams(vmem_limit_bytes=48 * 1024 * 1024),
    )(span_perm, doc_lengths, queries, outputs, out_grad, *kvs)


def moved(a, dy=0, dx=0, dz=0):
    pairs = []
    for y in range(NY):
        for x in range(NX):
            for z in range(NZ):
                to = (((y + dy) % NY) * NX + (x + dx) % NX) * NZ + (z + dz) % NZ
                pairs.append(((y * NX + x) * NZ + z, to))
    return lax.ppermute(a, "ctx", pairs)


def shards(queries, keys, values, outputs, out_grad, doc_lengths, span_perm):
    tq = queries.shape[0]
    kv = jnp.concatenate([keys, values], axis=1)
    kv = jnp.stack([kv, moved(kv, dz=1)])
    kv = jnp.stack([kv] + [moved(kv, dx=s) for s in range(1, NX)])
    kvs = [kv] + [moved(kv, dy=s) for s in range(1, NY)]
    kvs = [a.reshape(TOTAL // NY, 2 * HD) for a in kvs]
    query_grad, *parts, square = attention(
        span_perm, doc_lengths, queries, outputs, out_grad, kvs
    )
    parts = [parts[0]] + [moved(parts[s], dy=-s) for s in range(1, NY)]
    mine = sum(p.astype(f32) for p in parts).astype(bf16).reshape(NX, NZ, tq, 2 * HD)
    parts = [mine[0]] + [moved(mine[s], dx=-s) for s in range(1, NX)]
    mine = sum(p.astype(f32) for p in parts)
    other = moved(mine[1].astype(bf16), dz=1)
    both = (mine[0] + other.astype(f32)).astype(bf16)
    wide = both.astype(f32)
    local = jnp.sum(wide * wide) + square[0, 0]
    world = lax.axis_size(("ctx", "tp"))
    grad_square = jnp.sum(
        lax.all_to_all(jnp.broadcast_to(local, (world, 1)), ("ctx", "tp"), 0, 0)
    )
    return (query_grad, both[:, :HD], both[:, HD:], grad_square)


def solution(mesh):
    placed = (P("ctx", "tp"),) * 5 + (P(), P())
    return jax.shard_map(
        shards,
        mesh=mesh,
        in_specs=placed,
        out_specs=(P("ctx", "tp"), P("ctx", "tp"), P("ctx", "tp"), P()),
        check_vma=False,
    )
```

time: 591 us -> 145 us (0.25)
  waiting for transfers between devices: 368 us -> 76 us
  blocking collectives: 94.6 us -> 0 us
  matrix products: 74 us -> 0 us
  starting transfers between devices: 0.11 us -> 53.8 us
  other arithmetic: 20.2 us -> 1.93 us
  between operations: 15.8 us -> 2.02 us
  local copies, waits for them, and re-layouts: 16.5 us -> 4.16 us
  Pallas kernels: 0 us -> 6.45 us
    reduce_scatter x1 -> x0, waiting for transfers between devices: 233 us -> none  [shards(): lax.psum_scatter(partials, 'ctx', scatter_dimension=0, tiled=True)]
    all_gather x2 -> x0, waiting for transfers between devices: 134 us -> none  [the longest x1 79.6 us: shards(): lax.all_gather(keys, 'ctx', axis=0, tiled=True)]
    psum x1 -> x0, blocking collectives: 94.6 us -> none  [shards(): grad_square = lax.psum(local_square, ('ctx', 'tp'))]
    dot_general x48 -> x0, matrix products: 74 us -> none  [the longest x8 19.6 us: backward_core(): jnp.einsum('qgjd,kgd->gjqk', grad4, value_block, preferred_element_type=j...]
    ppermute x0 -> x14, waiting for transfers between devices: none -> 63.8 us  [moved(): return lax.ppermute(a, 'ctx', pairs)]
    ppermute x0 -> x14, starting transfers between devices: none -> 42.5 us  [moved(): return lax.ppermute(a, 'ctx', pairs)]
    reduce_sum x44 -> x2, other arithmetic: 14 us -> 1.51 us  [the longest x1 0.87 us: shards(): jnp.sum(lax.all_to_all(jnp.broadcast_to(local, (world, 1)), ('ctx', 'tp')...]
    all_to_all x0 -> x1, waiting for transfers between devices: none -> 12.2 us  [shards(): lax.all_to_all(jnp.broadcast_to(local, (world, 1)), ('ctx', 'tp'), 0, 0)]
  transfers between devices with their start and end apart: 3 -> 15, of which waited for: 3 -> 12; matrix products, arithmetic and copies ran while one was open for 6% -> 1% of each run, Pallas kernels for 0% -> 0%
where the time goes in v1:
time: 145 us; the launch traced here: 144 us
  waiting for transfers between devices  76 us (52%)
  starting transfers between devices  53.8 us (37%)
  Pallas kernels  6.45 us (4%)
  local copies, waits for them, and re-layouts  4.16 us (3%)
  between operations  2.02 us (1%)
  other arithmetic  1.93 us (1%)
    ppermute x14, waiting for transfers between devices, moved(): return lax.ppermute(a, 'ctx', pairs)  63.8 us
    ppermute x14, starting transfers between devices, moved(): return lax.ppermute(a, 'ctx', pairs)  42.5 us
    all_to_all x1, waiting for transfers between devices, shards(): lax.all_to_all(jnp.broadcast_to(local, (world, 1)), ('ctx', 'tp'), 0, 0)  12.2 us
    all_to_all x1, starting transfers between devices, shards(): lax.all_to_all(jnp.broadcast_to(local, (world, 1)), ('ctx', 'tp'), 0, 0)  11.3 us
    pallas_call x1, Pallas kernels, attention(): pl.pallas_call(attention_kernel, out_shape=(jax.ShapeDtypeStruct(queries....  6.45 us
  transfers between devices with their start and end apart: 15, of which 12 were waited for; matrix products, arithmetic and copies ran while one was open for 1% of the time, Pallas kernels for 0%

profile of v1, /device:TPU:1, one launch (start us, length us, event | category | flops | bytes accessed | tf_op | source)
XLA Modules:
  0.0 144.3 jit_solution(16572186404289751100)
XLA Ops:
  2.2 7.8 %collective-permute-start = (bf16[128,256]{1,0:T(8,128)(2,1)S(1)}, bf16[128,256]{1,0:T(8,128)(2,1)S(1)}, u32[]{:S(2)}, u32[]{:S(2)}) collective-permute-start(bf16[128,256]{1,0:T(8,128)(2,1)S(1)} %constant_dynamic-update-slice_fusion), channel_id=1, source_target_pairs={{0,8},{8,0},{16,24},{24,16},{32,40},{40,32},{48,56},{56,48},{64,72... | collective-permute-start | bytes 196616 | tf_op jit(solution)/shard_map/ppermute | solution.py:186
  10.1 1.8 %collective-permute-done = bf16[128,256]{1,0:T(8,128)(2,1)S(1)} collective-permute-done((bf16[128,256]{1,0:T(8,128)(2,1)S(1)}, bf16[128,256]{1,0:T(8,128)(2,1)S(1)}, u32[]{:S(2)}, u32[]{:S(2)}) %collective-permute-start) | collective-permute-done | bytes 65568 | tf_op jit(solution)/shard_map/ppermute | solution.py:186
  11.8 2.8 %collective-permute-start.2 = (bf16[2,128,256]{2,1,0:T(8,128)(2,1)S(1)}, bf16[2,128,256]{2,1,0:T(8,128)(2,1)S(1)}, u32[]{:S(2)}, u32[]{:S(2)}) collective-permute-start(bf16[2,128,256]{2,1,0:T(8,128)(2,1)S(1)} %get-tuple-element.23), channel_id=1, source_target_pairs={{0,32},{8,40},{16,48},{24,56},{32,0},{40,8},{48,16},{56,24},{64,96... | collective-permute-start | bytes 393224 | tf_op jit(solution)/shard_map/ppermute | solution.py:186
  15.0 2.4 %collective-permute-start.3 = (bf16[2,128,256]{2,1,0:T(8,128)(2,1)S(1)}, bf16[2,128,256]{2,1,0:T(8,128)(2,1)S(1)}, u32[]{:S(2)}, u32[]{:S(2)}) collective-permute-start(bf16[2,128,256]{2,1,0:T(8,128)(2,1)S(1)} %get-tuple-element.23), channel_id=1, source_target_pairs={{0,48},{8,56},{16,0},{24,8},{32,16},{40,24},{48,32},{56,40},{64,11... | collective-permute-start | bytes 393224 | tf_op jit(solution)/shard_map/ppermute | solution.py:186
  17.3 4.4 %collective-permute-done.1 = bf16[2,128,256]{2,1,0:T(8,128)(2,1)S(1)} collective-permute-done((bf16[2,128,256]{2,1,0:T(8,128)(2,1)S(1)}, bf16[2,128,256]{2,1,0:T(8,128)(2,1)S(1)}, u32[]{:S(2)}, u32[]{:S(2)}) %collective-permute-start.1) | collective-permute-done | bytes 131104 | tf_op jit(solution)/shard_map/ppermute | solution.py:186
  21.8 2.5 %collective-permute-start.6 = (bf16[4,2,128,256]{3,2,1,0:T(8,128)(2,1)S(1)}, bf16[4,2,128,256]{3,2,1,0:T(8,128)(2,1)S(1)}, u32[]{:S(2)}, u32[]{:S(2)}) collective-permute-start(bf16[4,2,128,256]{3,2,1,0:T(8,128)(2,1)S(1)} %pad_maximum_fusion), channel_id=1, source_target_pairs={{0,192},{8,200},{16,208},{24,216},{32,224},{40,232},{48,240},{56,2... | collective-permute-start | bytes 1572872 | tf_op jit(solution)/shard_map/ppermute | solution.py:186
  25.3 9.1 %collective-permute-done.6 = bf16[4,2,128,256]{3,2,1,0:T(8,128)(2,1)S(1)} collective-permute-done((bf16[4,2,128,256]{3,2,1,0:T(8,128)(2,1)S(1)}, bf16[4,2,128,256]{3,2,1,0:T(8,128)(2,1)S(1)}, u32[]{:S(2)}, u32[]{:S(2)}) %collective-permute-start.6) | collective-permute-done | bytes 524320 | tf_op jit(solution)/shard_map/ppermute | solution.py:186
  34.4 3.0 %collective-permute-done.5 = bf16[4,2,128,256]{3,2,1,0:T(8,128)(2,1)S(1)} collective-permute-done((bf16[4,2,128,256]{3,2,1,0:T(8,128)(2,1)S(1)}, bf16[4,2,128,256]{3,2,1,0:T(8,128)(2,1)S(1)}, u32[]{:S(2)}, u32[]{:S(2)}) %collective-permute-start.5) | collective-permute-done | bytes 524320 | tf_op jit(solution)/shard_map/ppermute | solution.py:186
  37.4 13.5 %collective-permute-done.4 = bf16[4,2,128,256]{3,2,1,0:T(8,128)(2,1)S(1)} collective-permute-done((bf16[4,2,128,256]{3,2,1,0:T(8,128)(2,1)S(1)}, bf16[4,2,128,256]{3,2,1,0:T(8,128)(2,1)S(1)}, u32[]{:S(2)}, u32[]{:S(2)}) %collective-permute-start.4) | collective-permute-done | bytes 524320 | tf_op jit(solution)/shard_map/ppermute | solution.py:186
  51.5 6.4 %shard_map.102 = (bf16[128,2048]{1,0:T(8,128)(2,1)}, bf16[1024,256]{1,0:T(8,128)(2,1)S(1)}, bf16[1024,256]{1,0:T(8,128)(2,1)S(1)}, bf16[1024,256]{1,0:T(8,128)(2...) custom-call(s32[64]{0:T(128)S(1)} %copy-done.3, s32[8]{0:T(128)S(1)} %copy-done.4, ...), custom_call_target="tpu_custom_call" | custom-call | tf_op jit(solution)/shard_map/pallas_call | solution.py:158
  58.0 3.5 %collective-permute-start.7 = (bf16[1024,256]{1,0:T(8,128)(2,1)S(1)}, bf16[1024,256]{1,0:T(8,128)(2,1)S(1)}, u32[]{:S(2)}, u32[]{:S(2)}) collective-permute-start(bf16[1024,256]{1,0:T(8,128)(2,1)S(1)} %get-tuple-element.12), channel_id=1, source_target_pairs={{0,192},{8,200},{16,208},{24,216},{32,224},{40,232},{48,240},{56,2... | collective-permute-start | bytes 1572872 | tf_op jit(solution)/shard_map/ppermute | solution.py:186
  61.5 10.3 %collective-permute-start.8 = (bf16[1024,256]{1,0:T(8,128)(2,1)S(1)}, bf16[1024,256]{1,0:T(8,128)(2,1)S(1)}, u32[]{:S(2)}, u32[]{:S(2)}) collective-permute-start(bf16[1024,256]{1,0:T(8,128)(2,1)S(1)} %get-tuple-element.13), channel_id=1, source_target_pairs={{0,128},{8,136},{16,144},{24,152},{32,160},{40,168},{48,176},{56,1... | collective-permute-start | bytes 1572872 | tf_op jit(solution)/shard_map/ppermute | solution.py:186
  71.9 8.9 %collective-permute-done.7 = bf16[1024,256]{1,0:T(8,128)(2,1)S(1)} collective-permute-done((bf16[1024,256]{1,0:T(8,128)(2,1)S(1)}, bf16[1024,256]{1,0:T(8,128)(2,1)S(1)}, u32[]{:S(2)}, u32[]{:S(2)}) %collective-permute-start.7) | collective-permute-done | bytes 524320 | tf_op jit(solution)/shard_map/ppermute | solution.py:186
  80.7 1.6 %collective-permute-done.8 = bf16[1024,256]{1,0:T(8,128)(2,1)S(1)} collective-permute-done((bf16[1024,256]{1,0:T(8,128)(2,1)S(1)}, bf16[1024,256]{1,0:T(8,128)(2,1)S(1)}, u32[]{:S(2)}, u32[]{:S(2)}) %collective-permute-start.8) | collective-permute-done | bytes 524320 | tf_op jit(solution)/shard_map/ppermute | solution.py:186
  82.3 13.2 %collective-permute-done.9 = bf16[1024,256]{1,0:T(8,128)(2,1)S(1)} collective-permute-done((bf16[1024,256]{1,0:T(8,128)(2,1)S(1)}, bf16[1024,256]{1,0:T(8,128)(2,1)S(1)}, u32[]{:S(2)}, u32[]{:S(2)}) %collective-permute-start.9) | collective-permute-done | bytes 524320 | tf_op jit(solution)/shard_map/ppermute | solution.py:186
  95.9 2.7 %collective-permute-start.10 = (bf16[2,128,256]{2,1,0:T(8,128)(2,1)S(1)}, bf16[2,128,256]{2,1,0:T(8,128)(2,1)S(1)}, u32[]{:S(2)}, u32[]{:S(2)}) collective-permute-start(bf16[2,128,256]{2,1,0:T(8,128)(2,1)S(1)} %bitcast.34), channel_id=1, source_target_pairs={{0,48},{8,56},{16,0},{24,8},{32,16},{40,24},{48,32},{56,40},{64,11... | collective-permute-start | bytes 393224 | tf_op jit(solution)/shard_map/ppermute | solution.py:186
  98.5 6.1 %collective-permute-start.11 = (bf16[2,128,256]{2,1,0:T(8,128)(2,1)S(1)}, bf16[2,128,256]{2,1,0:T(8,128)(2,1)S(1)}, u32[]{:S(2)}, u32[]{:S(2)}) collective-permute-start(bf16[2,128,256]{2,1,0:T(8,128)(2,1)S(1)} %bitcast.32), channel_id=1, source_target_pairs={{0,32},{8,40},{16,48},{24,56},{32,0},{40,8},{48,16},{56,24},{64,96... | collective-permute-start | bytes 393224 | tf_op jit(solution)/shard_map/ppermute | solution.py:186
  104.7 1.3 collective-permute-done.10
  106.0 3.5 %collective-permute-done.11 = bf16[2,128,256]{2,1,0:T(8,128)(2,1)S(1)} collective-permute-done((bf16[2,128,256]{2,1,0:T(8,128)(2,1)S(1)}, bf16[2,128,256]{2,1,0:T(8,128)(2,1)S(1)}, u32[]{:S(2)}, u32[]{:S(2)}) %collective-permute-start.11) | collective-permute-done | bytes 131104 | tf_op jit(solution)/shard_map/ppermute | solution.py:186
  109.5 2.9 %collective-permute-start.13 = (bf16[128,256]{1,0:T(8,128)(2,1)S(1)}, bf16[128,256]{1,0:T(8,128)(2,1)S(1)}, u32[]{:S(2)}, u32[]{:S(2)}) collective-permute-start(bf16[128,256]{1,0:T(8,128)(2,1)S(1)} %fusion.4), channel_id=1, source_target_pairs={{0,8},{8,0},{16,24},{24,16},{32,40},{40,32},{48,56},{56,48},{64,72... | collective-permute-start | bytes 196616 | tf_op jit(solution)/shard_map/ppermute | solution.py:186
  113.0 3.7 %collective-permute-done.13 = bf16[128,256]{1,0:T(8,128)(2,1)S(1)} collective-permute-done((bf16[128,256]{1,0:T(8,128)(2,1)S(1)}, bf16[128,256]{1,0:T(8,128)(2,1)S(1)}, u32[]{:S(2)}, u32[]{:S(2)}) %collective-permute-start.13) | collective-permute-done | bytes 65568 | tf_op jit(solution)/shard_map/ppermute | solution.py:186
  119.3 11.3 %all-to-all-start = ((f32[256,1,1]{2,1,0:T(1,128)}), f32[256,1,1]{2,1,0:T(1,128)S(1)}, u32[]{:S(2)}, u32[]{:S(2)}) async-start(f32[256,1,1]{2,1,0:T(1,128)} %broadcast_in_dim.3), calls=%async_computation | async-start | bytes 262144 | tf_op jit(solution)/shard_map/all_to_all | solution.py:209
  131.2 12.2 %all-to-all-done = f32[256,1,1]{2,1,0:T(1,128)S(1)} async-done(((f32[256,1,1]{2,1,0:T(1,128)}), f32[256,1,1]{2,1,0:T(1,128)S(1)}, u32[]{:S(2)}, u32[]{:S(2)}) %all-to-all-start) | async-done | bytes 1056 | tf_op jit(solution)/shard_map/all_to_all | solution.py:209
  143.4 0.9 reduce_sum.19
  (30 shorter events, 6.7 us)
Async XLA Ops:
  0.6 50.2 %copy-start.2 = (bf16[128,2048]{1,0:T(8,128)(2,1)S(1)}, bf16[128,2048]{1,0:T(8,128)(2,1)}, u32[]{:S(2)}) copy-start(bf16[128,2048]{1,0:T(8,128)(2,1)} %g_ref.1) | copy-start | bytes 1572868
  2.2 9.6 %collective-permute-start = (bf16[128,256]{1,0:T(8,128)(2,1)S(1)}, bf16[128,256]{1,0:T(8,128)(2,1)S(1)}, u32[]{:S(2)}, u32[]{:S(2)}) collective-permute-start(bf16[128,256]{1,0:T(8,128)(2,1)S(1)} %constant_dynamic-update-slice_fusion), channel_id=1, source_target_pairs={{0,8},{8,0},{16,24},{24,16},{32,40},{40,32},{48,56},{56,48},{64,72... | collective-permute-start | bytes 196616 | tf_op jit(solution)/shard_map/ppermute | solution.py:186
  11.8 5.5 %collective-permute-start.2 = (bf16[2,128,256]{2,1,0:T(8,128)(2,1)S(1)}, bf16[2,128,256]{2,1,0:T(8,128)(2,1)S(1)}, u32[]{:S(2)}, u32[]{:S(2)}) collective-permute-start(bf16[2,128,256]{2,1,0:T(8,128)(2,1)S(1)} %get-tuple-element.23), channel_id=1, source_target_pairs={{0,32},{8,40},{16,48},{24,56},{32,0},{40,8},{48,16},{56,24},{64,96... | collective-permute-start | bytes 393224 | tf_op jit(solution)/shard_map/ppermute | solution.py:186
  14.7 7.1 %collective-permute-start.1 = (bf16[2,128,256]{2,1,0:T(8,128)(2,1)S(1)}, bf16[2,128,256]{2,1,0:T(8,128)(2,1)S(1)}, u32[]{:S(2)}, u32[]{:S(2)}) collective-permute-start(bf16[2,128,256]{2,1,0:T(8,128)(2,1)S(1)} %get-tuple-element.23), channel_id=1, source_target_pairs={{0,16},{8,24},{16,32},{24,40},{32,48},{40,56},{48,0},{56,8},{64,80... | collective-permute-start | bytes 393224 | tf_op jit(solution)/shard_map/ppermute | solution.py:186
  15.0 6.8 %collective-permute-start.3 = (bf16[2,128,256]{2,1,0:T(8,128)(2,1)S(1)}, bf16[2,128,256]{2,1,0:T(8,128)(2,1)S(1)}, u32[]{:S(2)}, u32[]{:S(2)}) collective-permute-start(bf16[2,128,256]{2,1,0:T(8,128)(2,1)S(1)} %get-tuple-element.23), channel_id=1, source_target_pairs={{0,48},{8,56},{16,0},{24,8},{32,16},{40,24},{48,32},{56,40},{64,11... | collective-permute-start | bytes 393224 | tf_op jit(solution)/shard_map/ppermute | solution.py:186
  21.8 29.1 %copy-start = (bf16[128,2048]{1,0:T(8,128)(2,1)S(1)}, bf16[128,2048]{1,0:T(8,128)(2,1)}, u32[]{:S(2)}) copy-start(bf16[128,2048]{1,0:T(8,128)(2,1)} %q_ref.1) | copy-start | bytes 1572868
  21.8 29.1 %copy-start.1 = (bf16[128,2048]{1,0:T(8,128)(2,1)S(1)}, bf16[128,2048]{1,0:T(8,128)(2,1)}, u32[]{:S(2)}) copy-start(bf16[128,2048]{1,0:T(8,128)(2,1)} %o_ref.1) | copy-start | bytes 1572868
  21.8 12.6 %collective-permute-start.6 = (bf16[4,2,128,256]{3,2,1,0:T(8,128)(2,1)S(1)}, bf16[4,2,128,256]{3,2,1,0:T(8,128)(2,1)S(1)}, u32[]{:S(2)}, u32[]{:S(2)}) collective-permute-start(bf16[4,2,128,256]{3,2,1,0:T(8,128)(2,1)S(1)} %pad_maximum_fusion), channel_id=1, source_target_pairs={{0,192},{8,200},{16,208},{24,216},{32,224},{40,232},{48,240},{56,2... | collective-permute-start | bytes 1572872 | tf_op jit(solution)/shard_map/ppermute | solution.py:186
  24.3 13.1 %collective-permute-start.5 = (bf16[4,2,128,256]{3,2,1,0:T(8,128)(2,1)S(1)}, bf16[4,2,128,256]{3,2,1,0:T(8,128)(2,1)S(1)}, u32[]{:S(2)}, u32[]{:S(2)}) collective-permute-start(bf16[4,2,128,256]{3,2,1,0:T(8,128)(2,1)S(1)} %pad_maximum_fusion), channel_id=1, source_target_pairs={{0,128},{8,136},{16,144},{24,152},{32,160},{40,168},{48,176},{56,1... | collective-permute-start | bytes 1572872 | tf_op jit(solution)/shard_map/ppermute | solution.py:186
  24.6 26.2 %collective-permute-start.4 = (bf16[4,2,128,256]{3,2,1,0:T(8,128)(2,1)S(1)}, bf16[4,2,128,256]{3,2,1,0:T(8,128)(2,1)S(1)}, u32[]{:S(2)}, u32[]{:S(2)}) collective-permute-start(bf16[4,2,128,256]{3,2,1,0:T(8,128)(2,1)S(1)} %pad_maximum_fusion), channel_id=1, source_target_pairs={{0,64},{8,72},{16,80},{24,88},{32,96},{40,104},{48,112},{56,120},{... | collective-permute-start | bytes 1572872 | tf_op jit(solution)/shard_map/ppermute | solution.py:186
  50.9 0.7 copy-start.3
  50.9 0.7 copy-start.4
  58.0 22.7 %collective-permute-start.7 = (bf16[1024,256]{1,0:T(8,128)(2,1)S(1)}, bf16[1024,256]{1,0:T(8,128)(2,1)S(1)}, u32[]{:S(2)}, u32[]{:S(2)}) collective-permute-start(bf16[1024,256]{1,0:T(8,128)(2,1)S(1)} %get-tuple-element.12), channel_id=1, source_target_pairs={{0,192},{8,200},{16,208},{24,216},{32,224},{40,232},{48,240},{56,2... | collective-permute-start | bytes 1572872 | tf_op jit(solution)/shard_map/ppermute | solution.py:186
  61.5 20.8 %collective-permute-start.8 = (bf16[1024,256]{1,0:T(8,128)(2,1)S(1)}, bf16[1024,256]{1,0:T(8,128)(2,1)S(1)}, u32[]{:S(2)}, u32[]{:S(2)}) collective-permute-start(bf16[1024,256]{1,0:T(8,128)(2,1)S(1)} %get-tuple-element.13), channel_id=1, source_target_pairs={{0,128},{8,136},{16,144},{24,152},{32,160},{40,168},{48,176},{56,1... | collective-permute-start | bytes 1572872 | tf_op jit(solution)/shard_map/ppermute | solution.py:186
  71.8 23.6 %collective-permute-start.9 = (bf16[1024,256]{1,0:T(8,128)(2,1)S(1)}, bf16[1024,256]{1,0:T(8,128)(2,1)S(1)}, u32[]{:S(2)}, u32[]{:S(2)}) collective-permute-start(bf16[1024,256]{1,0:T(8,128)(2,1)S(1)} %get-tuple-element.14), channel_id=1, source_target_pairs={{0,64},{8,72},{16,80},{24,88},{32,96},{40,104},{48,112},{56,120},{... | collective-permute-start | bytes 1572872 | tf_op jit(solution)/shard_map/ppermute | solution.py:186
  95.8 8.9 %collective-permute-start.12 = (bf16[2,128,256]{2,1,0:T(8,128)(2,1)S(1)}, bf16[2,128,256]{2,1,0:T(8,128)(2,1)S(1)}, u32[]{:S(2)}, u32[]{:S(2)}) collective-permute-start(bf16[2,128,256]{2,1,0:T(8,128)(2,1)S(1)} %bitcast.36), channel_id=1, source_target_pairs={{0,16},{8,24},{16,32},{24,40},{32,48},{40,56},{48,0},{56,8},{64,80... | collective-permute-start | bytes 393224 | tf_op jit(solution)/shard_map/ppermute | solution.py:186
  95.9 10.1 %collective-permute-start.10 = (bf16[2,128,256]{2,1,0:T(8,128)(2,1)S(1)}, bf16[2,128,256]{2,1,0:T(8,128)(2,1)S(1)}, u32[]{:S(2)}, u32[]{:S(2)}) collective-permute-start(bf16[2,128,256]{2,1,0:T(8,128)(2,1)S(1)} %bitcast.34), channel_id=1, source_target_pairs={{0,48},{8,56},{16,0},{24,8},{32,16},{40,24},{48,32},{56,40},{64,11... | collective-permute-start | bytes 393224 | tf_op jit(solution)/shard_map/ppermute | solution.py:186
  98.5 10.9 %collective-permute-start.11 = (bf16[2,128,256]{2,1,0:T(8,128)(2,1)S(1)}, bf16[2,128,256]{2,1,0:T(8,128)(2,1)S(1)}, u32[]{:S(2)}, u32[]{:S(2)}) collective-permute-start(bf16[2,128,256]{2,1,0:T(8,128)(2,1)S(1)} %bitcast.32), channel_id=1, source_target_pairs={{0,32},{8,40},{16,48},{24,56},{32,0},{40,8},{48,16},{56,24},{64,96... | collective-permute-start | bytes 393224 | tf_op jit(solution)/shard_map/ppermute | solution.py:186
  109.5 7.1 %collective-permute-start.13 = (bf16[128,256]{1,0:T(8,128)(2,1)S(1)}, bf16[128,256]{1,0:T(8,128)(2,1)S(1)}, u32[]{:S(2)}, u32[]{:S(2)}) collective-permute-start(bf16[128,256]{1,0:T(8,128)(2,1)S(1)} %fusion.4), channel_id=1, source_target_pairs={{0,8},{8,0},{16,24},{24,16},{32,40},{40,32},{48,56},{56,48},{64,72... | collective-permute-start | bytes 196616 | tf_op jit(solution)/shard_map/ppermute | solution.py:186
  119.3 24.2 %all-to-all-start = ((f32[256,1,1]{2,1,0:T(1,128)}), f32[256,1,1]{2,1,0:T(1,128)S(1)}, u32[]{:S(2)}, u32[]{:S(2)}) async-start(f32[256,1,1]{2,1,0:T(1,128)} %broadcast_in_dim.3), calls=%async_computation | async-start | bytes 262144 | tf_op jit(solution)/shard_map/all_to_all | solution.py:209

commit v2 on v1

v2 whole, which is shorter than its diff:
```python
import jax
import jax.numpy as jnp
from jax import lax
from jax.experimental import pallas as pl
from jax.experimental.pallas import tpu as pltpu
from jax.sharding import Mesh
from jax.sharding import PartitionSpec as P

HD = 128
GROUP = 16
SPAN = 64
SPANS = 64
NY, NX, NZ = 4, 4, 2
ROWS = SPAN * GROUP
TILE = 512
TOTAL = SPAN * SPANS
SCALE = HD ** (-0.5)
LOG2E = 1.4426950408889634
NEG = -1e30
VMEM = 36 * 1024 * 1024

f32, bf16, i32 = jnp.float32, jnp.bfloat16, jnp.int32


def nt(a, b):
    return lax.dot_general(a, b, (((1,), (1,)), ((), ())), preferred_element_type=f32)


def nn(a, b):
    return lax.dot_general(a, b, (((1,), (0,)), ((), ())), preferred_element_type=f32)


def tn(a, b):
    return lax.dot_general(a, b, (((0,), (0,)), ((), ())), preferred_element_type=f32)


def position():
    y, x, z = lax.axis_index("y"), lax.axis_index("x"), lax.axis_index("zh")
    return y, x, z, (y * NX + x) * NZ + z


def slot_place(meta_ref, slot):
    return pl.multiple_of(meta_ref[slot] * SPAN, SPAN)


def each_query_span(meta_ref, body):
    me = position()[3]
    ends, total = [], 0
    for d in range(meta_ref.shape[0] - SPANS):
        total = total + meta_ref[SPANS + d]
        ends.append(total)
    lane = lax.broadcasted_iota(i32, (1, ROWS), 1)
    for a in range(2):
        span = meta_ref[me * 2 + a]
        place = span * SPAN + (lane & (SPAN - 1))
        begin = jnp.zeros_like(place)
        first, last = 0, 0
        for end in ends:
            begin = jnp.maximum(begin, jnp.where(end <= place, end, 0))
            first = jnp.maximum(first, jnp.where(end <= span * SPAN, end, 0))
            last = jnp.maximum(last, jnp.where(end <= span * SPAN + SPAN - 1, end, 0))
        start = (first // SPAN) * SPAN
        count = (span * SPAN + SPAN - start + TILE - 1) // TILE

        def visible(k0, c, n, place=place, begin=begin):
            kp = k0 + lax.broadcasted_iota(i32, (TILE, 1), 0)
            return (kp <= place[:, c : c + n]) & (kp >= begin[:, c : c + n])

        def tiles(step, masked=True, start=start, count=count, span=span, last=last):
            def one(t, carry):
                k0 = pl.multiple_of(start + t * TILE, SPAN)
                whole = (k0 >= last) & (k0 + TILE <= span * SPAN + 1)
                if not masked:
                    step(t, k0, None)
                    return carry

                @pl.when(whole)
                def _():
                    step(t, k0, lambda a, b, c=0, n=ROWS: a)

                @pl.when(jnp.logical_not(whole))
                def _():
                    step(t, k0, lambda a, b, c=0, n=ROWS: jnp.where(visible(k0, c, n), a, b))

                return carry

            lax.fori_loop(0, count, one, 0)

        body(a, pl.ds(a * ROWS, ROWS), tiles)


def sorted_blocks(meta_ref, ks, vs, kseq, vseq):
    y, x, z, _ = position()
    for sy in range(NY):
        for sx in range(NX):
            for zz in range(NZ * 2):
                home = ((y + NY - sy) % NY) * NX + (x + NX - sx) % NX
                at = slot_place(meta_ref, (home * NZ + (z + zz // 2) % NZ) * 2 + zz % 2)
                kseq[pl.ds(at, SPAN), :] = ks[sy][pl.ds((sx * 2 * NZ + zz) * SPAN, SPAN), :]
                vseq[pl.ds(at, SPAN), :] = vs[sx][pl.ds((sy * 2 * NZ + zz) * SPAN, SPAN), :]
    kseq[pl.ds(TOTAL, TILE), :] = jnp.zeros((TILE, HD), bf16)
    vseq[pl.ds(TOTAL, TILE), :] = jnp.zeros((TILE, HD), bf16)


def prepare_kernel(q_ref, o_ref, g_ref, qs, gs, qt, gt, delta):
    for a in range(2):
        prods = []
        for h in range(GROUP):
            dst = pl.ds(a * ROWS + h * SPAN, SPAN)
            src = (pl.ds(a * SPAN, SPAN), pl.ds(h * HD, HD))
            qs[dst, :] = q_ref[src]
            gs[dst, :] = g_ref[src]
            prods.append(g_ref[src].astype(f32) * o_ref[src].astype(f32))
        rows = pl.ds(a * ROWS, ROWS)
        qt[:, rows] = qs[rows, :].T
        gt[:, rows] = gs[rows, :].T
        prod = jnp.concatenate(prods, axis=0)
        high = prod.astype(bf16)
        low = (prod - high.astype(f32)).astype(bf16)
        ones = jnp.ones((16, HD), bf16)
        delta[pl.ds(a * 8, 8), :] = (nt(ones, high) + nt(ones, low))[:8]


def key_value_kernel(
    meta_ref, qs, gs, qt, gt, delta_ref, k0, k1, k2, k3, v0, v1, v2, v3,
    dkv_ref, lse_ref, kseq, vseq, acc, weights, peaks, peak, mass,
):
    sorted_blocks(meta_ref, (k0, k1, k2, k3), (v0, v1, v2, v3), kseq, vseq)
    acc[...] = jnp.zeros_like(acc)

    def span(a, rows, tiles):
        peak[...] = jnp.full_like(peak, NEG)
        mass[...] = jnp.zeros_like(mass)

        def stats(t, at, pick):
            k = kseq[pl.ds(at, TILE), :]
            for c in range(0, ROWS, 256):
                cols = pl.ds(c, 256)
                s = pick(nn(k, qt[:, pl.ds(a * ROWS + c, 256)]), NEG, c, 256)
                old = peak[:, cols]
                fresh = jnp.maximum(old, jnp.max(s, axis=0, keepdims=True))
                e = jnp.exp2(s * (SCALE * LOG2E) - fresh * (SCALE * LOG2E))
                mass[:, cols] = mass[:, cols] * jnp.exp2((old - fresh) * (SCALE * LOG2E)) + jnp.sum(
                    e, axis=0, keepdims=True
                )
                peak[:, cols] = fresh
                peaks[t, :, cols] = jnp.broadcast_to(fresh, (8, 256))
                weights[t, :, cols] = e

        tiles(stats)
        lse = peak[...] * (SCALE * LOG2E) + jnp.log2(mass[...])
        lse_ref[pl.ds(a * 8, 8), :] = jnp.broadcast_to(lse, (8, ROWS))
        delta, high, inverse = delta_ref[pl.ds(a * 8, 1), :], peak[...], 1.0 / mass[...]

        def step(t, at, pick):
            v = vseq[pl.ds(at, TILE), :]
            dk, dv = acc[pl.ds(at, TILE), :HD], acc[pl.ds(at, TILE), HD:]
            for c in range(0, ROWS, 256):
                cols, some = pl.ds(c, 256), pl.ds(a * ROWS + c, 256)
                w = jnp.exp2((peaks[t, :, cols][:1] - high[:, c : c + 256]) * (SCALE * LOG2E)) * inverse[:, c : c + 256]
                p = weights[t, :, cols] * w
                ds = p * (nn(v, gt[:, some]) - delta[:, c : c + 256])
                dv = dv + nn(p.astype(bf16), gs[some, :])
                dk = dk + nn(ds.astype(bf16), qs[some, :])
            acc[pl.ds(at, TILE), :HD] = dk
            acc[pl.ds(at, TILE), HD:] = dv

        tiles(step, masked=False)

    each_query_span(meta_ref, span)
    for slot in range(SPANS):
        at = slot_place(meta_ref, slot)
        row = pl.ds(slot * SPAN, SPAN)
        dkv_ref[row, :HD] = (acc[pl.ds(at, SPAN), :HD] * SCALE).astype(bf16)
        dkv_ref[row, HD:] = acc[pl.ds(at, SPAN), HD:].astype(bf16)


def query_kernel(
    meta_ref, qt, gt, delta_ref, lse_ref, k0, k1, k2, k3, v0, v1, v2, v3,
    dq_ref, sq_ref, kseq, vseq, acc,
):
    sorted_blocks(meta_ref, (k0, k1, k2, k3), (v0, v1, v2, v3), kseq, vseq)
    square = []

    def span(a, rows, tiles):
        lse, delta = lse_ref[pl.ds(a * 8, 1), :], delta_ref[pl.ds(a * 8, 1), :]
        acc[...] = jnp.zeros_like(acc)

        def step(t, at, pick):
            k = kseq[pl.ds(at, TILE), :]
            p = pick(jnp.exp2(nn(k, qt[:, rows]) * (SCALE * LOG2E) - lse), 0.0)
            ds = p * (nn(vseq[pl.ds(at, TILE), :], gt[:, rows]) - delta)
            acc[...] += tn(k, ds.astype(bf16))

        tiles(step)
        dq = (acc[...] * SCALE).T.astype(bf16)
        for h in range(GROUP):
            dq_ref[pl.ds(a * SPAN, SPAN), pl.ds(h * HD, HD)] = dq[h * SPAN : (h + 1) * SPAN]
        dq = dq.astype(f32)
        square.append(jnp.sum(jnp.sum(dq * dq, axis=0, keepdims=True), axis=1, keepdims=True))

    each_query_span(meta_ref, span)
    sq_ref[...] = jnp.broadcast_to(square[0] + square[1], sq_ref.shape)


def call(kernel, outs, smem, scratch, flops, *args):
    vm = pl.BlockSpec(memory_space=pltpu.VMEM)
    sm = pl.BlockSpec(memory_space=pltpu.SMEM)
    return pl.pallas_call(
        kernel,
        out_shape=tuple(jax.ShapeDtypeStruct(s, t) for s, t in outs),
        in_specs=[sm] * smem + [vm] * (len(args) - smem),
        out_specs=(vm,) * len(outs),
        scratch_shapes=[pltpu.VMEM(s, t) for s, t in scratch],
        compiler_params=pltpu.CompilerParams(vmem_limit_bytes=VMEM),
        cost_estimate=pl.CostEstimate(flops=flops, bytes_accessed=4 << 20, transcendentals=0),
    )(*args)


def shift(a, axis, step):
    n = lax.axis_size(axis)
    return lax.ppermute(a, axis, [(i, (i + step) % n) for i in range(n)])


def shards(queries, keys, values, outputs, out_grad, doc_lengths, span_perm):
    tq = queries.shape[0]
    k = jnp.stack([keys, shift(keys, "zh", 1)])
    v = jnp.stack([values, shift(values, "zh", 1)])
    k = [k] + [shift(k, "x", s) for s in range(1, NX)]
    v = [v] + [shift(v, "y", s) for s in range(1, NY)]
    k, v = lax.optimization_barrier((k, v))
    k, v = jnp.stack(k), jnp.stack(v)
    k = [k] + [shift(k, "y", s) for s in range(1, NY)]
    v = [v] + [shift(v, "x", s) for s in range(1, NX)]
    k = [a.reshape(TOTAL // NY, HD) for a in k]
    v = [a.reshape(TOTAL // NX, HD) for a in v]

    meta = jnp.concatenate([span_perm, doc_lengths])
    heads, turned = ((2 * ROWS, HD), bf16), ((HD, 2 * ROWS), bf16)
    row, one, longer = ((16, ROWS), f32), ((1, ROWS), f32), ((TOTAL + TILE, HD), bf16)
    most = -(-(TOTAL // 2 + SPAN) // TILE)
    qs, gs, qt, gt, delta = call(
        prepare_kernel,
        [heads, heads, turned, turned, row],
        0, [], 1 << 30, queries, outputs, out_grad,
    )
    parts, lse = call(
        key_value_kernel,
        [((TOTAL, 2 * HD), bf16), row],
        1,
        [
            longer, longer,
            ((TOTAL + TILE, 2 * HD), f32),
            ((most, TILE, ROWS), f32),
            ((most, 8, ROWS), f32),
            one, one,
        ],
        16 << 30,
        meta, qs, gs, qt, gt, delta, *k, *v,
    )
    parts = parts.reshape(NY * NX, NZ, tq, 2 * HD)
    parts = lax.all_to_all(parts, ("y", "x"), 0, 0)
    query_grad, square = call(
        query_kernel,
        [(queries.shape, bf16), ((8, HD), f32)],
        1,
        [longer, longer, ((HD, ROWS), f32)],
        16 << 30,
        meta, qt, gt, delta, lse, *k, *v,
    )
    parts, query_grad, square = lax.optimization_barrier((parts, query_grad, square))
    z = lax.axis_index("zh")

    def total(index):
        part = lax.dynamic_index_in_dim(parts, index, 1, False)
        return jnp.sum(part.astype(f32), axis=0)

    other = shift(total(1 - z).astype(bf16), "zh", 1)
    both = (total(z) + other.astype(f32)).astype(bf16)
    wide = both.astype(f32)
    local = jnp.sum(wide * wide) + square[0, 0]
    every = ("y", "x", "zh", "tp")
    world = lax.axis_size(every)
    grad_square = jnp.sum(lax.all_to_all(jnp.broadcast_to(local, (world, 1)), every, 0, 0))
    return (query_grad, both[:, :HD], both[:, HD:], grad_square)


def solution(mesh):
    tp = mesh.devices.shape[1]
    split = Mesh(mesh.devices.reshape(NY, NX, NZ, tp), ("y", "x", "zh", "tp"))
    both = P(("y", "x", "zh"), "tp")
    return jax.shard_map(
        shards,
        mesh=split,
        in_specs=(both,) * 5 + (P(), P()),
        out_specs=(both, both, both, P()),
        check_vma=False,
    )
```

time: 145 us -> 128 us (0.88)
  waiting for transfers between devices: 76 us -> 42.5 us
  Pallas kernels: 6.45 us -> 17.5 us
  other arithmetic: 1.93 us -> 5.93 us
    ppermute x14 -> x15, waiting for transfers between devices: 63.8 us -> 11.4 us  [shift(): return lax.ppermute(a, axis, [(i, (i + step) % n) for i in range(n)])]
    all_to_all x1 -> x2, waiting for transfers between devices: 12.2 us -> 31.1 us  [the longest x1 18.9 us: shards(): parts = lax.all_to_all(parts, ('y', 'x'), 0, 0)]
    all_to_all x1 -> x2, starting transfers between devices: 11.3 us -> 27.4 us  [the longest x1 14.2 us: shards(): lax.all_to_all(jnp.broadcast_to(local, (world, 1)), every, 0, 0)]
    ppermute x14 -> x15, starting transfers between devices: 42.5 us -> 27.2 us  [shift(): return lax.ppermute(a, axis, [(i, (i + step) % n) for i in range(n)])]
    pallas_call x1 -> x3, Pallas kernels: 6.45 us -> 17.5 us  [call(): pl.pallas_call(kernel, out_shape=tuple((jax.ShapeDtypeStruct(s, t) for s,...]
    reduce_sum x1 -> x3, other arithmetic: 0.87 us -> 3.62 us  [the longest x2 2.75 us: total(): return jnp.sum(part.astype(f32), axis=0)]
    unnamed x11 -> x10, local copies, waits for them, and re-layouts: 1.49 us -> 3.13 us
    another operation x2 -> x4, other arithmetic: 0.09 us -> 1.6 us  [the longest x1 0.76 us: shards(): k = jnp.stack([keys, shift(keys, 'zh', 1)])]
  transfers between devices with their start and end apart: 15 -> 17, of which waited for: 12 -> 9; matrix products, arithmetic and copies ran while one was open for 1% -> 3% of each run, Pallas kernels for 0% -> 5%
where the time goes in v2:
time: 128 us
  starting transfers between devices  54.7 us (43%)
  waiting for transfers between devices  42.5 us (33%)
  Pallas kernels  17.5 us (14%)
  other arithmetic  5.93 us (5%)
  local copies, waits for them, and re-layouts  4.99 us (4%)
  between operations  2 us (2%)
    ppermute x15, starting transfers between devices, shift(): return lax.ppermute(a, axis, [(i, (i + step) % n) for i in range(n)])  27.2 us
    all_to_all x1, waiting for transfers between devices, shards(): parts = lax.all_to_all(parts, ('y', 'x'), 0, 0)  18.9 us
    pallas_call x3, Pallas kernels, call(): pl.pallas_call(kernel, out_shape=tuple((jax.ShapeDtypeStruct(s, t) for s,...  17.5 us
    all_to_all x1, starting transfers between devices, shards(): lax.all_to_all(jnp.broadcast_to(local, (world, 1)), every, 0, 0)  14.2 us
    all_to_all x1, starting transfers between devices, shards(): parts = lax.all_to_all(parts, ('y', 'x'), 0, 0)  13.3 us
    all_to_all x1, waiting for transfers between devices, shards(): lax.all_to_all(jnp.broadcast_to(local, (world, 1)), every, 0, 0)  12.2 us
    ppermute x15, waiting for transfers between devices, shift(): return lax.ppermute(a, axis, [(i, (i + step) % n) for i in range(n)])  11.4 us
    unnamed x10, local copies, waits for them, and re-layouts  3.13 us
  transfers between devices with their start and end apart: 17, of which 9 were waited for; matrix products, arithmetic and copies ran while one was open for 3% of the time, Pallas kernels for 5%

profile of v2, /device:TPU:1, one launch (start us, length us, event | category | flops | bytes accessed | tf_op | source)
XLA Modules:
  0.0 127.6 jit_solution(14028001693107050079)
XLA Ops:
  0.6 7.8 %collective-permute-start = (bf16[128,128]{1,0:T(8,128)(2,1)}, bf16[128,128]{1,0:T(8,128)(2,1)S(1)}, u32[]{:S(2)}, u32[]{:S(2)}) collective-permute-start(bf16[128,128]{1,0:T(8,128)(2,1)} %param.8), channel_id=1, source_target_pairs={{0,8},{8,0},{1,9},{9,1},{2,10},{10,2},{3,11},{11,3},{4,12},{12,4},... | collective-permute-start | bytes 98312 | tf_op jit(solution)/shard_map/ppermute | solution.py:222
  8.6 1.4 %collective-permute-done = bf16[128,128]{1,0:T(8,128)(2,1)S(1)} collective-permute-done((bf16[128,128]{1,0:T(8,128)(2,1)}, bf16[128,128]{1,0:T(8,128)(2,1)S(1)}, u32[]{:S(2)}, u32[]{:S(2)}) %collective-permute-start) | collective-permute-done | bytes 32800 | tf_op jit(solution)/shard_map/ppermute | solution.py:222
  10.7 1.2 collective-permute-start.1
  11.9 2.5 %collective-permute-start.2 = (bf16[2,128,128]{2,1,0:T(8,128)(2,1)S(1)}, bf16[2,128,128]{2,1,0:T(8,128)(2,1)S(1)}, u32[]{:S(2)}, u32[]{:S(2)}) collective-permute-start(bf16[2,128,128]{2,1,0:T(8,128)(2,1)S(1)} %pad_maximum_fusion.2), channel_id=1, source_target_pairs={{0,32},{16,48},{32,0},{48,16},{1,33},{17,49},{33,1},{49,17},{2,34}... | collective-permute-start | bytes 196616 | tf_op jit(solution)/shard_map/ppermute | solution.py:222
  14.4 1.2 collective-permute-start.3
  16.5 1.3 %collective-permute-start.5 = (bf16[2,128,128]{2,1,0:T(8,128)(2,1)S(1)}, bf16[2,128,128]{2,1,0:T(8,128)(2,1)S(1)}, u32[]{:S(2)}, u32[]{:S(2)}) collective-permute-start(bf16[2,128,128]{2,1,0:T(8,128)(2,1)S(1)} %pad_maximum_fusion.3), channel_id=1, source_target_pairs={{0,64},{64,128},{128,192},{192,0},{1,65},{65,129},{129,193},{193,1... | collective-permute-start | bytes 196616 | tf_op jit(solution)/shard_map/ppermute | solution.py:222
  17.8 2.6 %collective-permute-start.6 = (bf16[2,128,128]{2,1,0:T(8,128)(2,1)S(1)}, bf16[2,128,128]{2,1,0:T(8,128)(2,1)S(1)}, u32[]{:S(2)}, u32[]{:S(2)}) collective-permute-start(bf16[2,128,128]{2,1,0:T(8,128)(2,1)S(1)} %pad_maximum_fusion.3), channel_id=1, source_target_pairs={{0,128},{64,192},{128,0},{192,64},{1,129},{65,193},{129,1},{193,65... | collective-permute-start | bytes 196616 | tf_op jit(solution)/shard_map/ppermute | solution.py:222
  20.4 1.1 collective-permute-start.7
  21.5 1.3 collective-permute-done.6
  23.8 1.2 collective-permute-start.11
  25.1 2.5 %collective-permute-start.12 = (bf16[4,2,128,128]{3,2,1,0:T(8,128)(2,1)S(1)}, bf16[4,2,128,128]{3,2,1,0:T(8,128)(2,1)S(1)}, u32[]{:S(2)}, u32[]{:S(2)}) collective-permute-start(bf16[4,2,128,128]{3,2,1,0:T(8,128)(2,1)S(1)} %pad_maximum_fusion.1), channel_id=1, source_target_pairs={{0,32},{16,48},{32,0},{48,16},{1,33},{17,49},{33,1},{49,17},{2,34}... | collective-permute-start | bytes 786440 | tf_op jit(solution)/shard_map/ppermute | solution.py:222
  27.5 1.2 collective-permute-start.13
  28.7 2.0 %collective-permute-start.9 = (bf16[4,2,128,128]{3,2,1,0:T(8,128)(2,1)S(1)}, bf16[4,2,128,128]{3,2,1,0:T(8,128)(2,1)S(1)}, u32[]{:S(2)}, u32[]{:S(2)}) collective-permute-start(bf16[4,2,128,128]{3,2,1,0:T(8,128)(2,1)S(1)} %pad_maximum_fusion), channel_id=1, source_target_pairs={{0,128},{64,192},{128,0},{192,64},{1,129},{65,193},{129,1},{193,65... | collective-permute-start | bytes 786440 | tf_op jit(solution)/shard_map/ppermute | solution.py:222
  36.0 2.9 %collective-permute-done.10 = bf16[4,2,128,128]{3,2,1,0:T(8,128)(2,1)S(1)} collective-permute-done((bf16[4,2,128,128]{3,2,1,0:T(8,128)(2,1)S(1)}, bf16[4,2,128,128]{3,2,1,0:T(8,128)(2,1)S(1)}, u32[]{:S(2)}, u32[]{:S(2)}) %collective-permute-start.10) | collective-permute-done | bytes 262176 | tf_op jit(solution)/shard_map/ppermute | solution.py:222
  39.4 10.7 %shard_map.103 = (bf16[4096,256]{1,0:T(8,128)(2,1)}, f32[16,1024]{1,0:T(8,128)S(1)}) custom-call(s32[72]{0:T(128)S(1)} %pad_add_fusion.meta_ref, bf16[2048,128]{1,0:T(8,128)(2,1)S(1)} %get-tuple-element.24.qs, bf16[2048,128]{1,0:T(8,128)(2,1)S(1)} %get-tuple-element.25.gs, bf16[128,2048]{1,0:T(8,128)(2,1)S(1)} %get-tuple-element.26.qt, ...), custom_call_target="tpu_custom_call" | custom-call | flops 17179869184 | bytes 4194304 | tf_op jit(solution)/shard_map/pallas_call | solution.py:209
  50.1 13.3 %all-to-all-start = ((bf16[16,2,128,256]{3,2,1,0:T(8,128)(2,1)}), bf16[16,2,128,256]{3,2,1,0:T(8,128)(2,1)}, u32[]{:S(2)}, u32[]{:S(2)}) async-start(bf16[16,2,128,256]{3,2,1,0:T(8,128)(2,1)} %bitcast.20), calls=%async_computation | async-start | bytes 4194304 | tf_op jit(solution)/shard_map/all_to_all | solution.py:262
  63.4 6.3 %shard_map.104 = (bf16[128,2048]{1,0:T(8,128)(2,1)}, f32[8,128]{1,0:T(8,128)S(1)}) custom-call(s32[72]{0:T(128)S(1)} %pad_add_fusion.meta_ref, bf16[128,2048]{1,0:T(8,128)(2,1)S(1)} %get-tuple-element.26.qt, bf16[128,2048]{1,0:T(8,128)(2,1)S(1)} %get-tuple-element.27.gt, f32[16,1024]{1,0:T(8,128)S(1)} %get-tuple-element.28.delta_ref, ...), custom_call_target="tpu_custom_call" | custom-call | flops 17179869184 | bytes 4194304 | tf_op jit(solution)/shard_map/pallas_call | solution.py:209
  69.6 18.9 %all-to-all-done = bf16[16,2,128,256]{3,2,1,0:T(8,128)(2,1)} async-done(((bf16[16,2,128,256]{3,2,1,0:T(8,128)(2,1)}), bf16[16,2,128,256]{3,2,1,0:T(8,128)(2,1)}, u32[]{:S(2)}, u32[]{:S(2)}) %all-to-all-start) | async-done | bytes 2097184 | tf_op jit(solution)/shard_map/all_to_all | solution.py:262
  88.5 1.4 %dynamic-slice_reduce_fusion = bf16[128,256]{1,0:T(8,128)(2,1)S(1)} fusion(bf16[16,2,128,256]{3,2,1,0:T(8,128)(2,1)} %all-to-all-done, s32[]{:T(128)S(6)} %select_n.8), kind=kLoop, calls=%fused_computation.1 | loop fusion | flops 491520 | bytes 1114116 | tf_op jit(solution)/shard_map/reduce_sum | solution.py:276
  89.9 1.1 collective-permute-start.14
  91.5 1.4 %convert_reduce_fusion = f32[128,256]{1,0:T(8,128)S(1)} fusion(bf16[16,2,128,256]{3,2,1,0:T(8,128)(2,1)} %all-to-all-done, s32[]{:T(128)S(6)} %select_n.7), kind=kLoop, calls=%fused_computation | loop fusion | flops 1015808 | bytes 1179652 | tf_op jit(solution)/shard_map/reduce_sum | solution.py:276
  92.9 4.1 %collective-permute-done.14 = bf16[128,256]{1,0:T(8,128)(2,1)S(1)} collective-permute-done((bf16[128,256]{1,0:T(8,128)(2,1)S(1)}, bf16[128,256]{1,0:T(8,128)(2,1)S(1)}, u32[]{:S(2)}, u32[]{:S(2)}) %collective-permute-start.14) | collective-permute-done | bytes 65568 | tf_op jit(solution)/shard_map/ppermute | solution.py:222
  99.6 14.2 %all-to-all-start.1 = ((f32[256,1,1]{2,1,0:T(1,128)}), f32[256,1,1]{2,1,0:T(1,128)S(1)}, u32[]{:S(2)}, u32[]{:S(2)}) async-start(f32[256,1,1]{2,1,0:T(1,128)} %broadcast_in_dim.3), calls=%async_computation.1 | async-start | bytes 262144 | tf_op jit(solution)/shard_map/all_to_all | solution.py:284
  114.5 12.2 %all-to-all-done.1 = f32[256,1,1]{2,1,0:T(1,128)S(1)} async-done(((f32[256,1,1]{2,1,0:T(1,128)}), f32[256,1,1]{2,1,0:T(1,128)S(1)}, u32[]{:S(2)}, u32[]{:S(2)}) %all-to-all-start.1) | async-done | bytes 1056 | tf_op jit(solution)/shard_map/all_to_all | solution.py:284
  (35 shorter events, 12.0 us)
Async XLA Ops:
  0.6 9.3 %collective-permute-start = (bf16[128,128]{1,0:T(8,128)(2,1)}, bf16[128,128]{1,0:T(8,128)(2,1)S(1)}, u32[]{:S(2)}, u32[]{:S(2)}) collective-permute-start(bf16[128,128]{1,0:T(8,128)(2,1)} %param.8), channel_id=1, source_target_pairs={{0,8},{8,0},{1,9},{9,1},{2,10},{10,2},{3,11},{11,3},{4,12},{12,4},... | collective-permute-start | bytes 98312 | tf_op jit(solution)/shard_map/ppermute | solution.py:222
  8.5 7.2 %collective-permute-start.4 = (bf16[128,128]{1,0:T(8,128)(2,1)}, bf16[128,128]{1,0:T(8,128)(2,1)S(1)}, u32[]{:S(2)}, u32[]{:S(2)}) collective-permute-start(bf16[128,128]{1,0:T(8,128)(2,1)} %param.9), channel_id=1, source_target_pairs={{0,8},{8,0},{1,9},{9,1},{2,10},{10,2},{3,11},{11,3},{4,12},{12,4},... | collective-permute-start | bytes 98312 | tf_op jit(solution)/shard_map/ppermute | solution.py:222
  10.7 9.6 %collective-permute-start.1 = (bf16[2,128,128]{2,1,0:T(8,128)(2,1)S(1)}, bf16[2,128,128]{2,1,0:T(8,128)(2,1)S(1)}, u32[]{:S(2)}, u32[]{:S(2)}) collective-permute-start(bf16[2,128,128]{2,1,0:T(8,128)(2,1)S(1)} %pad_maximum_fusion.2), channel_id=1, source_target_pairs={{0,16},{16,32},{32,48},{48,0},{1,17},{17,33},{33,49},{49,1},{2,18}... | collective-permute-start | bytes 196616 | tf_op jit(solution)/shard_map/ppermute | solution.py:222
  11.9 9.5 %collective-permute-start.2 = (bf16[2,128,128]{2,1,0:T(8,128)(2,1)S(1)}, bf16[2,128,128]{2,1,0:T(8,128)(2,1)S(1)}, u32[]{:S(2)}, u32[]{:S(2)}) collective-permute-start(bf16[2,128,128]{2,1,0:T(8,128)(2,1)S(1)} %pad_maximum_fusion.2), channel_id=1, source_target_pairs={{0,32},{16,48},{32,0},{48,16},{1,33},{17,49},{33,1},{49,17},{2,34}... | collective-permute-start | bytes 196616 | tf_op jit(solution)/shard_map/ppermute | solution.py:222
  14.4 7.1 %collective-permute-start.3 = (bf16[2,128,128]{2,1,0:T(8,128)(2,1)S(1)}, bf16[2,128,128]{2,1,0:T(8,128)(2,1)S(1)}, u32[]{:S(2)}, u32[]{:S(2)}) collective-permute-start(bf16[2,128,128]{2,1,0:T(8,128)(2,1)S(1)} %pad_maximum_fusion.2), channel_id=1, source_target_pairs={{0,48},{16,0},{32,16},{48,32},{1,49},{17,1},{33,17},{49,33},{2,50}... | collective-permute-start | bytes 196616 | tf_op jit(solution)/shard_map/ppermute | solution.py:222
  16.5 5.0 %collective-permute-start.5 = (bf16[2,128,128]{2,1,0:T(8,128)(2,1)S(1)}, bf16[2,128,128]{2,1,0:T(8,128)(2,1)S(1)}, u32[]{:S(2)}, u32[]{:S(2)}) collective-permute-start(bf16[2,128,128]{2,1,0:T(8,128)(2,1)S(1)} %pad_maximum_fusion.3), channel_id=1, source_target_pairs={{0,64},{64,128},{128,192},{192,0},{1,65},{65,129},{129,193},{193,1... | collective-permute-start | bytes 196616 | tf_op jit(solution)/shard_map/ppermute | solution.py:222
  17.8 5.0 %collective-permute-start.6 = (bf16[2,128,128]{2,1,0:T(8,128)(2,1)S(1)}, bf16[2,128,128]{2,1,0:T(8,128)(2,1)S(1)}, u32[]{:S(2)}, u32[]{:S(2)}) collective-permute-start(bf16[2,128,128]{2,1,0:T(8,128)(2,1)S(1)} %pad_maximum_fusion.3), channel_id=1, source_target_pairs={{0,128},{64,192},{128,0},{192,64},{1,129},{65,193},{129,1},{193,65... | collective-permute-start | bytes 196616 | tf_op jit(solution)/shard_map/ppermute | solution.py:222
  20.4 3.4 %collective-permute-start.7 = (bf16[2,128,128]{2,1,0:T(8,128)(2,1)S(1)}, bf16[2,128,128]{2,1,0:T(8,128)(2,1)S(1)}, u32[]{:S(2)}, u32[]{:S(2)}) collective-permute-start(bf16[2,128,128]{2,1,0:T(8,128)(2,1)S(1)} %pad_maximum_fusion.3), channel_id=1, source_target_pairs={{0,192},{64,0},{128,64},{192,128},{1,193},{65,1},{129,65},{193,129... | collective-permute-start | bytes 196616 | tf_op jit(solution)/shard_map/ppermute | solution.py:222
  23.8 7.3 %collective-permute-start.11 = (bf16[4,2,128,128]{3,2,1,0:T(8,128)(2,1)S(1)}, bf16[4,2,128,128]{3,2,1,0:T(8,128)(2,1)S(1)}, u32[]{:S(2)}, u32[]{:S(2)}) collective-permute-start(bf16[4,2,128,128]{3,2,1,0:T(8,128)(2,1)S(1)} %pad_maximum_fusion.1), channel_id=1, source_target_pairs={{0,16},{16,32},{32,48},{48,0},{1,17},{17,33},{33,49},{49,1},{2,18}... | collective-permute-start | bytes 786440 | tf_op jit(solution)/shard_map/ppermute | solution.py:222
  25.1 10.9 %collective-permute-start.12 = (bf16[4,2,128,128]{3,2,1,0:T(8,128)(2,1)S(1)}, bf16[4,2,128,128]{3,2,1,0:T(8,128)(2,1)S(1)}, u32[]{:S(2)}, u32[]{:S(2)}) collective-permute-start(bf16[4,2,128,128]{3,2,1,0:T(8,128)(2,1)S(1)} %pad_maximum_fusion.1), channel_id=1, source_target_pairs={{0,32},{16,48},{32,0},{48,16},{1,33},{17,49},{33,1},{49,17},{2,34}... | collective-permute-start | bytes 786440 | tf_op jit(solution)/shard_map/ppermute | solution.py:222
  27.5 8.5 %collective-permute-start.13 = (bf16[4,2,128,128]{3,2,1,0:T(8,128)(2,1)S(1)}, bf16[4,2,128,128]{3,2,1,0:T(8,128)(2,1)S(1)}, u32[]{:S(2)}, u32[]{:S(2)}) collective-permute-start(bf16[4,2,128,128]{3,2,1,0:T(8,128)(2,1)S(1)} %pad_maximum_fusion.1), channel_id=1, source_target_pairs={{0,48},{16,0},{32,16},{48,32},{1,49},{17,1},{33,17},{49,33},{2,50}... | collective-permute-start | bytes 786440 | tf_op jit(solution)/shard_map/ppermute | solution.py:222
  28.7 7.2 %copy-start.3 = (s32[8]{0:T(128)S(1)}, s32[8]{0:T(128)}, u32[]{:S(2)}) copy-start(s32[8]{0:T(128)} %param.12) | copy-start | bytes 100
  28.7 7.2 %copy-start.4 = (s32[64]{0:T(128)S(1)}, s32[64]{0:T(128)}, u32[]{:S(2)}) copy-start(s32[64]{0:T(128)} %param.13) | copy-start | bytes 772
  28.7 7.3 %collective-permute-start.9 = (bf16[4,2,128,128]{3,2,1,0:T(8,128)(2,1)S(1)}, bf16[4,2,128,128]{3,2,1,0:T(8,128)(2,1)S(1)}, u32[]{:S(2)}, u32[]{:S(2)}) collective-permute-start(bf16[4,2,128,128]{3,2,1,0:T(8,128)(2,1)S(1)} %pad_maximum_fusion), channel_id=1, source_target_pairs={{0,128},{64,192},{128,0},{192,64},{1,129},{65,193},{129,1},{193,65... | collective-permute-start | bytes 786440 | tf_op jit(solution)/shard_map/ppermute | solution.py:222
  30.7 8.1 %collective-permute-start.10 = (bf16[4,2,128,128]{3,2,1,0:T(8,128)(2,1)S(1)}, bf16[4,2,128,128]{3,2,1,0:T(8,128)(2,1)S(1)}, u32[]{:S(2)}, u32[]{:S(2)}) collective-permute-start(bf16[4,2,128,128]{3,2,1,0:T(8,128)(2,1)S(1)} %pad_maximum_fusion), channel_id=1, source_target_pairs={{0,192},{64,0},{128,64},{192,128},{1,193},{65,1},{129,65},{193,129... | collective-permute-start | bytes 786440 | tf_op jit(solution)/shard_map/ppermute | solution.py:222
  31.2 8.2 %collective-permute-start.8 = (bf16[4,2,128,128]{3,2,1,0:T(8,128)(2,1)S(1)}, bf16[4,2,128,128]{3,2,1,0:T(8,128)(2,1)S(1)}, u32[]{:S(2)}, u32[]{:S(2)}) collective-permute-start(bf16[4,2,128,128]{3,2,1,0:T(8,128)(2,1)S(1)} %pad_maximum_fusion), channel_id=1, source_target_pairs={{0,64},{64,128},{128,192},{192,0},{1,65},{65,129},{129,193},{193,1... | collective-permute-start | bytes 786440 | tf_op jit(solution)/shard_map/ppermute | solution.py:222
  32.2 1.0 copy-start
  33.3 1.0 copy-start.1
  34.3 1.0 copy-start.2
  50.1 38.4 %all-to-all-start = ((bf16[16,2,128,256]{3,2,1,0:T(8,128)(2,1)}), bf16[16,2,128,256]{3,2,1,0:T(8,128)(2,1)}, u32[]{:S(2)}, u32[]{:S(2)}) async-start(bf16[16,2,128,256]{3,2,1,0:T(8,128)(2,1)} %bitcast.20), calls=%async_computation | async-start | bytes 4194304 | tf_op jit(solution)/shard_map/all_to_all | solution.py:262
  89.9 7.1 %collective-permute-start.14 = (bf16[128,256]{1,0:T(8,128)(2,1)S(1)}, bf16[128,256]{1,0:T(8,128)(2,1)S(1)}, u32[]{:S(2)}, u32[]{:S(2)}) collective-permute-start(bf16[128,256]{1,0:T(8,128)(2,1)S(1)} %dynamic-slice_reduce_fusion), channel_id=1, source_target_pairs={{0,8},{8,0},{1,9},{9,1},{2,10},{10,2},{3,11},{11,3},{4,12},{12,4},... | collective-permute-start | bytes 196616 | tf_op jit(solution)/shard_map/ppermute | solution.py:222
  99.6 27.1 %all-to-all-start.1 = ((f32[256,1,1]{2,1,0:T(1,128)}), f32[256,1,1]{2,1,0:T(1,128)S(1)}, u32[]{:S(2)}, u32[]{:S(2)}) async-start(f32[256,1,1]{2,1,0:T(1,128)} %broadcast_in_dim.3), calls=%async_computation.1 | async-start | bytes 262144 | tf_op jit(solution)/shard_map/all_to_all | solution.py:284

commit v3 on v2

--- a/solution.py
+++ b/solution.py
@@ -17,7 +17,7 @@
 SCALE = HD ** (-0.5)
 LOG2E = 1.4426950408889634
 NEG = -1e30
-VMEM = 36 * 1024 * 1024
+VMEM = 16 * 1024 * 1024
 
 f32, bf16, i32 = jnp.float32, jnp.bfloat16, jnp.int32
 
@@ -89,17 +89,17 @@
         body(a, pl.ds(a * ROWS, ROWS), tiles)
 
 
-def sorted_blocks(meta_ref, ks, vs, kseq, vseq):
+def sorted_blocks(meta_ref, pieces, seq, keys):
     y, x, z, _ = position()
     for sy in range(NY):
         for sx in range(NX):
             for zz in range(NZ * 2):
                 home = ((y + NY - sy) % NY) * NX + (x + NX - sx) % NX
                 at = slot_place(meta_ref, (home * NZ + (z + zz // 2) % NZ) * 2 + zz % 2)
-                kseq[pl.ds(at, SPAN), :] = ks[sy][pl.ds((sx * 2 * NZ + zz) * SPAN, SPAN), :]
-                vseq[pl.ds(at, SPAN), :] = vs[sx][pl.ds((sy * 2 * NZ + zz) * SPAN, SPAN), :]
-    kseq[pl.ds(TOTAL, TILE), :] = jnp.zeros((TILE, HD), bf16)
-    vseq[pl.ds(TOTAL, TILE), :] = jnp.zeros((TILE, HD), bf16)
+                last, inner = (sy, sx) if keys else (sx, sy)
+                row = pl.ds((inner * 2 * NZ + zz) * SPAN, SPAN)
+                seq[pl.ds(at, SPAN), :] = pieces[last][row, :]
+    seq[pl.ds(TOTAL, TILE), :] = jnp.zeros((TILE, HD), bf16)
 
 
 def prepare_kernel(q_ref, o_ref, g_ref, qs, gs, qt, gt, delta):
@@ -121,16 +121,16 @@
         delta[pl.ds(a * 8, 8), :] = (nt(ones, high) + nt(ones, low))[:8]
 
 
-def key_value_kernel(
-    meta_ref, qs, gs, qt, gt, delta_ref, k0, k1, k2, k3, v0, v1, v2, v3,
-    dkv_ref, lse_ref, kseq, vseq, acc, weights, peaks, peak, mass,
+def score_kernel(
+    meta_ref, qt, k0, k1, k2, k3, weights0, weights1, peaks_ref, top_ref, kseq, peak, mass
 ):
-    sorted_blocks(meta_ref, (k0, k1, k2, k3), (v0, v1, v2, v3), kseq, vseq)
-    acc[...] = jnp.zeros_like(acc)
+    sorted_blocks(meta_ref, (k0, k1, k2, k3), kseq, True)
 
     def span(a, rows, tiles):
         peak[...] = jnp.full_like(peak, NEG)
         mass[...] = jnp.zeros_like(mass)
+
+        weights, peaks = (weights0, weights1)[a], peaks_ref.at[a]
 
         def stats(t, at, pick):
             k = kseq[pl.ds(at, TILE), :]
@@ -148,9 +148,27 @@
                 weights[t, :, cols] = e
 
         tiles(stats)
-        lse = peak[...] * (SCALE * LOG2E) + jnp.log2(mass[...])
+        top_ref[pl.ds(a * 8, 4), :] = jnp.broadcast_to(peak[...], (4, ROWS))
+        top_ref[pl.ds(a * 8 + 4, 4), :] = jnp.broadcast_to(mass[...], (4, ROWS))
+
+    each_query_span(meta_ref, span)
+
+
+def key_value_kernel(
+    meta_ref, qs, gs, gt, delta_ref, top_ref, weights0, weights1, peaks_ref, v0, v1, v2, v3,
+    dkv_ref, lse_ref, vseq, acc,
+):
+    sorted_blocks(meta_ref, (v0, v1, v2, v3), vseq, False)
+    acc[...] = jnp.zeros_like(acc)
+
+    def span(a, rows, tiles):
+        high, mass = top_ref[pl.ds(a * 8, 1), :], top_ref[pl.ds(a * 8 + 4, 1), :]
+        lse = high * (SCALE * LOG2E) + jnp.log2(mass)
         lse_ref[pl.ds(a * 8, 8), :] = jnp.broadcast_to(lse, (8, ROWS))
-        delta, high, inverse = delta_ref[pl.ds(a * 8, 1), :], peak[...], 1.0 / mass[...]
+        inverse = 1.0 / mass
+        delta = delta_ref[pl.ds(a * 8, 1), :]
+
+        weights, peaks = (weights0, weights1)[a], peaks_ref.at[a]
 
         def step(t, at, pick):
             v = vseq[pl.ds(at, TILE), :]
@@ -179,7 +197,8 @@
     meta_ref, qt, gt, delta_ref, lse_ref, k0, k1, k2, k3, v0, v1, v2, v3,
     dq_ref, sq_ref, kseq, vseq, acc,
 ):
-    sorted_blocks(meta_ref, (k0, k1, k2, k3), (v0, v1, v2, v3), kseq, vseq)
+    sorted_blocks(meta_ref, (k0, k1, k2, k3), kseq, True)
+    sorted_blocks(meta_ref, (v0, v1, v2, v3), vseq, False)
     square = []
 
     def span(a, rows, tiles):
@@ -201,6 +220,27 @@
 
     each_query_span(meta_ref, span)
     sq_ref[...] = jnp.broadcast_to(square[0] + square[1], sq_ref.shape)
+
+
+def sum_kernel(parts_ref, other_ref):
+    index = 1 - lax.axis_index("zh")
+    total = parts_ref[0, index].astype(f32)
+    for h in range(1, NY * NX):
+        total = total + parts_ref[h, index].astype(f32)
+    other_ref[...] = total.astype(bf16)
+
+
+def finish_kernel(parts_ref, other_ref, sq_ref, dk_ref, dv_ref, local_ref):
+    index = lax.axis_index("zh")
+    total = parts_ref[0, index].astype(f32)
+    for h in range(1, NY * NX):
+        total = total + parts_ref[h, index].astype(f32)
+    both = (total + other_ref[...].astype(f32)).astype(bf16)
+    dk_ref[...] = both[:, :HD]
+    dv_ref[...] = both[:, HD:]
+    wide = both.astype(f32)
+    local = jnp.sum(jnp.sum(wide * wide, axis=0, keepdims=True), axis=1, keepdims=True)
+    local_ref[...] = jnp.broadcast_to((local + sq_ref[:1, :1])[None], local_ref.shape)
 
 
 def call(kernel, outs, smem, scratch, flops, *args):
@@ -244,19 +284,21 @@
         [heads, heads, turned, turned, row],
         0, [], 1 << 30, queries, outputs, out_grad,
     )
+    weights0, weights1, peaks, top = call(
+        score_kernel,
+        [((most, TILE, ROWS), f32), ((most, TILE, ROWS), f32), ((2, most, 8, ROWS), f32), row],
+        1,
+        [longer, one, one],
+        8 << 30,
+        meta, qt, *k,
+    )
     parts, lse = call(
         key_value_kernel,
         [((TOTAL, 2 * HD), bf16), row],
         1,
-        [
-            longer, longer,
-            ((TOTAL + TILE, 2 * HD), f32),
-            ((most, TILE, ROWS), f32),
-            ((most, 8, ROWS), f32),
-            one, one,
-        ],
+        [longer, ((TOTAL + TILE, 2 * HD), f32)],
         16 << 30,
-        meta, qs, gs, qt, gt, delta, *k, *v,
+        meta, qs, gs, gt, delta, top, weights0, weights1, peaks, *v,
     )
     parts = parts.reshape(NY * NX, NZ, tq, 2 * HD)
     parts = lax.all_to_all(parts, ("y", "x"), 0, 0)
@@ -269,20 +311,16 @@
         meta, qt, gt, delta, lse, *k, *v,
     )
     parts, query_grad, square = lax.optimization_barrier((parts, query_grad, square))
-    z = lax.axis_index("zh")
-
-    def total(index):
-        part = lax.dynamic_index_in_dim(parts, index, 1, False)
-        return jnp.sum(part.astype(f32), axis=0)
-
-    other = shift(total(1 - z).astype(bf16), "zh", 1)
-    both = (total(z) + other.astype(f32)).astype(bf16)
-    wide = both.astype(f32)
-    local = jnp.sum(wide * wide) + square[0, 0]
+    half = ((tq, HD), bf16)
+    (other,) = call(sum_kernel, [((tq, 2 * HD), bf16)], 0, [], 1 << 20, parts)
     every = ("y", "x", "zh", "tp")
-    world = lax.axis_size(every)
-    grad_square = jnp.sum(lax.all_to_all(jnp.broadcast_to(local, (world, 1)), every, 0, 0))
-    return (query_grad, both[:, :HD], both[:, HD:], grad_square)
+    key_grad, value_grad, local = call(
+        finish_kernel,
+        [half, half, ((lax.axis_size(every), 1, HD), f32)],
+        0, [], 1 << 20, parts, shift(other, "zh", 1), square,
+    )
+    grad_square = jnp.sum(lax.all_to_all(local, every, 0, 0)[:, 0, 0])
+    return (query_grad, key_grad, value_grad, grad_square)
 
 
 def solution(mesh):

time: 128 us -> 122 us (0.953)
  blocking collectives: 0 us -> 26 us
  starting transfers between devices: 54.7 us -> 30.8 us
  waiting for transfers between devices: 42.5 us -> 34 us
  local copies, waits for them, and re-layouts: 4.99 us -> 9.42 us
  other arithmetic: 5.93 us -> 3.27 us
    all_to_all x0 -> x1, blocking collectives: none -> 26 us  [shards(): grad_square = jnp.sum(lax.all_to_all(local, every, 0, 0)[:, 0, 0])]
    all_to_all x1 -> x0, starting transfers between devices: 14.2 us -> none  [shards(): lax.all_to_all(jnp.broadcast_to(local, (world, 1)), every, 0, 0)]
    all_to_all x1 -> x0, waiting for transfers between devices: 12.2 us -> none  [shards(): lax.all_to_all(jnp.broadcast_to(local, (world, 1)), every, 0, 0)]
    ppermute x15, waiting for transfers between devices: 11.4 us -> 18.9 us  [shift(): return lax.ppermute(a, axis, [(i, (i + step) % n) for i in range(n)])]
    unnamed x10 -> x28, local copies, waits for them, and re-layouts: 3.13 us -> 9.42 us
    all_to_all x1, starting transfers between devices: 13.3 us -> 8.05 us  [shards(): parts = lax.all_to_all(parts, ('y', 'x'), 0, 0)]
    ppermute x15, starting transfers between devices: 27.2 us -> 22.7 us  [shift(): return lax.ppermute(a, axis, [(i, (i + step) % n) for i in range(n)])]
    all_to_all x1, waiting for transfers between devices: 18.9 us -> 15.1 us  [shards(): parts = lax.all_to_all(parts, ('y', 'x'), 0, 0)]
  transfers between devices with their start and end apart: 17 -> 16, of which waited for: 9 -> 8; matrix products, arithmetic and copies ran while one was open for 3% -> 2% of each run, Pallas kernels for 5% -> 9%
where the time goes in v3:
time: 122 us
  waiting for transfers between devices  34 us (28%)
  starting transfers between devices  30.8 us (25%)
  blocking collectives  26 us (21%)
  Pallas kernels  17.9 us (15%)
  local copies, waits for them, and re-layouts  9.42 us (8%)
  other arithmetic  3.27 us (3%)
    all_to_all x1, blocking collectives, shards(): grad_square = jnp.sum(lax.all_to_all(local, every, 0, 0)[:, 0, 0])  26 us
    ppermute x15, starting transfers between devices, shift(): return lax.ppermute(a, axis, [(i, (i + step) % n) for i in range(n)])  22.7 us
    ppermute x15, waiting for transfers between devices, shift(): return lax.ppermute(a, axis, [(i, (i + step) % n) for i in range(n)])  18.9 us
    pallas_call x6, Pallas kernels, call(): pl.pallas_call(kernel, out_shape=tuple((jax.ShapeDtypeStruct(s, t) for s,...  17.9 us
    all_to_all x1, waiting for transfers between devices, shards(): parts = lax.all_to_all(parts, ('y', 'x'), 0, 0)  15.1 us
    unnamed x28, local copies, waits for them, and re-layouts  9.42 us
    all_to_all x1, starting transfers between devices, shards(): parts = lax.all_to_all(parts, ('y', 'x'), 0, 0)  8.05 us
  transfers between devices with their start and end apart: 16, of which 8 were waited for; matrix products, arithmetic and copies ran while one was open for 2% of the time, Pallas kernels for 9%

profile of v3, /device:TPU:1, one launch (start us, length us, event | category | flops | bytes accessed | tf_op | source)
XLA Modules:
  0.0 122.2 jit_solution(3162934818079865060)
XLA Ops:
  0.6 7.8 %collective-permute-start.4 = (bf16[128,128]{1,0:T(8,128)(2,1)}, bf16[128,128]{1,0:T(8,128)(2,1)S(1)}, u32[]{:S(2)}, u32[]{:S(2)}) collective-permute-start(bf16[128,128]{1,0:T(8,128)(2,1)} %param.9), channel_id=1, source_target_pairs={{0,8},{8,0},{1,9},{9,1},{2,10},{10,2},{3,11},{11,3},{4,12},{12,4},... | collective-permute-start | bytes 98312 | tf_op jit(solution)/shard_map/ppermute | solution.py:262
  8.6 1.4 %collective-permute-done.4 = bf16[128,128]{1,0:T(8,128)(2,1)S(1)} collective-permute-done((bf16[128,128]{1,0:T(8,128)(2,1)}, bf16[128,128]{1,0:T(8,128)(2,1)S(1)}, u32[]{:S(2)}, u32[]{:S(2)}) %collective-permute-start.4) | collective-permute-done | bytes 32800 | tf_op jit(solution)/shard_map/ppermute | solution.py:262
  10.7 2.7 %collective-permute-start.7 = (bf16[2,128,128]{2,1,0:T(8,128)(2,1)S(1)}, bf16[2,128,128]{2,1,0:T(8,128)(2,1)S(1)}, u32[]{:S(2)}, u32[]{:S(2)}) collective-permute-start(bf16[2,128,128]{2,1,0:T(8,128)(2,1)S(1)} %pad_maximum_fusion.3), channel_id=1, source_target_pairs={{0,192},{64,0},{128,64},{192,128},{1,193},{65,1},{129,65},{193,129... | collective-permute-start | bytes 196616 | tf_op jit(solution)/shard_map/ppermute | solution.py:262
  14.5 1.2 collective-permute-done
  16.5 2.5 %collective-permute-start.3 = (bf16[2,128,128]{2,1,0:T(8,128)(2,1)S(1)}, bf16[2,128,128]{2,1,0:T(8,128)(2,1)S(1)}, u32[]{:S(2)}, u32[]{:S(2)}) collective-permute-start(bf16[2,128,128]{2,1,0:T(8,128)(2,1)S(1)} %pad_maximum_fusion.2), channel_id=1, source_target_pairs={{0,48},{16,0},{32,16},{48,32},{1,49},{17,1},{33,17},{49,33},{2,50}... | collective-permute-start | bytes 196616 | tf_op jit(solution)/shard_map/ppermute | solution.py:262
  20.3 3.3 %collective-permute-done.2 = bf16[2,128,128]{2,1,0:T(8,128)(2,1)S(1)} collective-permute-done((bf16[2,128,128]{2,1,0:T(8,128)(2,1)S(1)}, bf16[2,128,128]{2,1,0:T(8,128)(2,1)S(1)}, u32[]{:S(2)}, u32[]{:S(2)}) %collective-permute-start.2) | collective-permute-done | bytes 65568 | tf_op jit(solution)/shard_map/ppermute | solution.py:262
  24.3 2.8 %collective-permute-start.10 = (bf16[4,2,128,128]{3,2,1,0:T(8,128)(2,1)S(1)}, bf16[4,2,128,128]{3,2,1,0:T(8,128)(2,1)S(1)}, u32[]{:S(2)}, u32[]{:S(2)}) collective-permute-start(bf16[4,2,128,128]{3,2,1,0:T(8,128)(2,1)S(1)} %pad_maximum_fusion), channel_id=1, source_target_pairs={{0,192},{64,0},{128,64},{192,128},{1,193},{65,1},{129,65},{193,129... | collective-permute-start | bytes 786440 | tf_op jit(solution)/shard_map/ppermute | solution.py:262
  28.2 1.0 copy-done.1
  29.2 1.0 copy-done.2
  30.2 1.0 copy-done.3
  34.5 6.5 %collective-permute-done.8 = bf16[4,2,128,128]{3,2,1,0:T(8,128)(2,1)S(1)} collective-permute-done((bf16[4,2,128,128]{3,2,1,0:T(8,128)(2,1)S(1)}, bf16[4,2,128,128]{3,2,1,0:T(8,128)(2,1)S(1)}, u32[]{:S(2)}, u32[]{:S(2)}) %collective-permute-start.8) | collective-permute-done | bytes 262176 | tf_op jit(solution)/shard_map/ppermute | solution.py:262
  40.9 4.6 %shard_map.103 = (f32[5,512,1024]{2,1,0:T(8,128)S(1)}, f32[5,512,1024]{2,1,0:T(8,128)S(1)}, f32[2,5,8,1024]{3,2,1,0:T(8,128)S(1)}, f32[16,1024]{1,0:T(8,128)S(1)}) custom-call(s32[72]{0:T(128)S(1)} %pad_add_fusion.meta_ref, bf16[128,2048]{1,0:T(8,128)(2,1)S(1)} %get-tuple-element.35.qt, bf16[1024,128]{1,0:T(8,128)(2,1)S(1)} %bitcast.22, ...), custom_call_target="tpu_custom_call" | custom-call | flops 8589934592 | bytes 4194304 | tf_op jit(solution)/shard_map/pallas_call | solution.py:249
  45.6 5.4 %shard_map.104 = (bf16[4096,256]{1,0:T(8,128)(2,1)S(1)}, f32[16,1024]{1,0:T(8,128)S(1)}) custom-call(s32[72]{0:T(128)S(1)} %pad_add_fusion.meta_ref, bf16[2048,128]{1,0:T(8,128)(2,1)S(1)} %get-tuple-element.31.qs, bf16[2048,128]{1,0:T(8,128)(2,1)S(1)} %get-tuple-element.32.gs, bf16[128,2048]{1,0:T(8,128)(2,1)S(1)} %get-tuple-element.33.gt, ...), custom_call_target="tpu_custom_call" | custom-call | flops 17179869184 | bytes 4194304 | tf_op jit(solution)/shard_map/pallas_call | solution.py:249
  51.1 1.3 %copy-done = bf16[4096,256]{1,0:T(8,128)(2,1)} copy-done((bf16[4096,256]{1,0:T(8,128)(2,1)}, bf16[4096,256]{1,0:T(8,128)(2,1)S(1)}, u32[]{:S(2)}) %copy-start) | copy-done | bytes 2097176
  52.4 8.0 %all-to-all-start = ((bf16[16,2,128,256]{3,2,1,0:T(8,128)(2,1)}), bf16[16,2,128,256]{3,2,1,0:T(8,128)(2,1)S(1)}, u32[]{:S(2)}, u32[]{:S(2)}) async-start(bf16[16,2,128,256]{3,2,1,0:T(8,128)(2,1)} %bitcast.21), calls=%async_computation | async-start | bytes 4194304 | tf_op jit(solution)/shard_map/all_to_all | solution.py:304
  61.4 0.9 copy-done.7
  62.4 0.9 copy-done.9
  63.3 1.0 copy-done.11
  64.4 1.0 copy-done.13
  65.4 6.3 %shard_map.105 = (bf16[128,2048]{1,0:T(8,128)(2,1)}, f32[8,128]{1,0:T(8,128)S(1)}) custom-call(s32[72]{0:T(128)S(1)} %pad_add_fusion.meta_ref, bf16[128,2048]{1,0:T(8,128)(2,1)S(1)} %copy-done.11, bf16[128,2048]{1,0:T(8,128)(2,1)S(1)} %copy-done.13, f32[16,1024]{1,0:T(8,128)S(1)} %get-tuple-element.34.delta_ref, f32[16,1024]{1,0:T(8,128)S(1)} %get-tuple-element.49.lse_ref, ...), custom_call_target="tpu_custom_call" | custom-call | flops 17179869184 | bytes 4194304 | tf_op jit(solution)/shard_map/pallas_call | solution.py:249
  71.8 15.1 %all-to-all-done.parts_ref = bf16[16,2,128,256]{3,2,1,0:T(8,128)(2,1)S(1)} async-done(((bf16[16,2,128,256]{3,2,1,0:T(8,128)(2,1)}), bf16[16,2,128,256]{3,2,1,0:T(8,128)(2,1)S(1)}, u32[]{:S(2)}, u32[]{:S(2)}) %all-to-all-start) | async-done | bytes 2097184 | tf_op jit(solution)/shard_map/all_to_all | solution.py:304
  87.0 1.8 %collective-permute-start.14 = (bf16[128,256]{1,0:T(8,128)(2,1)S(1)}, bf16[128,256]{1,0:T(8,128)(2,1)S(1)}, u32[]{:S(2)}, u32[]{:S(2)}) collective-permute-start(bf16[128,256]{1,0:T(8,128)(2,1)S(1)} %shard_map.106), channel_id=1, source_target_pairs={{0,8},{8,0},{1,9},{9,1},{2,10},{10,2},{3,11},{11,3},{4,12},{12,4},... | collective-permute-start | bytes 196616 | tf_op jit(solution)/shard_map/ppermute | solution.py:262
  88.8 5.6 %collective-permute-done.14.other_ref = bf16[128,256]{1,0:T(8,128)(2,1)S(1)} collective-permute-done((bf16[128,256]{1,0:T(8,128)(2,1)S(1)}, bf16[128,256]{1,0:T(8,128)(2,1)S(1)}, u32[]{:S(2)}, u32[]{:S(2)}) %collective-permute-start.14) | collective-permute-done | bytes 65568 | tf_op jit(solution)/shard_map/ppermute | solution.py:262
  95.3 26.0 %all_to_all.10 = f32[256,1,128]{2,1,0:T(1,128)S(1)} all-to-all(f32[256,1,128]{2,1,0:T(1,128)S(1)} %get-tuple-element.57), channel_id=1, replica_groups=mesh['y'=4,'x'=4,'zh'=2,'tp'=8] {'y','x','zh','tp'}, dimensions={0} | all-to-all | bytes 262144 | tf_op jit(solution)/shard_map/all_to_all | solution.py:322
  (49 shorter events, 11.7 us)
Async XLA Ops:
  0.6 9.3 %collective-permute-start.4 = (bf16[128,128]{1,0:T(8,128)(2,1)}, bf16[128,128]{1,0:T(8,128)(2,1)S(1)}, u32[]{:S(2)}, u32[]{:S(2)}) collective-permute-start(bf16[128,128]{1,0:T(8,128)(2,1)} %param.9), channel_id=1, source_target_pairs={{0,8},{8,0},{1,9},{9,1},{2,10},{10,2},{3,11},{11,3},{4,12},{12,4},... | collective-permute-start | bytes 98312 | tf_op jit(solution)/shard_map/ppermute | solution.py:262
  8.5 7.2 %collective-permute-start = (bf16[128,128]{1,0:T(8,128)(2,1)}, bf16[128,128]{1,0:T(8,128)(2,1)S(1)}, u32[]{:S(2)}, u32[]{:S(2)}) collective-permute-start(bf16[128,128]{1,0:T(8,128)(2,1)} %param.8), channel_id=1, source_target_pairs={{0,8},{8,0},{1,9},{9,1},{2,10},{10,2},{3,11},{11,3},{4,12},{12,4},... | collective-permute-start | bytes 98312 | tf_op jit(solution)/shard_map/ppermute | solution.py:262
  10.7 8.7 %collective-permute-start.7 = (bf16[2,128,128]{2,1,0:T(8,128)(2,1)S(1)}, bf16[2,128,128]{2,1,0:T(8,128)(2,1)S(1)}, u32[]{:S(2)}, u32[]{:S(2)}) collective-permute-start(bf16[2,128,128]{2,1,0:T(8,128)(2,1)S(1)} %pad_maximum_fusion.3), channel_id=1, source_target_pairs={{0,192},{64,0},{128,64},{192,128},{1,193},{65,1},{129,65},{193,129... | collective-permute-start | bytes 196616 | tf_op jit(solution)/shard_map/ppermute | solution.py:262
  13.5 6.6 %collective-permute-start.6 = (bf16[2,128,128]{2,1,0:T(8,128)(2,1)S(1)}, bf16[2,128,128]{2,1,0:T(8,128)(2,1)S(1)}, u32[]{:S(2)}, u32[]{:S(2)}) collective-permute-start(bf16[2,128,128]{2,1,0:T(8,128)(2,1)S(1)} %pad_maximum_fusion.3), channel_id=1, source_target_pairs={{0,128},{64,192},{128,0},{192,64},{1,129},{65,193},{129,1},{193,65... | collective-permute-start | bytes 196616 | tf_op jit(solution)/shard_map/ppermute | solution.py:262
  13.8 6.3 %collective-permute-start.5 = (bf16[2,128,128]{2,1,0:T(8,128)(2,1)S(1)}, bf16[2,128,128]{2,1,0:T(8,128)(2,1)S(1)}, u32[]{:S(2)}, u32[]{:S(2)}) collective-permute-start(bf16[2,128,128]{2,1,0:T(8,128)(2,1)S(1)} %pad_maximum_fusion.3), channel_id=1, source_target_pairs={{0,64},{64,128},{128,192},{192,0},{1,65},{65,129},{129,193},{193,1... | collective-permute-start | bytes 196616 | tf_op jit(solution)/shard_map/ppermute | solution.py:262
  16.5 3.8 %collective-permute-start.3 = (bf16[2,128,128]{2,1,0:T(8,128)(2,1)S(1)}, bf16[2,128,128]{2,1,0:T(8,128)(2,1)S(1)}, u32[]{:S(2)}, u32[]{:S(2)}) collective-permute-start(bf16[2,128,128]{2,1,0:T(8,128)(2,1)S(1)} %pad_maximum_fusion.2), channel_id=1, source_target_pairs={{0,48},{16,0},{32,16},{48,32},{1,49},{17,1},{33,17},{49,33},{2,50}... | collective-permute-start | bytes 196616 | tf_op jit(solution)/shard_map/ppermute | solution.py:262
  18.9 4.7 %collective-permute-start.2 = (bf16[2,128,128]{2,1,0:T(8,128)(2,1)S(1)}, bf16[2,128,128]{2,1,0:T(8,128)(2,1)S(1)}, u32[]{:S(2)}, u32[]{:S(2)}) collective-permute-start(bf16[2,128,128]{2,1,0:T(8,128)(2,1)S(1)} %pad_maximum_fusion.2), channel_id=1, source_target_pairs={{0,32},{16,48},{32,0},{48,16},{1,33},{17,49},{33,1},{49,17},{2,34}... | collective-permute-start | bytes 196616 | tf_op jit(solution)/shard_map/ppermute | solution.py:262
  19.5 4.8 %collective-permute-start.1 = (bf16[2,128,128]{2,1,0:T(8,128)(2,1)S(1)}, bf16[2,128,128]{2,1,0:T(8,128)(2,1)S(1)}, u32[]{:S(2)}, u32[]{:S(2)}) collective-permute-start(bf16[2,128,128]{2,1,0:T(8,128)(2,1)S(1)} %pad_maximum_fusion.2), channel_id=1, source_target_pairs={{0,16},{16,32},{32,48},{48,0},{1,17},{17,33},{33,49},{49,1},{2,18}... | collective-permute-start | bytes 196616 | tf_op jit(solution)/shard_map/ppermute | solution.py:262
  24.3 9.5 %collective-permute-start.10 = (bf16[4,2,128,128]{3,2,1,0:T(8,128)(2,1)S(1)}, bf16[4,2,128,128]{3,2,1,0:T(8,128)(2,1)S(1)}, u32[]{:S(2)}, u32[]{:S(2)}) collective-permute-start(bf16[4,2,128,128]{3,2,1,0:T(8,128)(2,1)S(1)} %pad_maximum_fusion), channel_id=1, source_target_pairs={{0,192},{64,0},{128,64},{192,128},{1,193},{65,1},{129,65},{193,129... | collective-permute-start | bytes 786440 | tf_op jit(solution)/shard_map/ppermute | solution.py:262
  27.1 7.3 %collective-permute-start.9 = (bf16[4,2,128,128]{3,2,1,0:T(8,128)(2,1)S(1)}, bf16[4,2,128,128]{3,2,1,0:T(8,128)(2,1)S(1)}, u32[]{:S(2)}, u32[]{:S(2)}) collective-permute-start(bf16[4,2,128,128]{3,2,1,0:T(8,128)(2,1)S(1)} %pad_maximum_fusion), channel_id=1, source_target_pairs={{0,128},{64,192},{128,0},{192,64},{1,129},{65,193},{129,1},{193,65... | collective-permute-start | bytes 786440 | tf_op jit(solution)/shard_map/ppermute | solution.py:262
  27.5 13.4 %collective-permute-start.8 = (bf16[4,2,128,128]{3,2,1,0:T(8,128)(2,1)S(1)}, bf16[4,2,128,128]{3,2,1,0:T(8,128)(2,1)S(1)}, u32[]{:S(2)}, u32[]{:S(2)}) collective-permute-start(bf16[4,2,128,128]{3,2,1,0:T(8,128)(2,1)S(1)} %pad_maximum_fusion), channel_id=1, source_target_pairs={{0,64},{64,128},{128,192},{192,0},{1,65},{65,129},{129,193},{193,1... | collective-permute-start | bytes 786440 | tf_op jit(solution)/shard_map/ppermute | solution.py:262
  28.2 1.0 copy-start.1
  29.2 1.0 copy-start.2
  31.8 13.7 %copy-start.10 = (bf16[128,2048]{1,0:T(8,128)(2,1)}, bf16[128,2048]{1,0:T(8,128)(2,1)S(1)}, u32[]{:S(2)}) copy-start(bf16[128,2048]{1,0:T(8,128)(2,1)S(1)} %get-tuple-element.35.qt) | copy-start | bytes 1572868
  31.8 13.8 %copy-start.12 = (bf16[128,2048]{1,0:T(8,128)(2,1)}, bf16[128,2048]{1,0:T(8,128)(2,1)S(1)}, u32[]{:S(2)}) copy-start(bf16[128,2048]{1,0:T(8,128)(2,1)S(1)} %get-tuple-element.33.gt) | copy-start | bytes 1572868
  32.7 12.9 %collective-permute-start.13 = (bf16[4,2,128,128]{3,2,1,0:T(8,128)(2,1)S(1)}, bf16[4,2,128,128]{3,2,1,0:T(8,128)(2,1)S(1)}, u32[]{:S(2)}, u32[]{:S(2)}) collective-permute-start(bf16[4,2,128,128]{3,2,1,0:T(8,128)(2,1)S(1)} %pad_maximum_fusion.1), channel_id=1, source_target_pairs={{0,48},{16,0},{32,16},{48,32},{1,49},{17,1},{33,17},{49,33},{2,50}... | collective-permute-start | bytes 786440 | tf_op jit(solution)/shard_map/ppermute | solution.py:262
  33.0 12.6 %collective-permute-start.12 = (bf16[4,2,128,128]{3,2,1,0:T(8,128)(2,1)S(1)}, bf16[4,2,128,128]{3,2,1,0:T(8,128)(2,1)S(1)}, u32[]{:S(2)}, u32[]{:S(2)}) collective-permute-start(bf16[4,2,128,128]{3,2,1,0:T(8,128)(2,1)S(1)} %pad_maximum_fusion.1), channel_id=1, source_target_pairs={{0,32},{16,48},{32,0},{48,16},{1,33},{17,49},{33,1},{49,17},{2,34}... | collective-permute-start | bytes 786440 | tf_op jit(solution)/shard_map/ppermute | solution.py:262
  33.8 11.8 %collective-permute-start.11 = (bf16[4,2,128,128]{3,2,1,0:T(8,128)(2,1)S(1)}, bf16[4,2,128,128]{3,2,1,0:T(8,128)(2,1)S(1)}, u32[]{:S(2)}, u32[]{:S(2)}) collective-permute-start(bf16[4,2,128,128]{3,2,1,0:T(8,128)(2,1)S(1)} %pad_maximum_fusion.1), channel_id=1, source_target_pairs={{0,16},{16,32},{32,48},{48,0},{1,17},{17,33},{33,49},{49,1},{2,18}... | collective-permute-start | bytes 786440 | tf_op jit(solution)/shard_map/ppermute | solution.py:262
  45.6 5.5 %copy-start.4 = (bf16[4,2,128,128]{3,2,1,0:T(8,128)(2,1)}, bf16[4,2,128,128]{3,2,1,0:T(8,128)(2,1)S(1)}, u32[]{:S(2)}) copy-start(bf16[4,2,128,128]{3,2,1,0:T(8,128)(2,1)S(1)} %collective-permute-done.13) | copy-start | bytes 786436
  45.6 5.5 %copy-start.6 = (bf16[4,2,128,128]{3,2,1,0:T(8,128)(2,1)}, bf16[4,2,128,128]{3,2,1,0:T(8,128)(2,1)S(1)}, u32[]{:S(2)}) copy-start(bf16[4,2,128,128]{3,2,1,0:T(8,128)(2,1)S(1)} %collective-permute-done.12) | copy-start | bytes 786436
  45.6 5.4 %copy-start.8 = (bf16[4,2,128,128]{3,2,1,0:T(8,128)(2,1)}, bf16[4,2,128,128]{3,2,1,0:T(8,128)(2,1)S(1)}, u32[]{:S(2)}) copy-start(bf16[4,2,128,128]{3,2,1,0:T(8,128)(2,1)S(1)} %collective-permute-done.11) | copy-start | bytes 786436
  51.1 1.4 %copy-start = (bf16[4096,256]{1,0:T(8,128)(2,1)}, bf16[4096,256]{1,0:T(8,128)(2,1)S(1)}, u32[]{:S(2)}) copy-start(bf16[4096,256]{1,0:T(8,128)(2,1)S(1)} %get-tuple-element.48) | copy-start | bytes 6291460
  52.4 34.5 %all-to-all-start = ((bf16[16,2,128,256]{3,2,1,0:T(8,128)(2,1)}), bf16[16,2,128,256]{3,2,1,0:T(8,128)(2,1)S(1)}, u32[]{:S(2)}, u32[]{:S(2)}) async-start(bf16[16,2,128,256]{3,2,1,0:T(8,128)(2,1)} %bitcast.21), calls=%async_computation | async-start | bytes 4194304 | tf_op jit(solution)/shard_map/all_to_all | solution.py:304
  87.0 7.4 %collective-permute-start.14 = (bf16[128,256]{1,0:T(8,128)(2,1)S(1)}, bf16[128,256]{1,0:T(8,128)(2,1)S(1)}, u32[]{:S(2)}, u32[]{:S(2)}) collective-permute-start(bf16[128,256]{1,0:T(8,128)(2,1)S(1)} %shard_map.106), channel_id=1, source_target_pairs={{0,8},{8,0},{1,9},{9,1},{2,10},{10,2},{3,11},{11,3},{4,12},{12,4},... | collective-permute-start | bytes 196616 | tf_op jit(solution)/shard_map/ppermute | solution.py:262
  (6 other events, 6.0 us)

commit v4 on v3

--- a/solution.py
+++ b/solution.py
@@ -17,7 +17,7 @@
 SCALE = HD ** (-0.5)
 LOG2E = 1.4426950408889634
 NEG = -1e30
-VMEM = 16 * 1024 * 1024
+PARTS = 8
 
 f32, bf16, i32 = jnp.float32, jnp.bfloat16, jnp.int32
 
@@ -102,7 +102,15 @@
     seq[pl.ds(TOTAL, TILE), :] = jnp.zeros((TILE, HD), bf16)
 
 
-def prepare_kernel(q_ref, o_ref, g_ref, qs, gs, qt, gt, delta):
+def prepare_kernel(q_hbm, o_hbm, g_hbm, qs, gs, qt, gt, delta, q_ref, o_ref, g_ref, sems):
+    copies = [
+        pltpu.make_async_copy(s, d, sems.at[i])
+        for i, (s, d) in enumerate(((q_hbm, q_ref), (o_hbm, o_ref), (g_hbm, g_ref)))
+    ]
+    for c in copies:
+        c.start()
+    for c in copies:
+        c.wait()
     for a in range(2):
         prods = []
         for h in range(GROUP):
@@ -156,7 +164,7 @@
 
 def key_value_kernel(
     meta_ref, qs, gs, gt, delta_ref, top_ref, weights0, weights1, peaks_ref, v0, v1, v2, v3,
-    dkv_ref, lse_ref, vseq, acc,
+    dkv_hbm, lse_ref, vseq, acc, out, sems,
 ):
     sorted_blocks(meta_ref, (v0, v1, v2, v3), vseq, False)
     acc[...] = jnp.zeros_like(acc)
@@ -186,11 +194,18 @@
         tiles(step, masked=False)
 
     each_query_span(meta_ref, span)
-    for slot in range(SPANS):
-        at = slot_place(meta_ref, slot)
-        row = pl.ds(slot * SPAN, SPAN)
-        dkv_ref[row, :HD] = (acc[pl.ds(at, SPAN), :HD] * SCALE).astype(bf16)
-        dkv_ref[row, HD:] = acc[pl.ds(at, SPAN), HD:].astype(bf16)
+    copies = []
+    for part in range(PARTS):
+        for slot in range(part * SPANS // PARTS, (part + 1) * SPANS // PARTS):
+            at = slot_place(meta_ref, slot)
+            row = pl.ds(slot * SPAN, SPAN)
+            out[row, :HD] = (acc[pl.ds(at, SPAN), :HD] * SCALE).astype(bf16)
+            out[row, HD:] = acc[pl.ds(at, SPAN), HD:].astype(bf16)
+        rows = pl.ds(part * TOTAL // PARTS, TOTAL // PARTS)
+        copies.append(pltpu.make_async_copy(out.at[rows], dkv_hbm.at[rows], sems.at[part]))
+        copies[-1].start()
+    for c in copies:
+        c.wait()
 
 
 def query_kernel(
@@ -243,16 +258,29 @@
     local_ref[...] = jnp.broadcast_to((local + sq_ref[:1, :1])[None], local_ref.shape)
 
 
-def call(kernel, outs, smem, scratch, flops, *args):
-    vm = pl.BlockSpec(memory_space=pltpu.VMEM)
-    sm = pl.BlockSpec(memory_space=pltpu.SMEM)
+def call(kernel, outs, specs, scratch, flops, limit, *args):
+    kind = {
+        "S": pl.BlockSpec(memory_space=pltpu.SMEM),
+        "H": pl.BlockSpec(memory_space=pl.ANY),
+        "V": pl.BlockSpec(memory_space=pltpu.VMEM),
+    }
+    given, made = specs.split()
+    args = [
+        pltpu.with_memory_space_constraint(a, pltpu.HBM) if c == "H" else a
+        for a, c in zip(args, given, strict=True)
+    ]
     return pl.pallas_call(
         kernel,
-        out_shape=tuple(jax.ShapeDtypeStruct(s, t) for s, t in outs),
-        in_specs=[sm] * smem + [vm] * (len(args) - smem),
-        out_specs=(vm,) * len(outs),
-        scratch_shapes=[pltpu.VMEM(s, t) for s, t in scratch],
-        compiler_params=pltpu.CompilerParams(vmem_limit_bytes=VMEM),
+        out_shape=tuple(
+            pltpu.HBM(s, t) if c == "H" else jax.ShapeDtypeStruct(s, t)
+            for (s, t), c in zip(outs, made, strict=True)
+        ),
+        in_specs=[kind[c] for c in given],
+        out_specs=tuple(kind[c] for c in made),
+        scratch_shapes=[
+            pltpu.SemaphoreType.DMA(s) if t is None else pltpu.VMEM(s, t) for s, t in scratch
+        ],
+        compiler_params=pltpu.CompilerParams(vmem_limit_bytes=limit << 20),
         cost_estimate=pl.CostEstimate(flops=flops, bytes_accessed=4 << 20, transcendentals=0),
     )(*args)
 
@@ -264,60 +292,63 @@
 
 def shards(queries, keys, values, outputs, out_grad, doc_lengths, span_perm):
     tq = queries.shape[0]
-    k = jnp.stack([keys, shift(keys, "zh", 1)])
-    v = jnp.stack([values, shift(values, "zh", 1)])
+    meta = jnp.concatenate([span_perm, doc_lengths])
+    kv = jnp.stack([keys, values])
+    kv = jnp.stack([kv, shift(kv, "zh", 1)], axis=1)
+    k, v = kv[0], kv[1]
     k = [k] + [shift(k, "x", s) for s in range(1, NX)]
     v = [v] + [shift(v, "y", s) for s in range(1, NY)]
-    k, v = lax.optimization_barrier((k, v))
+    mine = (queries.shape, bf16)
+    heads, turned = ((2 * ROWS, HD), bf16), ((HD, 2 * ROWS), bf16)
+    row, one, longer = ((16, ROWS), f32), ((1, ROWS), f32), ((TOTAL + TILE, HD), bf16)
+    most = -(-(TOTAL // 2 + SPAN) // TILE)
+    ready = call(
+        prepare_kernel,
+        [heads, heads, turned, turned, row],
+        "HHH VVVVV",
+        [mine, mine, mine, ((3,), None)],
+        1 << 30, 16, queries, outputs, out_grad,
+    )
+    k, v, meta = lax.optimization_barrier((k, v, meta))
+    qs, gs, qt, gt, delta = ready
     k, v = jnp.stack(k), jnp.stack(v)
     k = [k] + [shift(k, "y", s) for s in range(1, NY)]
     v = [v] + [shift(v, "x", s) for s in range(1, NX)]
     k = [a.reshape(TOTAL // NY, HD) for a in k]
     v = [a.reshape(TOTAL // NX, HD) for a in v]
 
-    meta = jnp.concatenate([span_perm, doc_lengths])
-    heads, turned = ((2 * ROWS, HD), bf16), ((HD, 2 * ROWS), bf16)
-    row, one, longer = ((16, ROWS), f32), ((1, ROWS), f32), ((TOTAL + TILE, HD), bf16)
-    most = -(-(TOTAL // 2 + SPAN) // TILE)
-    qs, gs, qt, gt, delta = call(
-        prepare_kernel,
-        [heads, heads, turned, turned, row],
-        0, [], 1 << 30, queries, outputs, out_grad,
-    )
     weights0, weights1, peaks, top = call(
         score_kernel,
         [((most, TILE, ROWS), f32), ((most, TILE, ROWS), f32), ((2, most, 8, ROWS), f32), row],
-        1,
+        "SVVVVV VVVV",
         [longer, one, one],
-        8 << 30,
-        meta, qt, *k,
+        8 << 30, 16, meta, qt, *k,
     )
     parts, lse = call(
         key_value_kernel,
         [((TOTAL, 2 * HD), bf16), row],
-        1,
-        [longer, ((TOTAL + TILE, 2 * HD), f32)],
-        16 << 30,
-        meta, qs, gs, gt, delta, top, weights0, weights1, peaks, *v,
+        "SVVVVVVVVVVVV HV",
+        [longer, ((TOTAL + TILE, 2 * HD), f32), ((TOTAL, 2 * HD), bf16), ((PARTS,), None)],
+        16 << 30, 16, meta, qs, gs, gt, delta, top, weights0, weights1, peaks, *v,
     )
     parts = parts.reshape(NY * NX, NZ, tq, 2 * HD)
     parts = lax.all_to_all(parts, ("y", "x"), 0, 0)
     query_grad, square = call(
         query_kernel,
-        [(queries.shape, bf16), ((8, HD), f32)],
-        1,
+        [mine, ((8, HD), f32)],
+        "SVVVVVVVVVVVV VV",
         [longer, longer, ((HD, ROWS), f32)],
-        16 << 30,
-        meta, qt, gt, delta, lse, *k, *v,
+        16 << 30, 32, meta, qt, gt, delta, lse, *k, *v,
     )
     parts, query_grad, square = lax.optimization_barrier((parts, query_grad, square))
     half = ((tq, HD), bf16)
-    (other,) = call(sum_kernel, [((tq, 2 * HD), bf16)], 0, [], 1 << 20, parts)
+    (other,) = call(sum_kernel, [((tq, 2 * HD), bf16)], "V V", [], 1 << 20, 16, parts)
     every = ("y", "x", "zh", "tp")
     key_grad, value_grad, local = call(
         finish_kernel,
         [half, half, ((lax.axis_size(every), 1, HD), f32)],
-        0, [], 1 << 20, parts, shift(other, "zh", 1), square,
+        "VVV VVV",
+        [], 1 << 20, 16, parts, shift(other, "zh", 1), square,
     )
     grad_square = jnp.sum(lax.all_to_all(local, every, 0, 0)[:, 0, 0])
     return (query_grad, key_grad, value_grad, grad_square)

time: 122 us -> 120 us (0.984)
  waiting for transfers between devices: 34 us -> 27.3 us
  blocking collectives: 26 us -> 31.6 us
  Pallas kernels: 17.9 us -> 23.1 us
  local copies, waits for them, and re-layouts: 9.42 us -> 4.95 us
  starting transfers between devices: 30.8 us -> 29.5 us
    all_to_all x1, blocking collectives: 26 us -> 31.6 us  [shards(): grad_square = jnp.sum(lax.all_to_all(local, every, 0, 0)[:, 0, 0])]
    pallas_call x6, Pallas kernels: 17.9 us -> 23.1 us  [call(): pl.pallas_call(kernel, out_shape=tuple((pltpu.HBM(s, t) if c == 'H' else...]
    unnamed x28 -> x20, local copies, waits for them, and re-layouts: 9.42 us -> 4.95 us
    all_to_all x1, starting transfers between devices: 8.05 us -> 3.73 us  [shards(): parts = lax.all_to_all(parts, ('y', 'x'), 0, 0)]
    ppermute x15 -> x14, waiting for transfers between devices: 18.9 us -> 14.7 us  [shift(): return lax.ppermute(a, axis, [(i, (i + step) % n) for i in range(n)])]
    ppermute x15 -> x14, starting transfers between devices: 22.7 us -> 25.8 us  [shift(): return lax.ppermute(a, axis, [(i, (i + step) % n) for i in range(n)])]
    all_to_all x1, waiting for transfers between devices: 15.1 us -> 12.6 us  [shards(): parts = lax.all_to_all(parts, ('y', 'x'), 0, 0)]
  transfers between devices with their start and end apart: 16 -> 15, of which waited for: 8 -> 8; matrix products, arithmetic and copies ran while one was open for 2% -> 1% of each run, Pallas kernels for 9% -> 12%
where the time goes in v4:
time: 120 us
  blocking collectives  31.6 us (26%)
  starting transfers between devices  29.5 us (25%)
  waiting for transfers between devices  27.3 us (23%)
  Pallas kernels  23.1 us (19%)
  local copies, waits for them, and re-layouts  4.95 us (4%)
  other arithmetic  2.48 us (2%)
    all_to_all x1, blocking collectives, shards(): grad_square = jnp.sum(lax.all_to_all(local, every, 0, 0)[:, 0, 0])  31.6 us
    ppermute x14, starting transfers between devices, shift(): return lax.ppermute(a, axis, [(i, (i + step) % n) for i in range(n)])  25.8 us
    pallas_call x6, Pallas kernels, call(): pl.pallas_call(kernel, out_shape=tuple((pltpu.HBM(s, t) if c == 'H' else...  23.1 us
    ppermute x14, waiting for transfers between devices, shift(): return lax.ppermute(a, axis, [(i, (i + step) % n) for i in range(n)])  14.7 us
    all_to_all x1, waiting for transfers between devices, shards(): parts = lax.all_to_all(parts, ('y', 'x'), 0, 0)  12.6 us
    unnamed x20, local copies, waits for them, and re-layouts  4.95 us
    all_to_all x1, starting transfers between devices, shards(): parts = lax.all_to_all(parts, ('y', 'x'), 0, 0)  3.73 us
  transfers between devices with their start and end apart: 15, of which 8 were waited for; matrix products, arithmetic and copies ran while one was open for 1% of the time, Pallas kernels for 12%

profile of v4, /device:TPU:1, one launch (start us, length us, event | category | flops | bytes accessed | tf_op | source)
XLA Modules:
  0.0 119.8 jit_solution(7233902570352888575)
XLA Ops:
  1.4 7.8 %collective-permute-start = (bf16[2,128,128]{2,1,0:T(8,128)(2,1)S(1)}, bf16[2,128,128]{2,1,0:T(8,128)(2,1)S(1)}, u32[]{:S(2)}, u32[]{:S(2)}) collective-permute-start(bf16[2,128,128]{2,1,0:T(8,128)(2,1)S(1)} %get-tuple-element.62), channel_id=1, source_target_pairs={{0,8},{8,0},{1,9},{9,1},{2,10},{10,2},{3,11},{11,3},{4,12},{12,4},... | collective-permute-start | bytes 196616 | tf_op jit(solution)/shard_map/ppermute | solution.py:290
  9.2 1.8 %collective-permute-done = bf16[2,128,128]{2,1,0:T(8,128)(2,1)S(1)} collective-permute-done((bf16[2,128,128]{2,1,0:T(8,128)(2,1)S(1)}, bf16[2,128,128]{2,1,0:T(8,128)(2,1)S(1)}, u32[]{:S(2)}, u32[]{:S(2)}) %collective-permute-start) | collective-permute-done | bytes 65568 | tf_op jit(solution)/shard_map/ppermute | solution.py:290
  11.0 2.8 %collective-permute-start.6 = (bf16[2,128,128]{2,1,0:T(8,128)(2,1)S(1)}, bf16[2,128,128]{2,1,0:T(8,128)(2,1)S(1)}, u32[]{:S(2)}, u32[]{:S(2)}) collective-permute-start(bf16[2,128,128]{2,1,0:T(8,128)(2,1)S(1)} %get-tuple-element.46), channel_id=1, source_target_pairs={{0,192},{64,0},{128,64},{192,128},{1,193},{65,1},{129,65},{193,129... | collective-permute-start | bytes 196616 | tf_op jit(solution)/shard_map/ppermute | solution.py:290
  14.9 2.5 %collective-permute-start.3 = (bf16[2,128,128]{2,1,0:T(8,128)(2,1)S(1)}, bf16[2,128,128]{2,1,0:T(8,128)(2,1)S(1)}, u32[]{:S(2)}, u32[]{:S(2)}) collective-permute-start(bf16[2,128,128]{2,1,0:T(8,128)(2,1)S(1)} %get-tuple-element.38), channel_id=1, source_target_pairs={{0,48},{16,0},{32,16},{48,32},{1,49},{17,1},{33,17},{49,33},{2,50}... | collective-permute-start | bytes 196616 | tf_op jit(solution)/shard_map/ppermute | solution.py:290
  19.2 2.8 %collective-permute-done.2 = bf16[2,128,128]{2,1,0:T(8,128)(2,1)S(1)} collective-permute-done((bf16[2,128,128]{2,1,0:T(8,128)(2,1)S(1)}, bf16[2,128,128]{2,1,0:T(8,128)(2,1)S(1)}, u32[]{:S(2)}, u32[]{:S(2)}) %collective-permute-start.2) | collective-permute-done | bytes 65568 | tf_op jit(solution)/shard_map/ppermute | solution.py:290
  22.7 2.1 %collective-permute-start.9 = (bf16[4,2,128,128]{3,2,1,0:T(8,128)(2,1)S(1)}, bf16[4,2,128,128]{3,2,1,0:T(8,128)(2,1)S(1)}, u32[]{:S(2)}, u32[]{:S(2)}) collective-permute-start(bf16[4,2,128,128]{3,2,1,0:T(8,128)(2,1)S(1)} %pad_maximum_fusion), channel_id=1, source_target_pairs={{0,192},{64,0},{128,64},{192,128},{1,193},{65,1},{129,65},{193,129... | collective-permute-start | bytes 786440 | tf_op jit(solution)/shard_map/ppermute | solution.py:290
  24.8 1.4 %collective-permute-start.8 = (bf16[4,2,128,128]{3,2,1,0:T(8,128)(2,1)S(1)}, bf16[4,2,128,128]{3,2,1,0:T(8,128)(2,1)S(1)}, u32[]{:S(2)}, u32[]{:S(2)}) collective-permute-start(bf16[4,2,128,128]{3,2,1,0:T(8,128)(2,1)S(1)} %pad_maximum_fusion), channel_id=1, source_target_pairs={{0,128},{64,192},{128,0},{192,64},{1,129},{65,193},{129,1},{193,65... | collective-permute-start | bytes 786440 | tf_op jit(solution)/shard_map/ppermute | solution.py:290
  26.2 2.0 %shard_map.102 = (bf16[2048,128]{1,0:T(8,128)(2,1)S(1)}, bf16[2048,128]{1,0:T(8,128)(2,1)S(1)}, bf16[128,2048]{1,0:T(8,128)(2,1)S(1)}, bf16[128,2048]{1,0:T(8,128)(2,1)S(1)}, f32[16,1024]{1,0:T(8,128)S(1)}) custom-call(bf16[128,2048]{1,0:T(8,128)(2,1)} %q_hbm.1, bf16[128,2048]{1,0:T(8,128)(2,1)} %o_hbm.1, bf16[128,2048]{1,0:T(8,128)(2,1)} %g_hbm.1), custom_call_target="tpu_custom_call" | custom-call | flops 1073741824 | bytes 4194304 | tf_op jit(solution)/shard_map/pallas_call | solution.py:272
  28.6 0.9 collective-permute-start.11
  30.2 1.4 %collective-permute-done.8 = bf16[4,2,128,128]{3,2,1,0:T(8,128)(2,1)S(1)} collective-permute-done((bf16[4,2,128,128]{3,2,1,0:T(8,128)(2,1)S(1)}, bf16[4,2,128,128]{3,2,1,0:T(8,128)(2,1)S(1)}, u32[]{:S(2)}, u32[]{:S(2)}) %collective-permute-start.8) | collective-permute-done | bytes 262176 | tf_op jit(solution)/shard_map/ppermute | solution.py:290
  31.6 6.0 %collective-permute-done.7 = bf16[4,2,128,128]{3,2,1,0:T(8,128)(2,1)S(1)} collective-permute-done((bf16[4,2,128,128]{3,2,1,0:T(8,128)(2,1)S(1)}, bf16[4,2,128,128]{3,2,1,0:T(8,128)(2,1)S(1)}, u32[]{:S(2)}, u32[]{:S(2)}) %collective-permute-start.7) | collective-permute-done | bytes 262176 | tf_op jit(solution)/shard_map/ppermute | solution.py:290
  37.6 5.5 %shard_map.103 = (f32[5,512,1024]{2,1,0:T(8,128)S(1)}, f32[5,512,1024]{2,1,0:T(8,128)S(1)}, f32[2,5,8,1024]{3,2,1,0:T(8,128)S(1)}, f32[16,1024]{1,0:T(8,128)S(1)}) custom-call(s32[72]{0:T(128)S(1)} %pad_add_fusion.meta_ref, bf16[128,2048]{1,0:T(8,128)(2,1)S(1)} %get-tuple-element.37.qt, bf16[1024,128]{1,0:T(8,128)(2,1)S(1)} %bitcast.26, ...), custom_call_target="tpu_custom_call" | custom-call | flops 8589934592 | bytes 4194304 | tf_op jit(solution)/shard_map/pallas_call | solution.py:272
  43.1 7.5 %shard_map.104 = (bf16[4096,256]{1,0:T(8,128)(2,1)}, f32[16,1024]{1,0:T(8,128)S(1)}) custom-call(s32[72]{0:T(128)S(1)} %pad_add_fusion.meta_ref, bf16[2048,128]{1,0:T(8,128)(2,1)S(1)} %get-tuple-element.33.qs, bf16[2048,128]{1,0:T(8,128)(2,1)S(1)} %get-tuple-element.34.gs, bf16[128,2048]{1,0:T(8,128)(2,1)S(1)} %get-tuple-element.35.gt, ...), custom_call_target="tpu_custom_call" | custom-call | flops 17179869184 | bytes 4194304 | tf_op jit(solution)/shard_map/pallas_call | solution.py:272
  50.6 3.7 %all-to-all-start = ((bf16[16,2,128,256]{3,2,1,0:T(8,128)(2,1)}), bf16[16,2,128,256]{3,2,1,0:T(8,128)(2,1)S(1)}, u32[]{:S(2)}, u32[]{:S(2)}) async-start(bf16[16,2,128,256]{3,2,1,0:T(8,128)(2,1)} %bitcast.42), calls=%async_computation | async-start | bytes 4194304 | tf_op jit(solution)/shard_map/all_to_all | solution.py:335
  54.4 0.9 copy-done.1
  55.3 0.9 copy-done.3
  56.3 0.9 copy-done.5
  57.2 1.0 copy-done.7
  58.3 1.0 copy-done.9
  59.3 7.3 %shard_map.105 = (bf16[128,2048]{1,0:T(8,128)(2,1)}, f32[8,128]{1,0:T(8,128)S(1)}) custom-call(s32[72]{0:T(128)S(1)} %pad_add_fusion.meta_ref, bf16[128,2048]{1,0:T(8,128)(2,1)S(1)} %copy-done.7, bf16[128,2048]{1,0:T(8,128)(2,1)S(1)} %copy-done.9, f32[16,1024]{1,0:T(8,128)S(1)} %get-tuple-element.36.delta_ref, f32[16,1024]{1,0:T(8,128)S(1)} %get-tuple-element.51.lse_ref, ...), custom_call_target="tpu_custom_call" | custom-call | flops 17179869184 | bytes 4194304 | tf_op jit(solution)/shard_map/pallas_call | solution.py:272
  66.6 12.6 %all-to-all-done.parts_ref = bf16[16,2,128,256]{3,2,1,0:T(8,128)(2,1)S(1)} async-done(((bf16[16,2,128,256]{3,2,1,0:T(8,128)(2,1)}), bf16[16,2,128,256]{3,2,1,0:T(8,128)(2,1)S(1)}, u32[]{:S(2)}, u32[]{:S(2)}) %all-to-all-start) | async-done | bytes 2097184 | tf_op jit(solution)/shard_map/all_to_all | solution.py:335
  79.3 5.5 %collective-permute-start.13 = (bf16[128,256]{1,0:T(8,128)(2,1)S(1)}, bf16[128,256]{1,0:T(8,128)(2,1)S(1)}, u32[]{:S(2)}, u32[]{:S(2)}) collective-permute-start(bf16[128,256]{1,0:T(8,128)(2,1)S(1)} %shard_map.106), channel_id=1, source_target_pairs={{0,8},{8,0},{1,9},{9,1},{2,10},{10,2},{3,11},{11,3},{4,12},{12,4},... | collective-permute-start | bytes 196616 | tf_op jit(solution)/shard_map/ppermute | solution.py:290
  84.9 1.7 %collective-permute-done.13.other_ref = bf16[128,256]{1,0:T(8,128)(2,1)S(1)} collective-permute-done((bf16[128,256]{1,0:T(8,128)(2,1)S(1)}, bf16[128,256]{1,0:T(8,128)(2,1)S(1)}, u32[]{:S(2)}, u32[]{:S(2)}) %collective-permute-start.13) | collective-permute-done | bytes 65568 | tf_op jit(solution)/shard_map/ppermute | solution.py:290
  87.4 31.6 %all_to_all.10 = f32[256,1,128]{2,1,0:T(1,128)S(1)} all-to-all(f32[256,1,128]{2,1,0:T(1,128)S(1)} %get-tuple-element.59), channel_id=1, replica_groups=mesh['y'=4,'x'=4,'zh'=2,'tp'=8] {'y','x','zh','tp'}, dimensions={0} | all-to-all | bytes 262144 | tf_op jit(solution)/shard_map/all_to_all | solution.py:353
  (39 shorter events, 7.5 us)
Async XLA Ops:
  1.4 9.6 %collective-permute-start = (bf16[2,128,128]{2,1,0:T(8,128)(2,1)S(1)}, bf16[2,128,128]{2,1,0:T(8,128)(2,1)S(1)}, u32[]{:S(2)}, u32[]{:S(2)}) collective-permute-start(bf16[2,128,128]{2,1,0:T(8,128)(2,1)S(1)} %get-tuple-element.62), channel_id=1, source_target_pairs={{0,8},{8,0},{1,9},{9,1},{2,10},{10,2},{3,11},{11,3},{4,12},{12,4},... | collective-permute-start | bytes 196616 | tf_op jit(solution)/shard_map/ppermute | solution.py:290
  11.0 6.9 %collective-permute-start.6 = (bf16[2,128,128]{2,1,0:T(8,128)(2,1)S(1)}, bf16[2,128,128]{2,1,0:T(8,128)(2,1)S(1)}, u32[]{:S(2)}, u32[]{:S(2)}) collective-permute-start(bf16[2,128,128]{2,1,0:T(8,128)(2,1)S(1)} %get-tuple-element.46), channel_id=1, source_target_pairs={{0,192},{64,0},{128,64},{192,128},{1,193},{65,1},{129,65},{193,129... | collective-permute-start | bytes 196616 | tf_op jit(solution)/shard_map/ppermute | solution.py:290
  13.8 5.4 %collective-permute-start.5 = (bf16[2,128,128]{2,1,0:T(8,128)(2,1)S(1)}, bf16[2,128,128]{2,1,0:T(8,128)(2,1)S(1)}, u32[]{:S(2)}, u32[]{:S(2)}) collective-permute-start(bf16[2,128,128]{2,1,0:T(8,128)(2,1)S(1)} %get-tuple-element.46), channel_id=1, source_target_pairs={{0,128},{64,192},{128,0},{192,64},{1,129},{65,193},{129,1},{193,65... | collective-permute-start | bytes 196616 | tf_op jit(solution)/shard_map/ppermute | solution.py:290
  14.2 5.1 %collective-permute-start.4 = (bf16[2,128,128]{2,1,0:T(8,128)(2,1)S(1)}, bf16[2,128,128]{2,1,0:T(8,128)(2,1)S(1)}, u32[]{:S(2)}, u32[]{:S(2)}) collective-permute-start(bf16[2,128,128]{2,1,0:T(8,128)(2,1)S(1)} %get-tuple-element.46), channel_id=1, source_target_pairs={{0,64},{64,128},{128,192},{192,0},{1,65},{65,129},{129,193},{193,1... | collective-permute-start | bytes 196616 | tf_op jit(solution)/shard_map/ppermute | solution.py:290
  14.9 4.4 %collective-permute-start.3 = (bf16[2,128,128]{2,1,0:T(8,128)(2,1)S(1)}, bf16[2,128,128]{2,1,0:T(8,128)(2,1)S(1)}, u32[]{:S(2)}, u32[]{:S(2)}) collective-permute-start(bf16[2,128,128]{2,1,0:T(8,128)(2,1)S(1)} %get-tuple-element.38), channel_id=1, source_target_pairs={{0,48},{16,0},{32,16},{48,32},{1,49},{17,1},{33,17},{49,33},{2,50}... | collective-permute-start | bytes 196616 | tf_op jit(solution)/shard_map/ppermute | solution.py:290
  17.3 4.7 %collective-permute-start.2 = (bf16[2,128,128]{2,1,0:T(8,128)(2,1)S(1)}, bf16[2,128,128]{2,1,0:T(8,128)(2,1)S(1)}, u32[]{:S(2)}, u32[]{:S(2)}) collective-permute-start(bf16[2,128,128]{2,1,0:T(8,128)(2,1)S(1)} %get-tuple-element.38), channel_id=1, source_target_pairs={{0,32},{16,48},{32,0},{48,16},{1,33},{17,49},{33,1},{49,17},{2,34}... | collective-permute-start | bytes 196616 | tf_op jit(solution)/shard_map/ppermute | solution.py:290
  17.9 4.8 %collective-permute-start.1 = (bf16[2,128,128]{2,1,0:T(8,128)(2,1)S(1)}, bf16[2,128,128]{2,1,0:T(8,128)(2,1)S(1)}, u32[]{:S(2)}, u32[]{:S(2)}) collective-permute-start(bf16[2,128,128]{2,1,0:T(8,128)(2,1)S(1)} %get-tuple-element.38), channel_id=1, source_target_pairs={{0,16},{16,32},{32,48},{48,0},{1,17},{17,33},{33,49},{49,1},{2,18}... | collective-permute-start | bytes 196616 | tf_op jit(solution)/shard_map/ppermute | solution.py:290
  22.7 7.3 %collective-permute-start.9 = (bf16[4,2,128,128]{3,2,1,0:T(8,128)(2,1)S(1)}, bf16[4,2,128,128]{3,2,1,0:T(8,128)(2,1)S(1)}, u32[]{:S(2)}, u32[]{:S(2)}) collective-permute-start(bf16[4,2,128,128]{3,2,1,0:T(8,128)(2,1)S(1)} %pad_maximum_fusion), channel_id=1, source_target_pairs={{0,192},{64,0},{128,64},{192,128},{1,193},{65,1},{129,65},{193,129... | collective-permute-start | bytes 786440 | tf_op jit(solution)/shard_map/ppermute | solution.py:290
  24.8 6.8 %collective-permute-start.8 = (bf16[4,2,128,128]{3,2,1,0:T(8,128)(2,1)S(1)}, bf16[4,2,128,128]{3,2,1,0:T(8,128)(2,1)S(1)}, u32[]{:S(2)}, u32[]{:S(2)}) collective-permute-start(bf16[4,2,128,128]{3,2,1,0:T(8,128)(2,1)S(1)} %pad_maximum_fusion), channel_id=1, source_target_pairs={{0,128},{64,192},{128,0},{192,64},{1,129},{65,193},{129,1},{193,65... | collective-permute-start | bytes 786440 | tf_op jit(solution)/shard_map/ppermute | solution.py:290
  26.2 11.4 %collective-permute-start.7 = (bf16[4,2,128,128]{3,2,1,0:T(8,128)(2,1)S(1)}, bf16[4,2,128,128]{3,2,1,0:T(8,128)(2,1)S(1)}, u32[]{:S(2)}, u32[]{:S(2)}) collective-permute-start(bf16[4,2,128,128]{3,2,1,0:T(8,128)(2,1)S(1)} %pad_maximum_fusion), channel_id=1, source_target_pairs={{0,64},{64,128},{128,192},{192,0},{1,65},{65,129},{129,193},{193,1... | collective-permute-start | bytes 786440 | tf_op jit(solution)/shard_map/ppermute | solution.py:290
  28.1 14.9 %copy-start.6 = (bf16[128,2048]{1,0:T(8,128)(2,1)}, bf16[128,2048]{1,0:T(8,128)(2,1)S(1)}, u32[]{:S(2)}) copy-start(bf16[128,2048]{1,0:T(8,128)(2,1)S(1)} %get-tuple-element.37.qt) | copy-start | bytes 1572868
  28.2 15.0 %copy-start.8 = (bf16[128,2048]{1,0:T(8,128)(2,1)}, bf16[128,2048]{1,0:T(8,128)(2,1)S(1)}, u32[]{:S(2)}) copy-start(bf16[128,2048]{1,0:T(8,128)(2,1)S(1)} %get-tuple-element.35.gt) | copy-start | bytes 1572868
  28.2 14.8 %collective-permute-start.12 = (bf16[4,2,128,128]{3,2,1,0:T(8,128)(2,1)S(1)}, bf16[4,2,128,128]{3,2,1,0:T(8,128)(2,1)S(1)}, u32[]{:S(2)}, u32[]{:S(2)}) collective-permute-start(bf16[4,2,128,128]{3,2,1,0:T(8,128)(2,1)S(1)} %pad_maximum_fusion.1), channel_id=1, source_target_pairs={{0,48},{16,0},{32,16},{48,32},{1,49},{17,1},{33,17},{49,33},{2,50}... | collective-permute-start | bytes 786440 | tf_op jit(solution)/shard_map/ppermute | solution.py:290
  28.6 14.5 %collective-permute-start.11 = (bf16[4,2,128,128]{3,2,1,0:T(8,128)(2,1)S(1)}, bf16[4,2,128,128]{3,2,1,0:T(8,128)(2,1)S(1)}, u32[]{:S(2)}, u32[]{:S(2)}) collective-permute-start(bf16[4,2,128,128]{3,2,1,0:T(8,128)(2,1)S(1)} %pad_maximum_fusion.1), channel_id=1, source_target_pairs={{0,32},{16,48},{32,0},{48,16},{1,33},{17,49},{33,1},{49,17},{2,34}... | collective-permute-start | bytes 786440 | tf_op jit(solution)/shard_map/ppermute | solution.py:290
  30.0 13.1 %collective-permute-start.10 = (bf16[4,2,128,128]{3,2,1,0:T(8,128)(2,1)S(1)}, bf16[4,2,128,128]{3,2,1,0:T(8,128)(2,1)S(1)}, u32[]{:S(2)}, u32[]{:S(2)}) collective-permute-start(bf16[4,2,128,128]{3,2,1,0:T(8,128)(2,1)S(1)} %pad_maximum_fusion.1), channel_id=1, source_target_pairs={{0,16},{16,32},{32,48},{48,0},{1,17},{17,33},{33,49},{49,1},{2,18}... | collective-permute-start | bytes 786440 | tf_op jit(solution)/shard_map/ppermute | solution.py:290
  43.1 7.6 %copy-start = (bf16[4,2,128,128]{3,2,1,0:T(8,128)(2,1)}, bf16[4,2,128,128]{3,2,1,0:T(8,128)(2,1)S(1)}, u32[]{:S(2)}) copy-start(bf16[4,2,128,128]{3,2,1,0:T(8,128)(2,1)S(1)} %collective-permute-done.12) | copy-start | bytes 786436
  43.1 7.5 %copy-start.2 = (bf16[4,2,128,128]{3,2,1,0:T(8,128)(2,1)}, bf16[4,2,128,128]{3,2,1,0:T(8,128)(2,1)S(1)}, u32[]{:S(2)}) copy-start(bf16[4,2,128,128]{3,2,1,0:T(8,128)(2,1)S(1)} %collective-permute-done.11) | copy-start | bytes 786436
  43.1 7.5 %copy-start.4 = (bf16[4,2,128,128]{3,2,1,0:T(8,128)(2,1)}, bf16[4,2,128,128]{3,2,1,0:T(8,128)(2,1)S(1)}, u32[]{:S(2)}) copy-start(bf16[4,2,128,128]{3,2,1,0:T(8,128)(2,1)S(1)} %collective-permute-done.10) | copy-start | bytes 786436
  50.6 28.5 %all-to-all-start = ((bf16[16,2,128,256]{3,2,1,0:T(8,128)(2,1)}), bf16[16,2,128,256]{3,2,1,0:T(8,128)(2,1)S(1)}, u32[]{:S(2)}, u32[]{:S(2)}) async-start(bf16[16,2,128,256]{3,2,1,0:T(8,128)(2,1)} %bitcast.42), calls=%async_computation | async-start | bytes 4194304 | tf_op jit(solution)/shard_map/all_to_all | solution.py:335
  54.4 1.0 copy-start.1
  55.3 0.9 copy-start.3
  57.2 1.0 copy-start.7
  58.3 1.0 copy-start.9
  79.3 7.2 %collective-permute-start.13 = (bf16[128,256]{1,0:T(8,128)(2,1)S(1)}, bf16[128,256]{1,0:T(8,128)(2,1)S(1)}, u32[]{:S(2)}, u32[]{:S(2)}) collective-permute-start(bf16[128,256]{1,0:T(8,128)(2,1)S(1)} %shard_map.106), channel_id=1, source_target_pairs={{0,8},{8,0},{1,9},{9,1},{2,10},{10,2},{3,11},{11,3},{4,12},{12,4},... | collective-permute-start | bytes 196616 | tf_op jit(solution)/shard_map/ppermute | solution.py:290
  (1 other events, 0.9 us)

commit v5 on v4

--- a/solution.py
+++ b/solution.py
@@ -12,7 +12,7 @@
 SPANS = 64
 NY, NX, NZ = 4, 4, 2
 ROWS = SPAN * GROUP
-TILE = 512
+TILE = 704
 TOTAL = SPAN * SPANS
 SCALE = HD ** (-0.5)
 LOG2E = 1.4426950408889634
@@ -96,7 +96,7 @@
             for zz in range(NZ * 2):
                 home = ((y + NY - sy) % NY) * NX + (x + NX - sx) % NX
                 at = slot_place(meta_ref, (home * NZ + (z + zz // 2) % NZ) * 2 + zz % 2)
-                last, inner = (sy, sx) if keys else (sx, sy)
+                last, inner = (sx, sy) if keys else (sy, sx)
                 row = pl.ds((inner * 2 * NZ + zz) * SPAN, SPAN)
                 seq[pl.ds(at, SPAN), :] = pieces[last][row, :]
     seq[pl.ds(TOTAL, TILE), :] = jnp.zeros((TILE, HD), bf16)
@@ -296,8 +296,8 @@
     kv = jnp.stack([keys, values])
     kv = jnp.stack([kv, shift(kv, "zh", 1)], axis=1)
     k, v = kv[0], kv[1]
-    k = [k] + [shift(k, "x", s) for s in range(1, NX)]
-    v = [v] + [shift(v, "y", s) for s in range(1, NY)]
+    k = [k] + [shift(k, "y", s) for s in range(1, NY)]
+    v = [v] + [shift(v, "x", s) for s in range(1, NX)]
     mine = (queries.shape, bf16)
     heads, turned = ((2 * ROWS, HD), bf16), ((HD, 2 * ROWS), bf16)
     row, one, longer = ((16, ROWS), f32), ((1, ROWS), f32), ((TOTAL + TILE, HD), bf16)
@@ -312,8 +312,8 @@
     k, v, meta = lax.optimization_barrier((k, v, meta))
     qs, gs, qt, gt, delta = ready
     k, v = jnp.stack(k), jnp.stack(v)
-    k = [k] + [shift(k, "y", s) for s in range(1, NY)]
-    v = [v] + [shift(v, "x", s) for s in range(1, NX)]
+    k = [k] + [shift(k, "x", s) for s in range(1, NX)]
+    v = [v] + [shift(v, "y", s) for s in range(1, NY)]
     k = [a.reshape(TOTAL // NY, HD) for a in k]
     v = [a.reshape(TOTAL // NX, HD) for a in v]
 

time: 120 us -> 119 us (level)
  Pallas kernels: 23.1 us -> 16.8 us
  waiting for transfers between devices: 27.3 us -> 33.2 us
  blocking collectives: 31.6 us -> 29.5 us
  starting transfers between devices: 29.5 us -> 31.4 us
    pallas_call x6, Pallas kernels: 23.1 us -> 16.8 us  [call(): pl.pallas_call(kernel, out_shape=tuple((pltpu.HBM(s, t) if c == 'H' else...]
    all_to_all x1, starting transfers between devices: 3.73 us -> 8.62 us  [shards(): parts = lax.all_to_all(parts, ('y', 'x'), 0, 0)]
    ppermute x14, waiting for transfers between devices: 14.7 us -> 17.9 us  [shift(): return lax.ppermute(a, axis, [(i, (i + step) % n) for i in range(n)])]
    ppermute x14, starting transfers between devices: 25.8 us -> 22.8 us  [shift(): return lax.ppermute(a, axis, [(i, (i + step) % n) for i in range(n)])]
    all_to_all x1, waiting for transfers between devices: 12.6 us -> 15.2 us  [shards(): parts = lax.all_to_all(parts, ('y', 'x'), 0, 0)]
    all_to_all x1, blocking collectives: 31.6 us -> 29.5 us  [shards(): grad_square = jnp.sum(lax.all_to_all(local, every, 0, 0)[:, 0, 0])]
  transfers between devices with their start and end apart: 15 -> 15, of which waited for: 8 -> 8; matrix products, arithmetic and copies ran while one was open for 1% -> 1% of each run, Pallas kernels for 12% -> 9%
where the time goes in v5:
time: 119 us
  waiting for transfers between devices  33.2 us (28%)
  starting transfers between devices  31.4 us (26%)
  blocking collectives  29.5 us (25%)
  Pallas kernels  16.8 us (14%)
  local copies, waits for them, and re-layouts  4.95 us (4%)
  other arithmetic  2.48 us (2%)
    all_to_all x1, blocking collectives, shards(): grad_square = jnp.sum(lax.all_to_all(local, every, 0, 0)[:, 0, 0])  29.5 us
    ppermute x14, starting transfers between devices, shift(): return lax.ppermute(a, axis, [(i, (i + step) % n) for i in range(n)])  22.8 us
    ppermute x14, waiting for transfers between devices, shift(): return lax.ppermute(a, axis, [(i, (i + step) % n) for i in range(n)])  17.9 us
    pallas_call x6, Pallas kernels, call(): pl.pallas_call(kernel, out_shape=tuple((pltpu.HBM(s, t) if c == 'H' else...  16.8 us
    all_to_all x1, waiting for transfers between devices, shards(): parts = lax.all_to_all(parts, ('y', 'x'), 0, 0)  15.2 us
    all_to_all x1, starting transfers between devices, shards(): parts = lax.all_to_all(parts, ('y', 'x'), 0, 0)  8.62 us
    unnamed x20, local copies, waits for them, and re-layouts  4.95 us
  transfers between devices with their start and end apart: 15, of which 8 were waited for; matrix products, arithmetic and copies ran while one was open for 1% of the time, Pallas kernels for 9%

profile of v5, /device:TPU:1, one launch (start us, length us, event | category | flops | bytes accessed | tf_op | source)
XLA Modules:
  0.0 119.1 jit_solution(15200477043041631409)
XLA Ops:
  1.4 7.8 %collective-permute-start = (bf16[2,128,128]{2,1,0:T(8,128)(2,1)S(1)}, bf16[2,128,128]{2,1,0:T(8,128)(2,1)S(1)}, u32[]{:S(2)}, u32[]{:S(2)}) collective-permute-start(bf16[2,128,128]{2,1,0:T(8,128)(2,1)S(1)} %get-tuple-element.62), channel_id=1, source_target_pairs={{0,8},{8,0},{1,9},{9,1},{2,10},{10,2},{3,11},{11,3},{4,12},{12,4},... | collective-permute-start | bytes 196616 | tf_op jit(solution)/shard_map/ppermute | solution.py:290
  9.2 1.8 %collective-permute-done = bf16[2,128,128]{2,1,0:T(8,128)(2,1)S(1)} collective-permute-done((bf16[2,128,128]{2,1,0:T(8,128)(2,1)S(1)}, bf16[2,128,128]{2,1,0:T(8,128)(2,1)S(1)}, u32[]{:S(2)}, u32[]{:S(2)}) %collective-permute-start) | collective-permute-done | bytes 65568 | tf_op jit(solution)/shard_map/ppermute | solution.py:290
  11.0 2.6 %collective-permute-start.6 = (bf16[2,128,128]{2,1,0:T(8,128)(2,1)S(1)}, bf16[2,128,128]{2,1,0:T(8,128)(2,1)S(1)}, u32[]{:S(2)}, u32[]{:S(2)}) collective-permute-start(bf16[2,128,128]{2,1,0:T(8,128)(2,1)S(1)} %get-tuple-element.46), channel_id=1, source_target_pairs={{0,48},{16,0},{32,16},{48,32},{1,49},{17,1},{33,17},{49,33},{2,50}... | collective-permute-start | bytes 196616 | tf_op jit(solution)/shard_map/ppermute | solution.py:290
  14.7 2.7 %collective-permute-start.3 = (bf16[2,128,128]{2,1,0:T(8,128)(2,1)S(1)}, bf16[2,128,128]{2,1,0:T(8,128)(2,1)S(1)}, u32[]{:S(2)}, u32[]{:S(2)}) collective-permute-start(bf16[2,128,128]{2,1,0:T(8,128)(2,1)S(1)} %get-tuple-element.38), channel_id=1, source_target_pairs={{0,192},{64,0},{128,64},{192,128},{1,193},{65,1},{129,65},{193,129... | collective-permute-start | bytes 196616 | tf_op jit(solution)/shard_map/ppermute | solution.py:290
  19.2 2.9 %collective-permute-done.2 = bf16[2,128,128]{2,1,0:T(8,128)(2,1)S(1)} collective-permute-done((bf16[2,128,128]{2,1,0:T(8,128)(2,1)S(1)}, bf16[2,128,128]{2,1,0:T(8,128)(2,1)S(1)}, u32[]{:S(2)}, u32[]{:S(2)}) %collective-permute-start.2) | collective-permute-done | bytes 65568 | tf_op jit(solution)/shard_map/ppermute | solution.py:290
  22.8 2.1 %collective-permute-start.9 = (bf16[4,2,128,128]{3,2,1,0:T(8,128)(2,1)S(1)}, bf16[4,2,128,128]{3,2,1,0:T(8,128)(2,1)S(1)}, u32[]{:S(2)}, u32[]{:S(2)}) collective-permute-start(bf16[4,2,128,128]{3,2,1,0:T(8,128)(2,1)S(1)} %pad_maximum_fusion), channel_id=1, source_target_pairs={{0,48},{16,0},{32,16},{48,32},{1,49},{17,1},{33,17},{49,33},{2,50}... | collective-permute-start | bytes 786440 | tf_op jit(solution)/shard_map/ppermute | solution.py:290
  24.9 1.2 %collective-permute-start.8 = (bf16[4,2,128,128]{3,2,1,0:T(8,128)(2,1)S(1)}, bf16[4,2,128,128]{3,2,1,0:T(8,128)(2,1)S(1)}, u32[]{:S(2)}, u32[]{:S(2)}) collective-permute-start(bf16[4,2,128,128]{3,2,1,0:T(8,128)(2,1)S(1)} %pad_maximum_fusion), channel_id=1, source_target_pairs={{0,32},{16,48},{32,0},{48,16},{1,33},{17,49},{33,1},{49,17},{2,34}... | collective-permute-start | bytes 786440 | tf_op jit(solution)/shard_map/ppermute | solution.py:290
  26.2 2.0 %shard_map.102 = (bf16[2048,128]{1,0:T(8,128)(2,1)S(1)}, bf16[2048,128]{1,0:T(8,128)(2,1)S(1)}, bf16[128,2048]{1,0:T(8,128)(2,1)S(1)}, bf16[128,2048]{1,0:T(8,128)(2,1)S(1)}, f32[16,1024]{1,0:T(8,128)S(1)}) custom-call(bf16[128,2048]{1,0:T(8,128)(2,1)} %q_hbm.1, bf16[128,2048]{1,0:T(8,128)(2,1)} %o_hbm.1, bf16[128,2048]{1,0:T(8,128)(2,1)} %g_hbm.1), custom_call_target="tpu_custom_call" | custom-call | flops 1073741824 | bytes 4194304 | tf_op jit(solution)/shard_map/pallas_call | solution.py:272
  29.5 1.2 %collective-permute-done.9 = bf16[4,2,128,128]{3,2,1,0:T(8,128)(2,1)S(1)} collective-permute-done((bf16[4,2,128,128]{3,2,1,0:T(8,128)(2,1)S(1)}, bf16[4,2,128,128]{3,2,1,0:T(8,128)(2,1)S(1)}, u32[]{:S(2)}, u32[]{:S(2)}) %collective-permute-start.9) | collective-permute-done | bytes 262176 | tf_op jit(solution)/shard_map/ppermute | solution.py:290
  30.7 1.1 collective-permute-done.8
  31.8 6.1 %collective-permute-done.7 = bf16[4,2,128,128]{3,2,1,0:T(8,128)(2,1)S(1)} collective-permute-done((bf16[4,2,128,128]{3,2,1,0:T(8,128)(2,1)S(1)}, bf16[4,2,128,128]{3,2,1,0:T(8,128)(2,1)S(1)}, u32[]{:S(2)}, u32[]{:S(2)}) %collective-permute-start.7) | collective-permute-done | bytes 262176 | tf_op jit(solution)/shard_map/ppermute | solution.py:290
  37.8 3.5 %shard_map.103 = (f32[3,704,1024]{2,1,0:T(8,128)S(1)}, f32[3,704,1024]{2,1,0:T(8,128)S(1)}, f32[2,3,8,1024]{3,2,1,0:T(8,128)S(1)}, f32[16,1024]{1,0:T(8,128)S(1)}) custom-call(s32[72]{0:T(128)S(1)} %pad_add_fusion.meta_ref, bf16[128,2048]{1,0:T(8,128)(2,1)S(1)} %get-tuple-element.37.qt, bf16[1024,128]{1,0:T(8,128)(2,1)S(1)} %bitcast.26, ...), custom_call_target="tpu_custom_call" | custom-call | flops 8589934592 | bytes 4194304 | tf_op jit(solution)/shard_map/pallas_call | solution.py:272
  41.4 5.2 %shard_map.104 = (bf16[4096,256]{1,0:T(8,128)(2,1)}, f32[16,1024]{1,0:T(8,128)S(1)}) custom-call(s32[72]{0:T(128)S(1)} %pad_add_fusion.meta_ref, bf16[2048,128]{1,0:T(8,128)(2,1)S(1)} %get-tuple-element.33.qs, bf16[2048,128]{1,0:T(8,128)(2,1)S(1)} %get-tuple-element.34.gs, bf16[128,2048]{1,0:T(8,128)(2,1)S(1)} %get-tuple-element.35.gt, ...), custom_call_target="tpu_custom_call" | custom-call | flops 17179869184 | bytes 4194304 | tf_op jit(solution)/shard_map/pallas_call | solution.py:272
  46.7 8.6 %all-to-all-start = ((bf16[16,2,128,256]{3,2,1,0:T(8,128)(2,1)}), bf16[16,2,128,256]{3,2,1,0:T(8,128)(2,1)S(1)}, u32[]{:S(2)}, u32[]{:S(2)}) async-start(bf16[16,2,128,256]{3,2,1,0:T(8,128)(2,1)} %bitcast.42), calls=%async_computation | async-start | bytes 4194304 | tf_op jit(solution)/shard_map/all_to_all | solution.py:335
  55.3 0.9 copy-done.1
  56.3 0.9 copy-done.3
  57.2 0.9 copy-done.5
  58.2 1.0 copy-done.7
  59.2 1.0 copy-done.9
  60.3 5.1 %shard_map.105 = (bf16[128,2048]{1,0:T(8,128)(2,1)}, f32[8,128]{1,0:T(8,128)S(1)}) custom-call(s32[72]{0:T(128)S(1)} %pad_add_fusion.meta_ref, bf16[128,2048]{1,0:T(8,128)(2,1)S(1)} %copy-done.7, bf16[128,2048]{1,0:T(8,128)(2,1)S(1)} %copy-done.9, f32[16,1024]{1,0:T(8,128)S(1)} %get-tuple-element.36.delta_ref, f32[16,1024]{1,0:T(8,128)S(1)} %get-tuple-element.51.lse_ref, ...), custom_call_target="tpu_custom_call" | custom-call | flops 17179869184 | bytes 4194304 | tf_op jit(solution)/shard_map/pallas_call | solution.py:272
  65.4 15.2 %all-to-all-done.parts_ref = bf16[16,2,128,256]{3,2,1,0:T(8,128)(2,1)S(1)} async-done(((bf16[16,2,128,256]{3,2,1,0:T(8,128)(2,1)}), bf16[16,2,128,256]{3,2,1,0:T(8,128)(2,1)S(1)}, u32[]{:S(2)}, u32[]{:S(2)}) %all-to-all-start) | async-done | bytes 2097184 | tf_op jit(solution)/shard_map/all_to_all | solution.py:335
  80.8 2.9 %collective-permute-start.13 = (bf16[128,256]{1,0:T(8,128)(2,1)S(1)}, bf16[128,256]{1,0:T(8,128)(2,1)S(1)}, u32[]{:S(2)}, u32[]{:S(2)}) collective-permute-start(bf16[128,256]{1,0:T(8,128)(2,1)S(1)} %shard_map.106), channel_id=1, source_target_pairs={{0,8},{8,0},{1,9},{9,1},{2,10},{10,2},{3,11},{11,3},{4,12},{12,4},... | collective-permute-start | bytes 196616 | tf_op jit(solution)/shard_map/ppermute | solution.py:290
  83.7 4.2 %collective-permute-done.13.other_ref = bf16[128,256]{1,0:T(8,128)(2,1)S(1)} collective-permute-done((bf16[128,256]{1,0:T(8,128)(2,1)S(1)}, bf16[128,256]{1,0:T(8,128)(2,1)S(1)}, u32[]{:S(2)}, u32[]{:S(2)}) %collective-permute-start.13) | collective-permute-done | bytes 65568 | tf_op jit(solution)/shard_map/ppermute | solution.py:290
  88.7 29.5 %all_to_all.10 = f32[256,1,128]{2,1,0:T(1,128)S(1)} all-to-all(f32[256,1,128]{2,1,0:T(1,128)S(1)} %get-tuple-element.59), channel_id=1, replica_groups=mesh['y'=4,'x'=4,'zh'=2,'tp'=8] {'y','x','zh','tp'}, dimensions={0} | all-to-all | bytes 262144 | tf_op jit(solution)/shard_map/all_to_all | solution.py:353
  (39 shorter events, 7.6 us)
Async XLA Ops:
  1.4 9.6 %collective-permute-start = (bf16[2,128,128]{2,1,0:T(8,128)(2,1)S(1)}, bf16[2,128,128]{2,1,0:T(8,128)(2,1)S(1)}, u32[]{:S(2)}, u32[]{:S(2)}) collective-permute-start(bf16[2,128,128]{2,1,0:T(8,128)(2,1)S(1)} %get-tuple-element.62), channel_id=1, source_target_pairs={{0,8},{8,0},{1,9},{9,1},{2,10},{10,2},{3,11},{11,3},{4,12},{12,4},... | collective-permute-start | bytes 196616 | tf_op jit(solution)/shard_map/ppermute | solution.py:290
  11.0 6.8 %collective-permute-start.6 = (bf16[2,128,128]{2,1,0:T(8,128)(2,1)S(1)}, bf16[2,128,128]{2,1,0:T(8,128)(2,1)S(1)}, u32[]{:S(2)}, u32[]{:S(2)}) collective-permute-start(bf16[2,128,128]{2,1,0:T(8,128)(2,1)S(1)} %get-tuple-element.46), channel_id=1, source_target_pairs={{0,48},{16,0},{32,16},{48,32},{1,49},{17,1},{33,17},{49,33},{2,50}... | collective-permute-start | bytes 196616 | tf_op jit(solution)/shard_map/ppermute | solution.py:290
  13.6 5.7 %collective-permute-start.5 = (bf16[2,128,128]{2,1,0:T(8,128)(2,1)S(1)}, bf16[2,128,128]{2,1,0:T(8,128)(2,1)S(1)}, u32[]{:S(2)}, u32[]{:S(2)}) collective-permute-start(bf16[2,128,128]{2,1,0:T(8,128)(2,1)S(1)} %get-tuple-element.46), channel_id=1, source_target_pairs={{0,32},{16,48},{32,0},{48,16},{1,33},{17,49},{33,1},{49,17},{2,34}... | collective-permute-start | bytes 196616 | tf_op jit(solution)/shard_map/ppermute | solution.py:290
  14.1 5.1 %collective-permute-start.4 = (bf16[2,128,128]{2,1,0:T(8,128)(2,1)S(1)}, bf16[2,128,128]{2,1,0:T(8,128)(2,1)S(1)}, u32[]{:S(2)}, u32[]{:S(2)}) collective-permute-start(bf16[2,128,128]{2,1,0:T(8,128)(2,1)S(1)} %get-tuple-element.46), channel_id=1, source_target_pairs={{0,16},{16,32},{32,48},{48,0},{1,17},{17,33},{33,49},{49,1},{2,18}... | collective-permute-start | bytes 196616 | tf_op jit(solution)/shard_map/ppermute | solution.py:290
  14.7 4.5 %collective-permute-start.3 = (bf16[2,128,128]{2,1,0:T(8,128)(2,1)S(1)}, bf16[2,128,128]{2,1,0:T(8,128)(2,1)S(1)}, u32[]{:S(2)}, u32[]{:S(2)}) collective-permute-start(bf16[2,128,128]{2,1,0:T(8,128)(2,1)S(1)} %get-tuple-element.38), channel_id=1, source_target_pairs={{0,192},{64,0},{128,64},{192,128},{1,193},{65,1},{129,65},{193,129... | collective-permute-start | bytes 196616 | tf_op jit(solution)/shard_map/ppermute | solution.py:290
  17.4 4.7 %collective-permute-start.2 = (bf16[2,128,128]{2,1,0:T(8,128)(2,1)S(1)}, bf16[2,128,128]{2,1,0:T(8,128)(2,1)S(1)}, u32[]{:S(2)}, u32[]{:S(2)}) collective-permute-start(bf16[2,128,128]{2,1,0:T(8,128)(2,1)S(1)} %get-tuple-element.38), channel_id=1, source_target_pairs={{0,128},{64,192},{128,0},{192,64},{1,129},{65,193},{129,1},{193,65... | collective-permute-start | bytes 196616 | tf_op jit(solution)/shard_map/ppermute | solution.py:290
  17.8 5.0 %collective-permute-start.1 = (bf16[2,128,128]{2,1,0:T(8,128)(2,1)S(1)}, bf16[2,128,128]{2,1,0:T(8,128)(2,1)S(1)}, u32[]{:S(2)}, u32[]{:S(2)}) collective-permute-start(bf16[2,128,128]{2,1,0:T(8,128)(2,1)S(1)} %get-tuple-element.38), channel_id=1, source_target_pairs={{0,64},{64,128},{128,192},{192,0},{1,65},{65,129},{129,193},{193,1... | collective-permute-start | bytes 196616 | tf_op jit(solution)/shard_map/ppermute | solution.py:290
  22.8 7.9 %collective-permute-start.9 = (bf16[4,2,128,128]{3,2,1,0:T(8,128)(2,1)S(1)}, bf16[4,2,128,128]{3,2,1,0:T(8,128)(2,1)S(1)}, u32[]{:S(2)}, u32[]{:S(2)}) collective-permute-start(bf16[4,2,128,128]{3,2,1,0:T(8,128)(2,1)S(1)} %pad_maximum_fusion), channel_id=1, source_target_pairs={{0,48},{16,0},{32,16},{48,32},{1,49},{17,1},{33,17},{49,33},{2,50}... | collective-permute-start | bytes 786440 | tf_op jit(solution)/shard_map/ppermute | solution.py:290
  24.9 6.8 %collective-permute-start.8 = (bf16[4,2,128,128]{3,2,1,0:T(8,128)(2,1)S(1)}, bf16[4,2,128,128]{3,2,1,0:T(8,128)(2,1)S(1)}, u32[]{:S(2)}, u32[]{:S(2)}) collective-permute-start(bf16[4,2,128,128]{3,2,1,0:T(8,128)(2,1)S(1)} %pad_maximum_fusion), channel_id=1, source_target_pairs={{0,32},{16,48},{32,0},{48,16},{1,33},{17,49},{33,1},{49,17},{2,34}... | collective-permute-start | bytes 786440 | tf_op jit(solution)/shard_map/ppermute | solution.py:290
  26.2 11.7 %collective-permute-start.7 = (bf16[4,2,128,128]{3,2,1,0:T(8,128)(2,1)S(1)}, bf16[4,2,128,128]{3,2,1,0:T(8,128)(2,1)S(1)}, u32[]{:S(2)}, u32[]{:S(2)}) collective-permute-start(bf16[4,2,128,128]{3,2,1,0:T(8,128)(2,1)S(1)} %pad_maximum_fusion), channel_id=1, source_target_pairs={{0,16},{16,32},{32,48},{48,0},{1,17},{17,33},{33,49},{49,1},{2,18}... | collective-permute-start | bytes 786440 | tf_op jit(solution)/shard_map/ppermute | solution.py:290
  28.1 13.2 %copy-start.6 = (bf16[128,2048]{1,0:T(8,128)(2,1)}, bf16[128,2048]{1,0:T(8,128)(2,1)S(1)}, u32[]{:S(2)}) copy-start(bf16[128,2048]{1,0:T(8,128)(2,1)S(1)} %get-tuple-element.37.qt) | copy-start | bytes 1572868
  28.2 13.3 %copy-start.8 = (bf16[128,2048]{1,0:T(8,128)(2,1)}, bf16[128,2048]{1,0:T(8,128)(2,1)S(1)}, u32[]{:S(2)}) copy-start(bf16[128,2048]{1,0:T(8,128)(2,1)S(1)} %get-tuple-element.35.gt) | copy-start | bytes 1572868
  28.2 13.1 %collective-permute-start.12 = (bf16[4,2,128,128]{3,2,1,0:T(8,128)(2,1)S(1)}, bf16[4,2,128,128]{3,2,1,0:T(8,128)(2,1)S(1)}, u32[]{:S(2)}, u32[]{:S(2)}) collective-permute-start(bf16[4,2,128,128]{3,2,1,0:T(8,128)(2,1)S(1)} %pad_maximum_fusion.1), channel_id=1, source_target_pairs={{0,192},{64,0},{128,64},{192,128},{1,193},{65,1},{129,65},{193,129... | collective-permute-start | bytes 786440 | tf_op jit(solution)/shard_map/ppermute | solution.py:290
  28.6 12.8 %collective-permute-start.11 = (bf16[4,2,128,128]{3,2,1,0:T(8,128)(2,1)S(1)}, bf16[4,2,128,128]{3,2,1,0:T(8,128)(2,1)S(1)}, u32[]{:S(2)}, u32[]{:S(2)}) collective-permute-start(bf16[4,2,128,128]{3,2,1,0:T(8,128)(2,1)S(1)} %pad_maximum_fusion.1), channel_id=1, source_target_pairs={{0,128},{64,192},{128,0},{192,64},{1,129},{65,193},{129,1},{193,65... | collective-permute-start | bytes 786440 | tf_op jit(solution)/shard_map/ppermute | solution.py:290
  30.7 10.7 %collective-permute-start.10 = (bf16[4,2,128,128]{3,2,1,0:T(8,128)(2,1)S(1)}, bf16[4,2,128,128]{3,2,1,0:T(8,128)(2,1)S(1)}, u32[]{:S(2)}, u32[]{:S(2)}) collective-permute-start(bf16[4,2,128,128]{3,2,1,0:T(8,128)(2,1)S(1)} %pad_maximum_fusion.1), channel_id=1, source_target_pairs={{0,64},{64,128},{128,192},{192,0},{1,65},{65,129},{129,193},{193,1... | collective-permute-start | bytes 786440 | tf_op jit(solution)/shard_map/ppermute | solution.py:290
  41.4 5.3 %copy-start = (bf16[4,2,128,128]{3,2,1,0:T(8,128)(2,1)}, bf16[4,2,128,128]{3,2,1,0:T(8,128)(2,1)S(1)}, u32[]{:S(2)}) copy-start(bf16[4,2,128,128]{3,2,1,0:T(8,128)(2,1)S(1)} %collective-permute-done.12) | copy-start | bytes 786436
  41.4 5.3 %copy-start.2 = (bf16[4,2,128,128]{3,2,1,0:T(8,128)(2,1)}, bf16[4,2,128,128]{3,2,1,0:T(8,128)(2,1)S(1)}, u32[]{:S(2)}) copy-start(bf16[4,2,128,128]{3,2,1,0:T(8,128)(2,1)S(1)} %collective-permute-done.11) | copy-start | bytes 786436
  41.4 5.3 %copy-start.4 = (bf16[4,2,128,128]{3,2,1,0:T(8,128)(2,1)}, bf16[4,2,128,128]{3,2,1,0:T(8,128)(2,1)S(1)}, u32[]{:S(2)}) copy-start(bf16[4,2,128,128]{3,2,1,0:T(8,128)(2,1)S(1)} %collective-permute-done.10) | copy-start | bytes 786436
  46.7 33.9 %all-to-all-start = ((bf16[16,2,128,256]{3,2,1,0:T(8,128)(2,1)}), bf16[16,2,128,256]{3,2,1,0:T(8,128)(2,1)S(1)}, u32[]{:S(2)}, u32[]{:S(2)}) async-start(bf16[16,2,128,256]{3,2,1,0:T(8,128)(2,1)} %bitcast.42), calls=%async_computation | async-start | bytes 4194304 | tf_op jit(solution)/shard_map/all_to_all | solution.py:335
  55.3 1.0 copy-start.1
  56.3 0.9 copy-start.3
  58.2 1.0 copy-start.7
  59.2 1.0 copy-start.9
  80.8 7.1 %collective-permute-start.13 = (bf16[128,256]{1,0:T(8,128)(2,1)S(1)}, bf16[128,256]{1,0:T(8,128)(2,1)S(1)}, u32[]{:S(2)}, u32[]{:S(2)}) collective-permute-start(bf16[128,256]{1,0:T(8,128)(2,1)S(1)} %shard_map.106), channel_id=1, source_target_pairs={{0,8},{8,0},{1,9},{9,1},{2,10},{10,2},{3,11},{11,3},{4,12},{12,4},... | collective-permute-start | bytes 196616 | tf_op jit(solution)/shard_map/ppermute | solution.py:290
  (1 other events, 0.9 us)

commit v6 on v5

--- a/solution.py
+++ b/solution.py
@@ -237,19 +237,23 @@
     sq_ref[...] = jnp.broadcast_to(square[0] + square[1], sq_ref.shape)
 
 
-def sum_kernel(parts_ref, other_ref):
-    index = 1 - lax.axis_index("zh")
+def half_sum(parts_ref, index):
     total = parts_ref[0, index].astype(f32)
     for h in range(1, NY * NX):
         total = total + parts_ref[h, index].astype(f32)
-    other_ref[...] = total.astype(bf16)
-
-
-def finish_kernel(parts_ref, other_ref, sq_ref, dk_ref, dv_ref, local_ref):
-    index = lax.axis_index("zh")
-    total = parts_ref[0, index].astype(f32)
-    for h in range(1, NY * NX):
-        total = total + parts_ref[h, index].astype(f32)
+    return total
+
+
+def other_kernel(parts_ref, other_ref):
+    other_ref[...] = half_sum(parts_ref, 1 - lax.axis_index("zh")).astype(bf16)
+
+
+def own_kernel(parts_ref, own_ref):
+    own_ref[...] = half_sum(parts_ref, lax.axis_index("zh"))
+
+
+def finish_kernel(own_ref, other_ref, sq_ref, dk_ref, dv_ref, local_ref):
+    total = own_ref[...]
     both = (total + other_ref[...].astype(f32)).astype(bf16)
     dk_ref[...] = both[:, :HD]
     dv_ref[...] = both[:, HD:]
@@ -342,13 +346,14 @@
     )
     parts, query_grad, square = lax.optimization_barrier((parts, query_grad, square))
     half = ((tq, HD), bf16)
-    (other,) = call(sum_kernel, [((tq, 2 * HD), bf16)], "V V", [], 1 << 20, 16, parts)
+    (other,) = call(other_kernel, [((tq, 2 * HD), bf16)], "V V", [], 1 << 20, 16, parts)
+    (own,) = call(own_kernel, [((tq, 2 * HD), f32)], "V V", [], 1 << 30, 16, parts)
     every = ("y", "x", "zh", "tp")
     key_grad, value_grad, local = call(
         finish_kernel,
         [half, half, ((lax.axis_size(every), 1, HD), f32)],
         "VVV VVV",
-        [], 1 << 20, 16, parts, shift(other, "zh", 1), square,
+        [], 1 << 20, 16, own, shift(other, "zh", 1), square,
     )
     grad_square = jnp.sum(lax.all_to_all(local, every, 0, 0)[:, 0, 0])
     return (query_grad, key_grad, value_grad, grad_square)

time: 119 us -> 120 us (level)
  waiting for transfers between devices: 33.2 us -> 30.1 us
  starting transfers between devices: 31.4 us -> 33.8 us
  blocking collectives: 29.5 us -> 31.1 us
    ppermute x14, starting transfers between devices: 22.8 us -> 26 us  [shift(): return lax.ppermute(a, axis, [(i, (i + step) % n) for i in range(n)])]
    ppermute x14, waiting for transfers between devices: 17.9 us -> 15.3 us  [shift(): return lax.ppermute(a, axis, [(i, (i + step) % n) for i in range(n)])]
    all_to_all x1, blocking collectives: 29.5 us -> 31.1 us  [shards(): grad_square = jnp.sum(lax.all_to_all(local, every, 0, 0)[:, 0, 0])]
    pallas_call x6 -> x7, Pallas kernels: 16.8 us -> 16.8 us  [call(): pl.pallas_call(kernel, out_shape=tuple((pltpu.HBM(s, t) if c == 'H' else...]
where the time goes in v6:
time: 120 us
  starting transfers between devices  33.8 us (28%)
  blocking collectives  31.1 us (26%)
  waiting for transfers between devices  30.1 us (25%)
  Pallas kernels  16.8 us (14%)
  local copies, waits for them, and re-layouts  4.95 us (4%)
  other arithmetic  2.48 us (2%)
    all_to_all x1, blocking collectives, shards(): grad_square = jnp.sum(lax.all_to_all(local, every, 0, 0)[:, 0, 0])  31.1 us
    ppermute x14, starting transfers between devices, shift(): return lax.ppermute(a, axis, [(i, (i + step) % n) for i in range(n)])  26 us
    pallas_call x7, Pallas kernels, call(): pl.pallas_call(kernel, out_shape=tuple((pltpu.HBM(s, t) if c == 'H' else...  16.8 us
    ppermute x14, waiting for transfers between devices, shift(): return lax.ppermute(a, axis, [(i, (i + step) % n) for i in range(n)])  15.3 us
    all_to_all x1, waiting for transfers between devices, shards(): parts = lax.all_to_all(parts, ('y', 'x'), 0, 0)  14.8 us
    all_to_all x1, starting transfers between devices, shards(): parts = lax.all_to_all(parts, ('y', 'x'), 0, 0)  7.82 us
    unnamed x20, local copies, waits for them, and re-layouts  4.95 us
  transfers between devices with their start and end apart: 15, of which 8 were waited for; matrix products, arithmetic and copies ran while one was open for 1% of the time, Pallas kernels for 9%

profile of v6, /device:TPU:1, one launch (start us, length us, event | category | flops | bytes accessed | tf_op | source)
XLA Modules:
  0.0 120.0 jit_solution(6939412547004225748)
XLA Ops:
  1.4 7.8 %collective-permute-start = (bf16[2,128,128]{2,1,0:T(8,128)(2,1)S(1)}, bf16[2,128,128]{2,1,0:T(8,128)(2,1)S(1)}, u32[]{:S(2)}, u32[]{:S(2)}) collective-permute-start(bf16[2,128,128]{2,1,0:T(8,128)(2,1)S(1)} %get-tuple-element.62), channel_id=1, source_target_pairs={{0,8},{8,0},{1,9},{9,1},{2,10},{10,2},{3,11},{11,3},{4,12},{12,4},... | collective-permute-start | bytes 196616 | tf_op jit(solution)/shard_map/ppermute | solution.py:294
  9.2 1.8 %collective-permute-done = bf16[2,128,128]{2,1,0:T(8,128)(2,1)S(1)} collective-permute-done((bf16[2,128,128]{2,1,0:T(8,128)(2,1)S(1)}, bf16[2,128,128]{2,1,0:T(8,128)(2,1)S(1)}, u32[]{:S(2)}, u32[]{:S(2)}) %collective-permute-start) | collective-permute-done | bytes 65568 | tf_op jit(solution)/shard_map/ppermute | solution.py:294
  11.0 2.6 %collective-permute-start.6 = (bf16[2,128,128]{2,1,0:T(8,128)(2,1)S(1)}, bf16[2,128,128]{2,1,0:T(8,128)(2,1)S(1)}, u32[]{:S(2)}, u32[]{:S(2)}) collective-permute-start(bf16[2,128,128]{2,1,0:T(8,128)(2,1)S(1)} %get-tuple-element.46), channel_id=1, source_target_pairs={{0,48},{16,0},{32,16},{48,32},{1,49},{17,1},{33,17},{49,33},{2,50}... | collective-permute-start | bytes 196616 | tf_op jit(solution)/shard_map/ppermute | solution.py:294
  14.7 2.7 %collective-permute-start.3 = (bf16[2,128,128]{2,1,0:T(8,128)(2,1)S(1)}, bf16[2,128,128]{2,1,0:T(8,128)(2,1)S(1)}, u32[]{:S(2)}, u32[]{:S(2)}) collective-permute-start(bf16[2,128,128]{2,1,0:T(8,128)(2,1)S(1)} %get-tuple-element.38), channel_id=1, source_target_pairs={{0,192},{64,0},{128,64},{192,128},{1,193},{65,1},{129,65},{193,129... | collective-permute-start | bytes 196616 | tf_op jit(solution)/shard_map/ppermute | solution.py:294
  19.2 2.9 %collective-permute-done.2 = bf16[2,128,128]{2,1,0:T(8,128)(2,1)S(1)} collective-permute-done((bf16[2,128,128]{2,1,0:T(8,128)(2,1)S(1)}, bf16[2,128,128]{2,1,0:T(8,128)(2,1)S(1)}, u32[]{:S(2)}, u32[]{:S(2)}) %collective-permute-start.2) | collective-permute-done | bytes 65568 | tf_op jit(solution)/shard_map/ppermute | solution.py:294
  22.8 2.1 %collective-permute-start.9 = (bf16[4,2,128,128]{3,2,1,0:T(8,128)(2,1)S(1)}, bf16[4,2,128,128]{3,2,1,0:T(8,128)(2,1)S(1)}, u32[]{:S(2)}, u32[]{:S(2)}) collective-permute-start(bf16[4,2,128,128]{3,2,1,0:T(8,128)(2,1)S(1)} %pad_maximum_fusion), channel_id=1, source_target_pairs={{0,48},{16,0},{32,16},{48,32},{1,49},{17,1},{33,17},{49,33},{2,50}... | collective-permute-start | bytes 786440 | tf_op jit(solution)/shard_map/ppermute | solution.py:294
  24.9 1.2 %collective-permute-start.8 = (bf16[4,2,128,128]{3,2,1,0:T(8,128)(2,1)S(1)}, bf16[4,2,128,128]{3,2,1,0:T(8,128)(2,1)S(1)}, u32[]{:S(2)}, u32[]{:S(2)}) collective-permute-start(bf16[4,2,128,128]{3,2,1,0:T(8,128)(2,1)S(1)} %pad_maximum_fusion), channel_id=1, source_target_pairs={{0,32},{16,48},{32,0},{48,16},{1,33},{17,49},{33,1},{49,17},{2,34}... | collective-permute-start | bytes 786440 | tf_op jit(solution)/shard_map/ppermute | solution.py:294
  26.2 2.0 %shard_map.102 = (bf16[2048,128]{1,0:T(8,128)(2,1)S(1)}, bf16[2048,128]{1,0:T(8,128)(2,1)S(1)}, bf16[128,2048]{1,0:T(8,128)(2,1)S(1)}, bf16[128,2048]{1,0:T(8,128)(2,1)S(1)}, f32[16,1024]{1,0:T(8,128)S(1)}) custom-call(bf16[128,2048]{1,0:T(8,128)(2,1)} %q_hbm.1, bf16[128,2048]{1,0:T(8,128)(2,1)} %o_hbm.1, bf16[128,2048]{1,0:T(8,128)(2,1)} %g_hbm.1), custom_call_target="tpu_custom_call" | custom-call | flops 1073741824 | bytes 4194304 | tf_op jit(solution)/shard_map/pallas_call | solution.py:276
  29.5 1.2 %collective-permute-done.9 = bf16[4,2,128,128]{3,2,1,0:T(8,128)(2,1)S(1)} collective-permute-done((bf16[4,2,128,128]{3,2,1,0:T(8,128)(2,1)S(1)}, bf16[4,2,128,128]{3,2,1,0:T(8,128)(2,1)S(1)}, u32[]{:S(2)}, u32[]{:S(2)}) %collective-permute-start.9) | collective-permute-done | bytes 262176 | tf_op jit(solution)/shard_map/ppermute | solution.py:294
  30.7 1.1 collective-permute-done.8
  31.8 6.1 %collective-permute-done.7 = bf16[4,2,128,128]{3,2,1,0:T(8,128)(2,1)S(1)} collective-permute-done((bf16[4,2,128,128]{3,2,1,0:T(8,128)(2,1)S(1)}, bf16[4,2,128,128]{3,2,1,0:T(8,128)(2,1)S(1)}, u32[]{:S(2)}, u32[]{:S(2)}) %collective-permute-start.7) | collective-permute-done | bytes 262176 | tf_op jit(solution)/shard_map/ppermute | solution.py:294
  37.8 3.5 %shard_map.103 = (f32[3,704,1024]{2,1,0:T(8,128)S(1)}, f32[3,704,1024]{2,1,0:T(8,128)S(1)}, f32[2,3,8,1024]{3,2,1,0:T(8,128)S(1)}, f32[16,1024]{1,0:T(8,128)S(1)}) custom-call(s32[72]{0:T(128)S(1)} %pad_add_fusion.meta_ref, bf16[128,2048]{1,0:T(8,128)(2,1)S(1)} %get-tuple-element.37.qt, bf16[1024,128]{1,0:T(8,128)(2,1)S(1)} %bitcast.26, ...), custom_call_target="tpu_custom_call" | custom-call | flops 8589934592 | bytes 4194304 | tf_op jit(solution)/shard_map/pallas_call | solution.py:276
  41.4 5.2 %shard_map.104 = (bf16[4096,256]{1,0:T(8,128)(2,1)}, f32[16,1024]{1,0:T(8,128)S(1)}) custom-call(s32[72]{0:T(128)S(1)} %pad_add_fusion.meta_ref, bf16[2048,128]{1,0:T(8,128)(2,1)S(1)} %get-tuple-element.33.qs, bf16[2048,128]{1,0:T(8,128)(2,1)S(1)} %get-tuple-element.34.gs, bf16[128,2048]{1,0:T(8,128)(2,1)S(1)} %get-tuple-element.35.gt, ...), custom_call_target="tpu_custom_call" | custom-call | flops 17179869184 | bytes 4194304 | tf_op jit(solution)/shard_map/pallas_call | solution.py:276
  46.7 7.8 %all-to-all-start = ((bf16[16,2,128,256]{3,2,1,0:T(8,128)(2,1)}), bf16[16,2,128,256]{3,2,1,0:T(8,128)(2,1)S(1)}, u32[]{:S(2)}, u32[]{:S(2)}) async-start(bf16[16,2,128,256]{3,2,1,0:T(8,128)(2,1)} %bitcast.42), calls=%async_computation | async-start | bytes 4194304 | tf_op jit(solution)/shard_map/all_to_all | solution.py:339
  54.5 0.9 copy-done.1
  55.5 0.9 copy-done.3
  56.4 0.9 copy-done.5
  57.4 1.0 copy-done.7
  58.4 1.0 copy-done.9
  59.5 5.1 %shard_map.105 = (bf16[128,2048]{1,0:T(8,128)(2,1)}, f32[8,128]{1,0:T(8,128)S(1)}) custom-call(s32[72]{0:T(128)S(1)} %pad_add_fusion.meta_ref, bf16[128,2048]{1,0:T(8,128)(2,1)S(1)} %copy-done.7, bf16[128,2048]{1,0:T(8,128)(2,1)S(1)} %copy-done.9, f32[16,1024]{1,0:T(8,128)S(1)} %get-tuple-element.36.delta_ref, f32[16,1024]{1,0:T(8,128)S(1)} %get-tuple-element.51.lse_ref, ...), custom_call_target="tpu_custom_call" | custom-call | flops 17179869184 | bytes 4194304 | tf_op jit(solution)/shard_map/pallas_call | solution.py:276
  64.6 14.8 %all-to-all-done.parts_ref = bf16[16,2,128,256]{3,2,1,0:T(8,128)(2,1)S(1)} async-done(((bf16[16,2,128,256]{3,2,1,0:T(8,128)(2,1)}), bf16[16,2,128,256]{3,2,1,0:T(8,128)(2,1)S(1)}, u32[]{:S(2)}, u32[]{:S(2)}) %all-to-all-start) | async-done | bytes 2097184 | tf_op jit(solution)/shard_map/all_to_all | solution.py:339
  79.6 6.1 %collective-permute-start.13 = (bf16[128,256]{1,0:T(8,128)(2,1)S(1)}, bf16[128,256]{1,0:T(8,128)(2,1)S(1)}, u32[]{:S(2)}, u32[]{:S(2)}) collective-permute-start(bf16[128,256]{1,0:T(8,128)(2,1)S(1)} %shard_map.107), channel_id=1, source_target_pairs={{0,8},{8,0},{1,9},{9,1},{2,10},{10,2},{3,11},{11,3},{4,12},{12,4},... | collective-permute-start | bytes 196616 | tf_op jit(solution)/shard_map/ppermute | solution.py:294
  85.8 1.6 %collective-permute-done.13.other_ref = bf16[128,256]{1,0:T(8,128)(2,1)S(1)} collective-permute-done((bf16[128,256]{1,0:T(8,128)(2,1)S(1)}, bf16[128,256]{1,0:T(8,128)(2,1)S(1)}, u32[]{:S(2)}, u32[]{:S(2)}) %collective-permute-start.13) | collective-permute-done | bytes 65568 | tf_op jit(solution)/shard_map/ppermute | solution.py:294
  88.0 31.1 %all_to_all.10 = f32[256,1,128]{2,1,0:T(1,128)S(1)} all-to-all(f32[256,1,128]{2,1,0:T(1,128)S(1)} %get-tuple-element.59), channel_id=1, replica_groups=mesh['y'=4,'x'=4,'zh'=2,'tp'=8] {'y','x','zh','tp'}, dimensions={0} | all-to-all | bytes 262144 | tf_op jit(solution)/shard_map/all_to_all | solution.py:358
  (40 shorter events, 7.5 us)
Async XLA Ops:
  1.4 9.6 %collective-permute-start = (bf16[2,128,128]{2,1,0:T(8,128)(2,1)S(1)}, bf16[2,128,128]{2,1,0:T(8,128)(2,1)S(1)}, u32[]{:S(2)}, u32[]{:S(2)}) collective-permute-start(bf16[2,128,128]{2,1,0:T(8,128)(2,1)S(1)} %get-tuple-element.62), channel_id=1, source_target_pairs={{0,8},{8,0},{1,9},{9,1},{2,10},{10,2},{3,11},{11,3},{4,12},{12,4},... | collective-permute-start | bytes 196616 | tf_op jit(solution)/shard_map/ppermute | solution.py:294
  11.0 6.8 %collective-permute-start.6 = (bf16[2,128,128]{2,1,0:T(8,128)(2,1)S(1)}, bf16[2,128,128]{2,1,0:T(8,128)(2,1)S(1)}, u32[]{:S(2)}, u32[]{:S(2)}) collective-permute-start(bf16[2,128,128]{2,1,0:T(8,128)(2,1)S(1)} %get-tuple-element.46), channel_id=1, source_target_pairs={{0,48},{16,0},{32,16},{48,32},{1,49},{17,1},{33,17},{49,33},{2,50}... | collective-permute-start | bytes 196616 | tf_op jit(solution)/shard_map/ppermute | solution.py:294
  13.6 5.7 %collective-permute-start.5 = (bf16[2,128,128]{2,1,0:T(8,128)(2,1)S(1)}, bf16[2,128,128]{2,1,0:T(8,128)(2,1)S(1)}, u32[]{:S(2)}, u32[]{:S(2)}) collective-permute-start(bf16[2,128,128]{2,1,0:T(8,128)(2,1)S(1)} %get-tuple-element.46), channel_id=1, source_target_pairs={{0,32},{16,48},{32,0},{48,16},{1,33},{17,49},{33,1},{49,17},{2,34}... | collective-permute-start | bytes 196616 | tf_op jit(solution)/shard_map/ppermute | solution.py:294
  14.1 5.1 %collective-permute-start.4 = (bf16[2,128,128]{2,1,0:T(8,128)(2,1)S(1)}, bf16[2,128,128]{2,1,0:T(8,128)(2,1)S(1)}, u32[]{:S(2)}, u32[]{:S(2)}) collective-permute-start(bf16[2,128,128]{2,1,0:T(8,128)(2,1)S(1)} %get-tuple-element.46), channel_id=1, source_target_pairs={{0,16},{16,32},{32,48},{48,0},{1,17},{17,33},{33,49},{49,1},{2,18}... | collective-permute-start | bytes 196616 | tf_op jit(solution)/shard_map/ppermute | solution.py:294
  14.7 4.5 %collective-permute-start.3 = (bf16[2,128,128]{2,1,0:T(8,128)(2,1)S(1)}, bf16[2,128,128]{2,1,0:T(8,128)(2,1)S(1)}, u32[]{:S(2)}, u32[]{:S(2)}) collective-permute-start(bf16[2,128,128]{2,1,0:T(8,128)(2,1)S(1)} %get-tuple-element.38), channel_id=1, source_target_pairs={{0,192},{64,0},{128,64},{192,128},{1,193},{65,1},{129,65},{193,129... | collective-permute-start | bytes 196616 | tf_op jit(solution)/shard_map/ppermute | solution.py:294
  17.4 4.7 %collective-permute-start.2 = (bf16[2,128,128]{2,1,0:T(8,128)(2,1)S(1)}, bf16[2,128,128]{2,1,0:T(8,128)(2,1)S(1)}, u32[]{:S(2)}, u32[]{:S(2)}) collective-permute-start(bf16[2,128,128]{2,1,0:T(8,128)(2,1)S(1)} %get-tuple-element.38), channel_id=1, source_target_pairs={{0,128},{64,192},{128,0},{192,64},{1,129},{65,193},{129,1},{193,65... | collective-permute-start | bytes 196616 | tf_op jit(solution)/shard_map/ppermute | solution.py:294
  17.8 5.0 %collective-permute-start.1 = (bf16[2,128,128]{2,1,0:T(8,128)(2,1)S(1)}, bf16[2,128,128]{2,1,0:T(8,128)(2,1)S(1)}, u32[]{:S(2)}, u32[]{:S(2)}) collective-permute-start(bf16[2,128,128]{2,1,0:T(8,128)(2,1)S(1)} %get-tuple-element.38), channel_id=1, source_target_pairs={{0,64},{64,128},{128,192},{192,0},{1,65},{65,129},{129,193},{193,1... | collective-permute-start | bytes 196616 | tf_op jit(solution)/shard_map/ppermute | solution.py:294
  22.8 7.9 %collective-permute-start.9 = (bf16[4,2,128,128]{3,2,1,0:T(8,128)(2,1)S(1)}, bf16[4,2,128,128]{3,2,1,0:T(8,128)(2,1)S(1)}, u32[]{:S(2)}, u32[]{:S(2)}) collective-permute-start(bf16[4,2,128,128]{3,2,1,0:T(8,128)(2,1)S(1)} %pad_maximum_fusion), channel_id=1, source_target_pairs={{0,48},{16,0},{32,16},{48,32},{1,49},{17,1},{33,17},{49,33},{2,50}... | collective-permute-start | bytes 786440 | tf_op jit(solution)/shard_map/ppermute | solution.py:294
  24.9 6.8 %collective-permute-start.8 = (bf16[4,2,128,128]{3,2,1,0:T(8,128)(2,1)S(1)}, bf16[4,2,128,128]{3,2,1,0:T(8,128)(2,1)S(1)}, u32[]{:S(2)}, u32[]{:S(2)}) collective-permute-start(bf16[4,2,128,128]{3,2,1,0:T(8,128)(2,1)S(1)} %pad_maximum_fusion), channel_id=1, source_target_pairs={{0,32},{16,48},{32,0},{48,16},{1,33},{17,49},{33,1},{49,17},{2,34}... | collective-permute-start | bytes 786440 | tf_op jit(solution)/shard_map/ppermute | solution.py:294
  26.2 11.7 %collective-permute-start.7 = (bf16[4,2,128,128]{3,2,1,0:T(8,128)(2,1)S(1)}, bf16[4,2,128,128]{3,2,1,0:T(8,128)(2,1)S(1)}, u32[]{:S(2)}, u32[]{:S(2)}) collective-permute-start(bf16[4,2,128,128]{3,2,1,0:T(8,128)(2,1)S(1)} %pad_maximum_fusion), channel_id=1, source_target_pairs={{0,16},{16,32},{32,48},{48,0},{1,17},{17,33},{33,49},{49,1},{2,18}... | collective-permute-start | bytes 786440 | tf_op jit(solution)/shard_map/ppermute | solution.py:294
  28.1 13.2 %copy-start.6 = (bf16[128,2048]{1,0:T(8,128)(2,1)}, bf16[128,2048]{1,0:T(8,128)(2,1)S(1)}, u32[]{:S(2)}) copy-start(bf16[128,2048]{1,0:T(8,128)(2,1)S(1)} %get-tuple-element.37.qt) | copy-start | bytes 1572868
  28.2 13.3 %copy-start.8 = (bf16[128,2048]{1,0:T(8,128)(2,1)}, bf16[128,2048]{1,0:T(8,128)(2,1)S(1)}, u32[]{:S(2)}) copy-start(bf16[128,2048]{1,0:T(8,128)(2,1)S(1)} %get-tuple-element.35.gt) | copy-start | bytes 1572868
  28.2 13.1 %collective-permute-start.12 = (bf16[4,2,128,128]{3,2,1,0:T(8,128)(2,1)S(1)}, bf16[4,2,128,128]{3,2,1,0:T(8,128)(2,1)S(1)}, u32[]{:S(2)}, u32[]{:S(2)}) collective-permute-start(bf16[4,2,128,128]{3,2,1,0:T(8,128)(2,1)S(1)} %pad_maximum_fusion.1), channel_id=1, source_target_pairs={{0,192},{64,0},{128,64},{192,128},{1,193},{65,1},{129,65},{193,129... | collective-permute-start | bytes 786440 | tf_op jit(solution)/shard_map/ppermute | solution.py:294
  28.6 12.8 %collective-permute-start.11 = (bf16[4,2,128,128]{3,2,1,0:T(8,128)(2,1)S(1)}, bf16[4,2,128,128]{3,2,1,0:T(8,128)(2,1)S(1)}, u32[]{:S(2)}, u32[]{:S(2)}) collective-permute-start(bf16[4,2,128,128]{3,2,1,0:T(8,128)(2,1)S(1)} %pad_maximum_fusion.1), channel_id=1, source_target_pairs={{0,128},{64,192},{128,0},{192,64},{1,129},{65,193},{129,1},{193,65... | collective-permute-start | bytes 786440 | tf_op jit(solution)/shard_map/ppermute | solution.py:294
  30.7 10.7 %collective-permute-start.10 = (bf16[4,2,128,128]{3,2,1,0:T(8,128)(2,1)S(1)}, bf16[4,2,128,128]{3,2,1,0:T(8,128)(2,1)S(1)}, u32[]{:S(2)}, u32[]{:S(2)}) collective-permute-start(bf16[4,2,128,128]{3,2,1,0:T(8,128)(2,1)S(1)} %pad_maximum_fusion.1), channel_id=1, source_target_pairs={{0,64},{64,128},{128,192},{192,0},{1,65},{65,129},{129,193},{193,1... | collective-permute-start | bytes 786440 | tf_op jit(solution)/shard_map/ppermute | solution.py:294
  41.4 5.3 %copy-start = (bf16[4,2,128,128]{3,2,1,0:T(8,128)(2,1)}, bf16[4,2,128,128]{3,2,1,0:T(8,128)(2,1)S(1)}, u32[]{:S(2)}) copy-start(bf16[4,2,128,128]{3,2,1,0:T(8,128)(2,1)S(1)} %collective-permute-done.12) | copy-start | bytes 786436
  41.4 5.3 %copy-start.2 = (bf16[4,2,128,128]{3,2,1,0:T(8,128)(2,1)}, bf16[4,2,128,128]{3,2,1,0:T(8,128)(2,1)S(1)}, u32[]{:S(2)}) copy-start(bf16[4,2,128,128]{3,2,1,0:T(8,128)(2,1)S(1)} %collective-permute-done.11) | copy-start | bytes 786436
  41.4 5.3 %copy-start.4 = (bf16[4,2,128,128]{3,2,1,0:T(8,128)(2,1)}, bf16[4,2,128,128]{3,2,1,0:T(8,128)(2,1)S(1)}, u32[]{:S(2)}) copy-start(bf16[4,2,128,128]{3,2,1,0:T(8,128)(2,1)S(1)} %collective-permute-done.10) | copy-start | bytes 786436
  46.7 32.7 %all-to-all-start = ((bf16[16,2,128,256]{3,2,1,0:T(8,128)(2,1)}), bf16[16,2,128,256]{3,2,1,0:T(8,128)(2,1)S(1)}, u32[]{:S(2)}, u32[]{:S(2)}) async-start(bf16[16,2,128,256]{3,2,1,0:T(8,128)(2,1)} %bitcast.42), calls=%async_computation | async-start | bytes 4194304 | tf_op jit(solution)/shard_map/all_to_all | solution.py:339
  54.5 1.0 copy-start.1
  55.5 0.9 copy-start.3
  57.4 1.0 copy-start.7
  58.4 1.0 copy-start.9
  79.6 7.8 %collective-permute-start.13 = (bf16[128,256]{1,0:T(8,128)(2,1)S(1)}, bf16[128,256]{1,0:T(8,128)(2,1)S(1)}, u32[]{:S(2)}, u32[]{:S(2)}) collective-permute-start(bf16[128,256]{1,0:T(8,128)(2,1)S(1)} %shard_map.107), channel_id=1, source_target_pairs={{0,8},{8,0},{1,9},{9,1},{2,10},{10,2},{3,11},{11,3},{4,12},{12,4},... | collective-permute-start | bytes 196616 | tf_op jit(solution)/shard_map/ppermute | solution.py:294
  (1 other events, 0.9 us)
